TPU v7x, 32 devices: a whole 2x2x4 slice. The times are simulated.
32 devices in a mesh: shot: 4 (over y, x), dom: 8 (over z, core).
Axes of the slice: x: 2, y: 2, z: 4, core: 2. Of those that a mesh axis runs over, the one named last changes fastest.
Arguments:
- forward: float32 [8, 9, 125, 2048], P('shot', None, None, 'dom'), may hold values from -6 to 6
- adjoint: float32 [8, 9, 125, 2048], P('shot', None, None, 'dom'), may hold values from -6 to 6
- material: float32 [3, 125, 2048], P(None, None, 'dom'), may hold values from 0.5 to 2
- counts: int32 [8], P('dom'), may hold values from 64 to 256, as said below
- send_list: int32 [8, 4, 32], P('dom'), may hold values from 0 to 256, as said below
- neighbours: int32 [8, 1536], P('dom'), may hold values from 0 to 1665
Outputs:
- forward_next: float32 [8, 9, 125, 2048], P('shot', None, None, 'dom')
- adjoint_next: float32 [8, 9, 125, 2048], P('shot', None, None, 'dom')
- gradient: float32 [3, 125, 2048], P(None, None, 'dom')
Inputs may be any that keep to these rules, and one draw needn't show every extreme that they name: Device d holds counts[d] octants in its first slots, in Morton order of its tree; some device holds 256 and some device holds only one layer, 64. `send_list`: entry [d, s, p] is the slot of device d's octant on lateral side s (-x, +x, -y, +y) at position p = (horizontal coordinate along the side) * 4 + layer, or 256 where the position holds no octant; every listed slot is live.
All inputs are finite; a program needn't handle non-finite values.
Results may differ from a plain program's by a relative error of at most 0.0003.
Values sent between devices are 32-bit elements; how exact they have to be, the bound alone decides.
No kernel may reach another device: no remote copies, remote signals or barrier semaphores. Data moves between devices by JAX's collectives and lax.ppermute only.
A program may use at most 192 MiB of HBM per device.

v0:
```python
import functools

import jax
import jax.numpy as jnp
import numpy as np
from jax import lax
from jax.experimental import pallas as pl
from jax.experimental.pallas import tpu as pltpu
from jax.sharding import PartitionSpec as P

DEV_Y = 4
ORDER = 5
NODES = ORDER**3
FACE = ORDER * ORDER
FIELDS = 9
LANES = 128
SUBS = 8
step_size = 0.01
lift_weight = 10.0
VMEM_BYTES = 16 * 1024 * 1024

FACE_OFF = (0, 100, 0, 20, 0, 4)
FACE_U = (5, 5, 25, 25, 25, 25)
FACE_V = (1, 1, 1, 1, 5, 5)


def derivative_matrix():
    points = np.array([-1.0, -np.sqrt(3.0 / 7.0), 0.0, np.sqrt(3.0 / 7.0), 1.0])
    barycentric = np.array(
        [1.0 / np.prod([points[a] - points[b] for b in range(5) if b != a]) for a in range(5)]
    )
    matrix = np.zeros((5, 5))
    for a in range(5):
        for b in range(5):
            if a != b:
                matrix[a, b] = barycentric[b] / barycentric[a] / (points[a] - points[b])
        matrix[a, a] = -np.sum(matrix[a])
    return matrix


MAT = derivative_matrix()


def derivative(u):
    e0, e1 = u[0] + u[4], u[1] + u[3]
    o0, o1 = u[0] - u[4], u[1] - u[3]
    mid = u[2] + u[2]
    e0, e1 = e0 - mid, e1 - mid
    out = [None] * 5
    for a in range(2):
        even = float(0.5 * (MAT[a, 0] + MAT[a, 4])) * e0 + float(0.5 * (MAT[a, 1] + MAT[a, 3])) * e1
        odd = float(0.5 * (MAT[a, 0] - MAT[a, 4])) * o0 + float(0.5 * (MAT[a, 1] - MAT[a, 3])) * o1
        out[a] = odd + even
        out[4 - a] = odd - even
    out[2] = float(MAT[2, 0]) * o0 + float(MAT[2, 1]) * o1
    return out


def sub_iota():
    return lax.broadcasted_iota(jnp.int32, (SUBS, LANES), 0)


def half_of():
    return sub_iota() >> 2


def live_tile(counts_ref):
    lane = lax.broadcasted_iota(jnp.int32, (SUBS, LANES), 1)
    return half_of() * LANES + lane < counts_ref[0]


def swap_halves(x):
    return pltpu.roll(x, SUBS // 2, axis=0)


def lane_pick(x, idx):
    return jnp.take_along_axis(x, idx, axis=1, mode="promise_in_bounds")


def code_tile(codes_ref, face, slots):
    base = face * slots
    rows = []
    for h in range(2):
        at = base + h * LANES
        at = at if isinstance(at, int) else pl.multiple_of(at, LANES)
        rows.append(jnp.broadcast_to(codes_ref[0:1, pl.ds(at, LANES)], (SUBS, LANES)))
    first, second = rows
    return jnp.where(half_of() == 0, first, second)


def side_offset(axis, up):
    return up * FACE_OFF[2 * axis + 1]


def pack_side(state, list_ref, out, axis, up, slots):
    half = half_of()
    low = half == 0
    lane_group = lax.broadcasted_iota(jnp.int32, (SUBS, LANES), 1) >> 5
    masks = [lane_group == q for q in range(1, 4)]
    side = 2 * axis
    row = jnp.where(up > 0, list_ref[0, side + 1 : side + 2, :], list_ref[0, side : side + 1, :])
    listed = jnp.broadcast_to(jnp.concatenate([row] * 4, axis=1), (SUBS, LANES))
    idx = listed & (LANES - 1)
    here = (listed < slots) & ((listed >> 7) == half)
    start = side_offset(axis, up)

    def combine(parts):
        picked = [lane_pick(part, idx) for part in parts]
        groups = []
        for x in range(2):
            four = picked[4 * x : 4 * x + 4]
            tile = four[0]
            for q in range(1, len(four)):
                tile = jnp.where(masks[q - 1], four[q], tile)
            tile = jnp.where(here, tile, 0.0)
            groups.append(tile + swap_halves(tile))
        return jnp.where(low, groups[0], groups[1])

    for p in range(FACE):
        node = start + FACE_U[side] * (p // ORDER) + FACE_V[side] * (p % ORDER)
        out[p] = combine([state[k * NODES + node] for k in range(8)])
    for g in range(4):
        parts = []
        for w in range(8):
            p = min(8 * g + w, FACE - 1)
            node = start + FACE_U[side] * (p // ORDER) + FACE_V[side] * (p % ORDER)
            parts.append(state[8 * NODES + node])
        out[FACE + g] = combine(parts)


def add_rows(acc, node, jumps, coef, direction, sign):
    lam, mu, buoy, speed = coef
    a, b, c = direction, (direction + 1) % 3, (direction + 2) % 3
    s_aa, s_bb, s_cc = 3 + a, 3 + b, 3 + c
    s_ab, s_ac, s_bc = 6 + c, 6 + b, 6 + a
    across = lam * jumps[a]
    flux = {
        a: buoy * jumps[s_aa],
        b: buoy * jumps[s_ab],
        c: buoy * jumps[s_ac],
        s_aa: across + (mu + mu) * jumps[a],
        s_bb: across,
        s_cc: across,
        s_ab: mu * jumps[b],
        s_ac: mu * jumps[c],
    }
    for k in range(FIELDS):
        row = k * NODES + node
        total = speed * jumps[k]
        if k in flux:
            total = total + flux[k] if sign > 0 else total - flux[k]
        acc[row] = acc[row] + total


def coefs(med, node):
    return [med[m * NODES + node] for m in range(4)]


def volume_pass(state, acc, med, products, average, scaled):
    def x_lines(j, carry):
        for k in range(5):
            for field, row in ((0, 3), (1, 8), (2, 7), (3, 0), (8, 1), (7, 2)):
                out = derivative([state[field * NODES + 25 * i + 5 * j + k] for i in range(5)])
                for i in range(5):
                    acc[row * NODES + 25 * i + 5 * j + k] = out[i]
        return carry

    lax.fori_loop(0, ORDER, x_lines, 0)

    def y_lines(i, carry):
        for k in range(5):
            for field, row, more in ((0, 8, 1), (1, 4, 0), (2, 6, 0), (8, 0, 1), (4, 1, 1), (6, 2, 1)):
                out = derivative([state[field * NODES + 25 * i + 5 * j + k] for j in range(5)])
                for j in range(5):
                    at = row * NODES + 25 * i + 5 * j + k
                    acc[at] = acc[at] + out[j] if more else out[j]
        return carry

    lax.fori_loop(0, ORDER, y_lines, 0)

    def z_line(first):
        parts = {}
        for field in (0, 1, 2, 7, 6, 5):
            parts[field] = derivative([state[field * NODES + first + k] for k in range(5)])
        for k in range(5):
            node = first + k
            lam, mu, buoy = (scaled(value) for value in coefs(med, node)[:3])
            old = [acc[row * NODES + node] for row in range(FIELDS) if row != 5]
            sdiv = [old[0] + parts[7][k], old[1] + parts[6][k], old[2] + parts[5][k]]
            g11, g22, g33 = old[3], old[4], parts[2][k]
            r23 = old[5] + parts[1][k]
            r13 = old[6] + parts[0][k]
            r12 = old[7]
            div = g11 + g22 + g33
            spread = lam * div
            mu2 = mu + mu
            volume = [buoy * s for s in sdiv]
            volume += [spread + mu2 * g for g in (g11, g22, g33)]
            volume += [mu * r for r in (r23, r13, r12)]
            own = [state[row * NODES + node] for row in range(FIELDS)]
            for row in range(FIELDS):
                acc[row * NODES + node] = average(own[row], row * NODES + node) + volume[row]
            dual = [pltpu.roll(x, SUBS - 2, axis=0) for x in own]
            pressure = div * (dual[3] + dual[4] + dual[5])
            normal = g11 * dual[3] + g22 * dual[4] + g33 * dual[5]
            shear = normal + normal + (r23 * dual[6] + r13 * dual[7] + r12 * dual[8])
            light = sdiv[0] * dual[0] + sdiv[1] * dual[1] + sdiv[2] * dual[2]
            for m, value in enumerate((pressure, shear, light)):
                products[pl.ds((m * LANES + node) * SUBS, SUBS), :] = value

    def z_lines(i, carry):
        for j in range(5):
            z_line(25 * i + 5 * j)
        return carry

    lax.fori_loop(0, ORDER, z_lines, 0)


def shot_sums(products, emit):
    for m in range(3):
        for g in range((NODES + 7) // 8):
            rows = min(8, NODES - 8 * g)
            base = (m * LANES + 8 * g) * SUBS
            for h in range(2):
                first = products[pl.ds(base + 4 * h, 8, stride=SUBS), :]
                second = products[pl.ds(base + 4 * h + 1, 8, stride=SUBS), :]
                emit(m, 8 * g, rows, h, (first + second)[:rows])


def local_pass(state, acc, med, codes_ref, slots, weight):
    half = half_of()
    low = half == 0
    free_code = 6 * slots + 4 * 32
    for face in range(6):
        codes = code_tile(codes_ref, face, slots)
        idx = codes & (LANES - 1)
        match = (codes >> 8) == (face ^ 1)
        same = match & (((codes >> 7) & 1) == half)
        cross = match & (((codes >> 7) & 1) != half)
        free = codes == free_code
        factor_v = jnp.where(free, 0.0, weight)
        factor_s = jnp.where(free, 2.0 * weight, weight)
        other = face ^ 1

        def body(u, carry, face=face, other=other, idx=idx, same=same, cross=cross,
                 factor_v=factor_v, factor_s=factor_s):
            for v in range(ORDER):
                shift = FACE_U[face] * u + FACE_V[face] * v
                node = FACE_OFF[face] + shift
                source = FACE_OFF[other] + shift
                jumps = []
                for k in range(FIELDS):
                    there = state[k * NODES + source]
                    outer = jnp.where(same, lane_pick(there, idx), 0.0)
                    outer = jnp.where(cross, lane_pick(swap_halves(there), idx), outer)
                    jump = outer - state[k * NODES + node]
                    jumps.append(jump * (factor_v if k < 3 else factor_s))
                add_rows(acc, node, jumps, coefs(med, node), face // 2, 2 * (face % 2) - 1)
            return carry

        lax.fori_loop(0, ORDER, body, 0, unroll=True)


def ghost_tiles(ghost, p, low):
    tile = ghost[p]
    turned = swap_halves(tile)
    tile9 = ghost[FACE + (p >> 3)]
    turned9 = swap_halves(tile9)
    chosen = half_of() == ((p >> 2) & 1)
    return jnp.where(low, tile, turned), jnp.where(low, turned, tile), jnp.where(chosen, tile9, turned9)


def ghost_pass(acc, med, codes_ref, ghost, axis, up, slots, scale):
    low = half_of() == 0
    face = 2 * axis + up
    sign = (2 * up - 1).astype(jnp.float32)
    codes = code_tile(codes_ref, face, slots) - (6 * slots + 32 * face)
    inside = (codes >= 0) & (codes < 32)
    weight = jnp.where(inside, scale, 0.0)
    idx = codes & 31
    shifted = [idx + 32 * q for q in range(4)]
    start = side_offset(axis, up)

    def body(u, carry):
        for v in range(ORDER):
            p = ORDER * u + v
            node = start + FACE_U[2 * axis] * u + FACE_V[2 * axis] * v
            first, second, nine = ghost_tiles(ghost, p, low)
            jumps = []
            for k in range(8):
                jumps.append(lane_pick(first if k < 4 else second, shifted[k % 4]) * weight)
            jumps.append(lane_pick(nine, idx + 32 * (p & 3)) * weight)
            lam, mu, buoy, speed = coefs(med, node)
            add_rows(acc, node, jumps, (sign * lam, sign * mu, sign * buoy, speed), axis, 1)
        return carry

    lax.fori_loop(0, ORDER, body, 0, unroll=True)


def other_sources(state, acc, med, codes_ref, ghosts, ups, axes, outer, slots, scale):
    half = half_of()
    low = half == 0
    first_ghost = 6 * slots

    def codes_of(face):
        return code_tile(codes_ref, face, slots)

    left = jnp.zeros((SUBS, LANES), jnp.int32)
    for face in range(6):
        codes = codes_of(face)
        source = jnp.where(codes < first_ghost, codes >> 8, 6 + ((codes - first_ghost) >> 5))
        usual = (source == (face ^ 1)) | (source >= 10)
        if face < 4:
            usual = usual | (source == 6 + face)
        left = left | jnp.where(usual, 0, 1)
    remaining = jnp.max(left)

    @pl.when(remaining > 0)
    def _():
        def pair(t, carry):
            face, origin = t // 10, t % 10
            codes = code_tile(codes_ref, face, slots)
            source = jnp.where(codes < first_ghost, codes >> 8, 6 + ((codes - first_ghost) >> 5))
            mine = source == origin
            done = (origin == (face ^ 1)) | ((face < 4) & (origin == 6 + face))
            count = jnp.max(jnp.where(mine, 1, 0))

            @pl.when((count > 0) & jnp.logical_not(done))
            def _():
                weight = jnp.where(mine, scale, 0.0)
                axis, sign = face >> 1, (2 * (face & 1) - 1).astype(jnp.float32)

                def strides(which):
                    line = which >> 1
                    off = (which & 1) * jnp.where(line == 0, 100, jnp.where(line == 1, 20, 4))
                    return off, jnp.where(line == 0, 5, 25), jnp.where(line == 2, 5, 1)

                off, du, dv = strides(face)
                off2, du2, dv2 = strides(jnp.minimum(origin, 5))

                def at_node(p, carry):
                    u, v = p // ORDER, p % ORDER
                    node = off + du * u + dv * v

                    @pl.when(origin < 6)
                    def _():
                        there_node = off2 + du2 * u + dv2 * v
                        idx = codes & (LANES - 1)
                        same = ((codes >> 7) & 1) == half
                        for k in range(FIELDS):
                            there = state[k * NODES + there_node]
                            turned = swap_halves(there)
                            outer[k] = jnp.where(same, lane_pick(there, idx), lane_pick(turned, idx)) * weight

                    @pl.when(origin >= 6)
                    def _():
                        for k in range(FIELDS):
                            outer[k] = jnp.zeros((SUBS, LANES), jnp.float32)

                    for ghost, up, line in zip(ghosts, ups, axes):

                        @pl.when(origin == 6 + 2 * line + up)
                        def _(ghost=ghost):
                            idx = (codes - first_ghost) & 31
                            first, second, nine = ghost_tiles(ghost, p, low)
                            for k in range(8):
                                tile = first if k < 4 else second
                                outer[k] = lane_pick(tile, idx + 32 * (k % 4)) * weight
                            outer[8] = lane_pick(nine, idx + 32 * (p & 3)) * weight

                    lam, mu, buoy, speed = coefs(med, node)
                    a = axis
                    b, c = lax.rem(axis + 1, 3), lax.rem(axis + 2, 3)
                    across = lam * outer[a]
                    flux = (
                        (a, buoy * outer[3 + a]),
                        (b, buoy * outer[6 + c]),
                        (c, buoy * outer[6 + b]),
                        (3 + a, across + (mu + mu) * outer[a]),
                        (3 + b, across),
                        (3 + c, across),
                        (6 + c, mu * outer[b]),
                        (6 + b, mu * outer[c]),
                        (6 + a, None),
                    )
                    for k, value in flux:
                        row = k * NODES + node
                        total = speed * outer[k]
                        if value is not None:
                            total = total + sign * value
                        acc[row] = acc[row] + total
                    return carry

                lax.fori_loop(0, FACE, at_node, 0)

            return carry

        lax.fori_loop(0, 60, pair, 0)


def link_ups(place_ref, links):
    return [1 - ((lax.div(place_ref[0], stride) + parity) & 1) for _, stride, parity in links]


def load_kernel(slots, links, mat_hbm, fwd_hbm, adj_hbm, state_ref, med_ref, mat_ref, sems, mat_sem):
    mat_copy = pltpu.make_async_copy(mat_hbm, mat_ref, mat_sem)
    mat_copy.start()
    copies = []
    for k in range(FIELDS):
        span = pl.ds(k * NODES, NODES)
        for n, far in enumerate((fwd_hbm, adj_hbm)):
            copies.append(pltpu.make_async_copy(far.at[span], state_ref.at[span, :, n], sems.at[n, k]))
            copies[-1].start()
    mat_copy.wait()
    spread_material(mat_ref, med_ref)
    for copy in copies:
        copy.wait()


def pack_kernel(slots, links, place_ref, state_ref, list_ref, *sends):
    ups = link_ups(place_ref, links)
    for n, link in enumerate(links):
        pack_side(state_ref, list_ref, sends[n], link[0], ups[n], slots)


def spread_material(mat_ref, med_ref):
    low = half_of() == 0
    for node in range(NODES):
        rows = []
        for m in range(3):
            first = jnp.broadcast_to(mat_ref[m, node : node + 1, 0:LANES], (SUBS, LANES))
            second = jnp.broadcast_to(mat_ref[m, node : node + 1, LANES : 2 * LANES], (SUBS, LANES))
            rows.append(jnp.where(low, first, second))
        lam, mu, buoy = rows
        speed = jnp.sqrt((lam + 2.0 * mu) * buoy)
        for m, value in enumerate((lam, mu, buoy, speed)):
            med_ref[m * NODES + node] = step_size * value


def first_kernel(slots, links, counts_ref, state_ref, med_ref, codes_ref, acc_ref, grad_ref, products):
    volume_pass(state_ref, acc_ref, med_ref, products, lambda own, row: own, lambda value: value)
    shot_sums(products, store_gradient(counts_ref, grad_ref, None))
    local_pass(state_ref, acc_ref, med_ref, codes_ref, slots, 0.5 * lift_weight)


def store_gradient(counts_ref, grad_ref, earlier_ref):
    lane = lax.broadcasted_iota(jnp.int32, (SUBS, LANES), 1)

    def emit(m, start, rows, h, value):
        at = (m, slice(start, start + rows), slice(h * LANES, (h + 1) * LANES))
        if earlier_ref is not None:
            value = (0.5 * step_size) * (earlier_ref[at] + value)
        grad_ref[at] = jnp.where((h * LANES + lane < counts_ref[0])[:rows], value, 0.0)

    return emit


def ghost_stage(slots, links, ups, state_ref, acc_ref, med_ref, codes_ref, ghosts, outer, scale):
    axes = [link[0] for link in links]
    for axis, up, ghost in zip(axes, ups, ghosts):
        ghost_pass(acc_ref, med_ref, codes_ref, ghost, axis, up, slots, scale)
    other_sources(state_ref, acc_ref, med_ref, codes_ref, ghosts, ups, axes, outer, slots, scale)


def middle_kernel(slots, links, place_ref, acc_in, state_ref, med_ref, codes_ref, list_ref, *rest):
    count = len(links)
    ghosts, mid_ref, sends, outer = rest[:count], rest[count], rest[count + 1 : 2 * count + 1], rest[-1]
    ups = link_ups(place_ref, links)
    ghost_stage(slots, links, ups, state_ref, mid_ref, med_ref, codes_ref, ghosts, outer, 0.5 * lift_weight)
    for n, link in enumerate(links):
        pack_side(mid_ref, list_ref, sends[n], link[0], ups[n], slots)


def second_volume_kernel(slots, links, counts_ref, mid_ref, state_ref, med_ref, first_ref, acc_ref, grad_ref, products):
    share = jnp.where(live_tile(counts_ref), 0.5, 0.0)
    volume_pass(
        mid_ref, acc_ref, med_ref, products,
        lambda own, row: share * (own + state_ref[row]), lambda value: share * value,
    )
    shot_sums(products, store_gradient(counts_ref, grad_ref, first_ref))


def second_faces_kernel(slots, links, counts_ref, acc_in, mid_ref, med_ref, codes_ref, acc_ref):
    weight = jnp.where(live_tile(counts_ref), 0.25 * lift_weight, 0.0)
    local_pass(mid_ref, acc_ref, med_ref, codes_ref, slots, weight)


def second_ghosts_kernel(chosen, slots, links, place_ref, acc_in, med_ref, codes_ref, *rest):
    ghosts, acc_ref = rest[: len(chosen)], rest[-1]
    ups = link_ups(place_ref, links)
    for n, ghost in zip(chosen, ghosts):
        ghost_pass(acc_ref, med_ref, codes_ref, ghost, links[n][0], ups[n], slots, 0.25 * lift_weight)


def other_sources_kernel(slots, links, place_ref, acc_in, mid_ref, med_ref, codes_ref, *rest):
    ghosts, (acc_ref, outer) = rest[: len(links)], rest[len(links) :]
    ups = link_ups(place_ref, links)
    axes = [link[0] for link in links]
    other_sources(mid_ref, acc_ref, med_ref, codes_ref, ghosts, ups, axes, outer, slots, 0.25 * lift_weight)


def split_kernel(slots, links, grad_ref, *rest):
    first_ref, second_ref = rest[len(links) :]
    cut = first_ref.shape[1]
    first_ref[...] = grad_ref[:, :cut]
    second_ref[...] = grad_ref[:, cut:]


def partial_kernel(slots, links, acc_in, a_ref, b_ref, near_ref, far_ref, acc_ref, first_ref, second_ref):
    first_ref[...] = a_ref[...] + near_ref[...]
    second_ref[...] = b_ref[...] + far_ref[...]


def total_kernel(slots, links, a_ref, b_ref, c_ref, d_ref, grad_ref):
    cut = a_ref.shape[1]
    grad_ref[:, :cut] = a_ref[...] + c_ref[...]
    grad_ref[:, cut:] = b_ref[...] + d_ref[...]


def store_kernel(slots, links, acc_ref, fwd_hbm, adj_hbm, sems):
    copies = []
    for k in range(FIELDS):
        span = pl.ds(k * NODES, NODES)
        for n, far in enumerate((fwd_hbm, adj_hbm)):
            copies.append(pltpu.make_async_copy(acc_ref.at[span, :, n], far.at[span], sems.at[n, k]))
            copies[-1].start()
    for copy in copies:
        copy.wait()


def tree_links(devices):
    links = []
    for axis, stride in ((0, DEV_Y), (1, 1)):
        for parity in range(2):
            pairs = [(d, d + stride) for d in range(devices - stride) if (d // stride) % 2 == parity]
            if pairs:
                links.append((axis, stride, parity, pairs + [(b, a) for a, b in pairs]))
    return links


def swapped(block, axis, distance):
    route = [(i, i ^ distance) for i in range(lax.axis_size(axis))]
    return lax.ppermute(block, axis, route)


def shards(forward, adjoint, material, counts, send_list, neighbours):
    shots, fields, nodes, slots = forward.shape
    halves = slots // LANES
    rows = fields * nodes
    assert 2 * shots * halves == SUBS and nodes == NODES and fields == FIELDS

    def dense(values):
        cut = values.reshape(shots, fields, nodes, halves, LANES)
        tiles = cut.transpose(1, 2, 3, 0, 4).reshape(rows, halves, shots, LANES)
        return pltpu.with_memory_space_constraint(tiles, pltpu.HBM)

    def restored(values):
        cut = values.reshape(fields, nodes, halves, shots, LANES)
        return cut.transpose(3, 0, 1, 2, 4).reshape(shots, fields, nodes, slots)

    links = tree_links(lax.axis_size("dom"))
    axes = tuple(link[:3] for link in links)
    place = lax.axis_index("dom").astype(jnp.int32).reshape(1)

    def exchange(sends):
        return [lax.ppermute(send, "dom", link[3]) for send, link in zip(sends, links)]

    vmem = pl.BlockSpec(memory_space=pltpu.VMEM)
    smem = pl.BlockSpec(memory_space=pltpu.SMEM)
    hbm = pl.BlockSpec(memory_space=pltpu.HBM)
    f32 = jnp.float32
    state_shape = pltpu.VMEM((rows, SUBS, LANES), f32)
    send_shape = pltpu.VMEM((FACE + 4, SUBS, LANES), f32)
    med_shape = pltpu.VMEM((4 * nodes, SUBS, LANES), f32)
    grad_shape = pltpu.VMEM(material.shape, f32)
    apart = (rows, halves, 2, shots, LANES)
    part_shape = jax.ShapeDtypeStruct((rows, halves, shots, LANES), f32)
    products = pltpu.VMEM((3 * LANES * SUBS, LANES), f32)
    outer = pltpu.VMEM((FIELDS, SUBS, LANES), f32)
    field_sems = pltpu.SemaphoreType.DMA((2, FIELDS))

    def call(kernel, out_shape, in_specs, name, micros, scratch=(), out_specs=None, aliases=None):
        return pl.pallas_call(
            functools.partial(kernel, slots, axes),
            out_shape=out_shape,
            in_specs=in_specs,
            out_specs=out_specs or [vmem] * len(out_shape),
            scratch_shapes=list(scratch),
            input_output_aliases=aliases or {},
            compiler_params=pltpu.CompilerParams(vmem_limit_bytes=VMEM_BYTES),
            cost_estimate=pl.CostEstimate(flops=0, bytes_accessed=micros * 3000000, transcendentals=0),
            name=name,
        )

    count = len(links)
    state, med = call(
        load_kernel, [pltpu.VMEM(apart, f32), med_shape], [hbm] * 3, "load", 4,
        [pltpu.VMEM(material.shape, f32), field_sems, pltpu.SemaphoreType.DMA],
    )(pltpu.with_memory_space_constraint(material, pltpu.HBM), dense(forward), dense(adjoint))
    state = state.reshape(rows, SUBS, LANES)
    sends = call(pack_kernel, [send_shape] * count, [smem, vmem, vmem], "pack", 2)(place, state, send_list)
    ghosts = exchange(sends)
    acc, grad_first = call(
        first_kernel, [state_shape, grad_shape], [smem] + [vmem] * 3, "first_section", 8, [products]
    )(counts, state, med, neighbours)
    mid, *sends = call(
        middle_kernel, [state_shape] + [send_shape] * count, [smem] + [vmem] * (5 + count), "first_ghosts", 4,
        [outer], aliases={1: 0},
    )(place, acc, state, med, neighbours, send_list, *ghosts)
    ghosts = exchange(sends)
    acc, grad = call(
        second_volume_kernel, [state_shape, grad_shape], [smem] + [vmem] * 4, "second_volume", 4, [products]
    )(counts, mid, state, med, grad_first)
    shot_devices = lax.axis_size("shot")
    doubling = shot_devices == 4
    if doubling:
        cut = (nodes // 2 + SUBS // 2) // SUBS * SUBS
        part_shapes = [pltpu.VMEM((3, size, slots), f32) for size in (cut, nodes - cut)]
        halved = call(split_kernel, part_shapes, [vmem] * (1 + count), "gradient_split", 0)(grad, *ghosts)
        pieces = [swapped(halved[0], "shot", 1), swapped(halved[1], "shot", 2)]
    (acc,) = call(
        second_faces_kernel, [state_shape], [smem] + [vmem] * 4, "second_faces", 4, aliases={1: 0}
    )(counts, acc, mid, med, neighbours)

    def add_ghosts(acc, chosen):
        (acc,) = call(
            functools.partial(second_ghosts_kernel, chosen), [state_shape], [smem] + [vmem] * (3 + len(chosen)),
            "second_ghosts", 2, aliases={1: 0},
        )(place, acc, med, neighbours, *[ghosts[n] for n in chosen])
        return acc

    acc = add_ghosts(acc, range(1))
    if doubling:
        acc, *parts = call(
            partial_kernel, [state_shape] + part_shapes, [vmem] * 5, "gradient_partial", 0, aliases={0: 0}
        )(acc, *halved, *pieces)
        pieces = [swapped(parts[0], "shot", 2), swapped(parts[1], "shot", 1)]
    else:
        gradient = lax.psum(grad, "shot")
    acc = add_ghosts(acc, range(1, count))
    (acc,) = call(
        other_sources_kernel, [state_shape], [smem] + [vmem] * (4 + count), "other_sources", 0, [outer], aliases={1: 0}
    )(place, acc, mid, med, neighbours, *ghosts)
    fwd, adj = call(store_kernel, [part_shape, part_shape], [vmem], "store", 4, [field_sems], [hbm, hbm])(
        acc.reshape(apart)
    )
    if doubling:
        (gradient,) = call(
            total_kernel, [jax.ShapeDtypeStruct(material.shape, f32)], [vmem] * 4, "gradient_total", 0
        )(*parts, *pieces)
    return restored(fwd), restored(adj), gradient


def solution(mesh):
    placed = (
        P("shot", None, None, "dom"),
        P("shot", None, None, "dom"),
        P(None, None, "dom"),
        P("dom"),
        P("dom", None, None),
        P("dom", None),
    )
    return jax.shard_map(
        shards,
        mesh=mesh,
        in_specs=placed,
        out_specs=(
            P("shot", None, None, "dom"),
            P("shot", None, None, "dom"),
            P(None, None, "dom"),
        ),
        check_vma=False,
    )
```

profile of v0, /device:TPU:0, one launch (start us, length us, event | category | flops | bytes accessed | tf_op | source)
XLA Modules:
  0.0 48.2 jit_solution(11545357356069107470)
XLA Ops:
  0.6 0.0 copy-start.1
  0.6 0.0 copy-start
  0.7 3.0 %load.1 = (f32[1125,2,2,2,128]{4,3,2,1,0:T(2,128)S(1)}, f32[500,8,128]{2,1,0:T(8,128)S(1)}) custom-call(f32[3,125,256]{2,1,0:T(8,128)} %mat_hbm.1, f32[1125,2,2,128]{3,2,1,0:T(2,128)} %bitcast.28, f32[1125,2,2,128]{3,2,1,0:T(2,128)} %bitcast.29), custom_call_target="tpu_custom_call" | custom-call | bytes 12000000 | tf_op jit(solution)/shard_map/load/pallas_call | solution.py:596
  3.6 0.0 copy-done.1
  3.7 1.0 %pack.1 = (f32[29,8,128]{2,1,0:T(8,128)S(1)}, f32[29,8,128]{2,1,0:T(8,128)S(1)}, f32[29,8,128]{2,1,0:T(8,128)S(1)}) custom-call(s32[1]{0:T(128)} %bitcast.place_ref, f32[1125,8,128]{2,1,0:T(8,128)S(1)} %bitcast.24, s32[1,4,32]{2,1,0:T(4,128)S(1)} %copy-done.1), custom_call_target="tpu_custom_call" | custom-call | bytes 6000000 | tf_op jit(solution)/shard_map/pack/pallas_call | solution.py:601
  4.7 4.1 %collective-permute-start = (f32[29,8,128]{2,1,0:T(8,128)S(1)}, f32[29,8,128]{2,1,0:T(8,128)S(1)}, u32[]{:S(2)}, u32[]{:S(2)}) collective-permute-start(f32[29,8,128]{2,1,0:T(8,128)S(1)} %get-tuple-element.26), channel_id=1, source_target_pairs={{0,4},{1,5},{2,6},{3,7},{4,0},{5,1},{6,2},{7,3},{8,12},{9,13},{10,... | collective-permute-start | bytes 356360 | tf_op jit(solution)/shard_map/ppermute | solution.py:566
  8.8 0.0 collective-permute-start.1
  8.8 0.7 %collective-permute-start.2 = (f32[29,8,128]{2,1,0:T(8,128)S(1)}, f32[29,8,128]{2,1,0:T(8,128)S(1)}, u32[]{:S(2)}, u32[]{:S(2)}) collective-permute-start(f32[29,8,128]{2,1,0:T(8,128)S(1)} %get-tuple-element.28), channel_id=1, source_target_pairs={{1,2},{3,4},{5,6},{2,1},{4,3},{6,5},{9,10},{11,12},{13,14},{10,9},... | collective-permute-start | bytes 356360 | tf_op jit(solution)/shard_map/ppermute | solution.py:566
  10.1 0.0 copy-done
  10.1 6.0 %first_section.1 = (f32[1125,8,128]{2,1,0:T(8,128)S(1)}, f32[3,125,256]{2,1,0:T(8,128)S(1)}) custom-call(s32[1]{0:T(128)S(6)} %copy.25.counts_ref, f32[1125,8,128]{2,1,0:T(8,128)S(1)} %bitcast.25, f32[500,8,128]{2,1,0:T(8,128)S(1)} %get-tuple-element.24.med_ref, s32[1,1536]{1,0:T(1,128)S(1)} %copy-done), custom_call_target="tpu_custom_call" | custom-call | bytes 24000000 | tf_op jit(solution)/shard_map/first_section/pallas_call | solution.py:603
  16.1 0.0 collective-permute-done.rest_0_
  16.1 0.0 collective-permute-done.1.rest_1_
  16.1 0.0 collective-permute-done.2.rest_2_
  16.1 2.9 %first_ghosts.1 = (f32[1125,8,128]{2,1,0:T(8,128)S(1)}, f32[29,8,128]{2,1,0:T(8,128)S(1)}, f32[29,8,128]{2,1,0:T(8,128)S(1)}, f32[29,8,128]{2,1,0:T(8,128)S(1)}) custom-call(s32[1]{0:T(128)} %bitcast.place_ref, f32[1125,8,128]{2,1,0:T(8,128)S(1)} %get-tuple-element.25.acc_in, f32[1125,8,128]{2,1,0:T(8,128)S(1)} %bitcast.26, ...), custom_call_target="tpu_custom_call", output_to_operand_aliasing={{0}: (1, {})} | custom-call | bytes 12000000 | tf_op jit(solution)/shard_map/first_ghosts/pallas_call | solution.py:606
  19.0 4.5 %collective-permute-start.3 = (f32[29,8,128]{2,1,0:T(8,128)S(1)}, f32[29,8,128]{2,1,0:T(8,128)S(1)}, u32[]{:S(2)}, u32[]{:S(2)}) collective-permute-start(f32[29,8,128]{2,1,0:T(8,128)S(1)} %get-tuple-element.32), channel_id=1, source_target_pairs={{0,4},{1,5},{2,6},{3,7},{4,0},{5,1},{6,2},{7,3},{8,12},{9,13},{10,... | collective-permute-start | bytes 356360 | tf_op jit(solution)/shard_map/ppermute | solution.py:566
  23.5 0.0 collective-permute-start.4
  23.5 0.8 %collective-permute-start.5 = (f32[29,8,128]{2,1,0:T(8,128)S(1)}, f32[29,8,128]{2,1,0:T(8,128)S(1)}, u32[]{:S(2)}, u32[]{:S(2)}) collective-permute-start(f32[29,8,128]{2,1,0:T(8,128)S(1)} %get-tuple-element.35), channel_id=1, source_target_pairs={{1,2},{3,4},{5,6},{2,1},{4,3},{6,5},{9,10},{11,12},{13,14},{10,9},... | collective-permute-start | bytes 356360 | tf_op jit(solution)/shard_map/ppermute | solution.py:566
  24.4 3.4 %second_volume.1 = (f32[1125,8,128]{2,1,0:T(8,128)S(1)}, f32[3,125,256]{2,1,0:T(8,128)S(1)}) custom-call(s32[1]{0:T(128)S(6)} %copy.25.counts_ref, f32[1125,8,128]{2,1,0:T(8,128)S(1)} %get-tuple-element.29.mid_ref, f32[1125,8,128]{2,1,0:T(8,128)S(1)} %bitcast.27, f32[500,8,128]{2,1,0:T(8,128)S(1)} %get-tuple-element.24.med_ref, ...), custom_call_target="tpu_custom_call" | custom-call | bytes 12000000 | tf_op jit(solution)/shard_map/second_volume/pallas_call | solution.py:611
  27.8 2.1 %collective-permute-done.3.rest_0_ = f32[29,8,128]{2,1,0:T(8,128)S(1)} collective-permute-done((f32[29,8,128]{2,1,0:T(8,128)S(1)}, f32[29,8,128]{2,1,0:T(8,128)S(1)}, u32[]{:S(2)}, u32[]{:S(2)}) %collective-permute-start.3) | collective-permute-done | bytes 118816 | tf_op jit(solution)/shard_map/ppermute | solution.py:566
  29.9 0.0 collective-permute-done.4.rest_1_.rest_0_
  29.9 0.0 collective-permute-done.5.rest_2_.rest_1_
  29.9 1.6 %collective-permute-start.6 = (f32[3,64,256]{2,1,0:T(8,128)S(1)}, f32[3,64,256]{2,1,0:T(8,128)S(1)}, u32[]{:S(2)}, u32[]{:S(2)}) collective-permute-start(f32[3,64,256]{2,1,0:T(8,128)S(1)} %get-tuple-element.36.a_ref), channel_id=1, source_target_pairs={{0,8},{8,0},{16,24},{24,16},{1,9},{9,1},{17,25},{25,17},{2,10},{10... | collective-permute-start | bytes 589832 | tf_op jit(solution)/shard_map/ppermute | solution.py:543
  31.5 1.5 %collective-permute-start.7 = (f32[3,61,256]{2,1,0:T(8,128)S(1)}, f32[3,61,256]{2,1,0:T(8,128)S(1)}, u32[]{:S(2)}, u32[]{:S(2)}) collective-permute-start(f32[3,61,256]{2,1,0:T(8,128)S(1)} %get-tuple-element.37.b_ref), channel_id=1, source_target_pairs={{0,16},{8,24},{16,0},{24,8},{1,17},{9,25},{17,1},{25,9},{2,18},{10... | collective-permute-start | bytes 562184 | tf_op jit(solution)/shard_map/ppermute | solution.py:543
  33.0 3.1 %second_faces.1.acc_in = f32[1125,8,128]{2,1,0:T(8,128)S(1)} custom-call(s32[1]{0:T(128)S(6)} %copy.25.counts_ref, f32[1125,8,128]{2,1,0:T(8,128)S(1)} %get-tuple-element.31.acc_in, f32[1125,8,128]{2,1,0:T(8,128)S(1)} %get-tuple-element.29.mid_ref, f32[500,8,128]{2,1,0:T(8,128)S(1)} %get-tuple-element.24.med_ref, ...), custom_call_target="tpu_custom_call", output_to_operand_aliasing={{}: (1, {})} | custom-call | bytes 12000000 | tf_op jit(solution)/shard_map/second_faces/pallas_call | solution.py:621
  36.1 0.7 %second_ghosts.2.acc_in = f32[1125,8,128]{2,1,0:T(8,128)S(1)} custom-call(s32[1]{0:T(128)} %bitcast.place_ref, f32[1125,8,128]{2,1,0:T(8,128)S(1)} %second_faces.1.acc_in, f32[500,8,128]{2,1,0:T(8,128)S(1)} %get-tuple-element.24.med_ref, s32[1,1536]{1,0:T(1,128)S(1)} %copy-done, ...), custom_call_target="tpu_custom_call", output_to_operand_aliasing={{}: (1, {})} | custom-call | bytes 6000000 | tf_op jit(solution)/shard_map/second_ghosts/pallas_call | solution.py:626
  36.8 2.4 %collective-permute-done.7.far_ref = f32[3,61,256]{2,1,0:T(8,128)S(1)} collective-permute-done((f32[3,61,256]{2,1,0:T(8,128)S(1)}, f32[3,61,256]{2,1,0:T(8,128)S(1)}, u32[]{:S(2)}, u32[]{:S(2)}) %collective-permute-start.7) | collective-permute-done | bytes 187424 | tf_op jit(solution)/shard_map/ppermute | solution.py:543
  39.1 0.0 collective-permute-done.6.near_ref
  39.2 1.6 %collective-permute-start.8 = (f32[3,64,256]{2,1,0:T(8,128)S(1)}, f32[3,64,256]{2,1,0:T(8,128)S(1)}, u32[]{:S(2)}, u32[]{:S(2)}) collective-permute-start(f32[3,64,256]{2,1,0:T(8,128)S(1)} %get-tuple-element.41.a_ref), channel_id=1, source_target_pairs={{0,16},{8,24},{16,0},{24,8},{1,17},{9,25},{17,1},{25,9},{2,18},{10... | collective-permute-start | bytes 589832 | tf_op jit(solution)/shard_map/ppermute | solution.py:543
  40.8 0.5 %collective-permute-start.9 = (f32[3,61,256]{2,1,0:T(8,128)S(1)}, f32[3,61,256]{2,1,0:T(8,128)S(1)}, u32[]{:S(2)}, u32[]{:S(2)}) collective-permute-start(f32[3,61,256]{2,1,0:T(8,128)S(1)} %get-tuple-element.42.b_ref), channel_id=1, source_target_pairs={{0,8},{8,0},{16,24},{24,16},{1,9},{9,1},{17,25},{25,17},{2,10},{10... | collective-permute-start | bytes 562184 | tf_op jit(solution)/shard_map/ppermute | solution.py:543
  41.3 1.3 %second_ghosts.3.acc_in = f32[1125,8,128]{2,1,0:T(8,128)S(1)} custom-call(s32[1]{0:T(128)} %bitcast.place_ref, f32[1125,8,128]{2,1,0:T(8,128)S(1)} %get-tuple-element.38.acc_in, f32[500,8,128]{2,1,0:T(8,128)S(1)} %get-tuple-element.24.med_ref, s32[1,1536]{1,0:T(1,128)S(1)} %copy-done, ...), custom_call_target="tpu_custom_call", output_to_operand_aliasing={{}: (1, {})} | custom-call | bytes 6000000 | tf_op jit(solution)/shard_map/second_ghosts/pallas_call | solution.py:626
  42.6 0.2 other_sources.1
  42.9 2.3 %store.1 = (f32[1125,2,2,128]{3,2,1,0:T(2,128)}, f32[1125,2,2,128]{3,2,1,0:T(2,128)}) custom-call(f32[1125,2,2,2,128]{4,3,2,1,0:T(2,128)S(1)} %bitcast.23), custom_call_target="tpu_custom_call" | custom-call | bytes 12000000 | tf_op jit(solution)/shard_map/store/pallas_call | solution.py:644
  45.2 2.3 %collective-permute-done.9.d_ref = f32[3,61,256]{2,1,0:T(8,128)S(1)} collective-permute-done((f32[3,61,256]{2,1,0:T(8,128)S(1)}, f32[3,61,256]{2,1,0:T(8,128)S(1)}, u32[]{:S(2)}, u32[]{:S(2)}) %collective-permute-start.9) | collective-permute-done | bytes 187424 | tf_op jit(solution)/shard_map/ppermute | solution.py:543
  47.4 0.0 collective-permute-done.8.c_ref
  47.4 0.8 %gradient_total.1 = f32[3,125,256]{2,1,0:T(8,128)} custom-call(f32[3,64,256]{2,1,0:T(8,128)S(1)} %get-tuple-element.41.a_ref, f32[3,61,256]{2,1,0:T(8,128)S(1)} %get-tuple-element.42.b_ref, f32[3,64,256]{2,1,0:T(8,128)S(1)} %collective-permute-done.8.c_ref, f32[3,61,256]{2,1,0:T(8,128)S(1)} %collective-permute-done.9.d_ref), custom_call_target="tpu_custom_call" | custom-call | tf_op jit(solution)/shard_map/gradient_total/pallas_call | solution.py:648
  (2 shorter events, 0.1 us)
Async XLA Ops:
  0.6 3.0 %copy-start.1 = (s32[1,4,32]{2,1,0:T(4,128)S(1)}, s32[1,4,32]{2,1,0:T(4,128)}, u32[]{:S(2)}) copy-start(s32[1,4,32]{2,1,0:T(4,128)} %list_ref.3) | copy-start | bytes 1540
  0.6 9.5 %copy-start = (s32[1,1536]{1,0:T(1,128)S(1)}, s32[1,1536]{1,0:T(1,128)}, u32[]{:S(2)}) copy-start(s32[1,1536]{1,0:T(1,128)} %codes_ref.11) | copy-start | bytes 18436
  4.7 11.4 %collective-permute-start = (f32[29,8,128]{2,1,0:T(8,128)S(1)}, f32[29,8,128]{2,1,0:T(8,128)S(1)}, u32[]{:S(2)}, u32[]{:S(2)}) collective-permute-start(f32[29,8,128]{2,1,0:T(8,128)S(1)} %get-tuple-element.26), channel_id=1, source_target_pairs={{0,4},{1,5},{2,6},{3,7},{4,0},{5,1},{6,2},{7,3},{8,12},{9,13},{10,... | collective-permute-start | bytes 356360 | tf_op jit(solution)/shard_map/ppermute | solution.py:566
  8.8 7.3 %collective-permute-start.1 = (f32[29,8,128]{2,1,0:T(8,128)S(1)}, f32[29,8,128]{2,1,0:T(8,128)S(1)}, u32[]{:S(2)}, u32[]{:S(2)}) collective-permute-start(f32[29,8,128]{2,1,0:T(8,128)S(1)} %get-tuple-element.27), channel_id=1, source_target_pairs={{0,1},{2,3},{4,5},{6,7},{1,0},{3,2},{5,4},{7,6},{8,9},{10,11},{12,... | collective-permute-start | bytes 356360 | tf_op jit(solution)/shard_map/ppermute | solution.py:566
  8.8 7.3 %collective-permute-start.2 = (f32[29,8,128]{2,1,0:T(8,128)S(1)}, f32[29,8,128]{2,1,0:T(8,128)S(1)}, u32[]{:S(2)}, u32[]{:S(2)}) collective-permute-start(f32[29,8,128]{2,1,0:T(8,128)S(1)} %get-tuple-element.28), channel_id=1, source_target_pairs={{1,2},{3,4},{5,6},{2,1},{4,3},{6,5},{9,10},{11,12},{13,14},{10,9},... | collective-permute-start | bytes 356360 | tf_op jit(solution)/shard_map/ppermute | solution.py:566
  19.0 10.8 %collective-permute-start.3 = (f32[29,8,128]{2,1,0:T(8,128)S(1)}, f32[29,8,128]{2,1,0:T(8,128)S(1)}, u32[]{:S(2)}, u32[]{:S(2)}) collective-permute-start(f32[29,8,128]{2,1,0:T(8,128)S(1)} %get-tuple-element.32), channel_id=1, source_target_pairs={{0,4},{1,5},{2,6},{3,7},{4,0},{5,1},{6,2},{7,3},{8,12},{9,13},{10,... | collective-permute-start | bytes 356360 | tf_op jit(solution)/shard_map/ppermute | solution.py:566
  23.5 6.4 %collective-permute-start.4 = (f32[29,8,128]{2,1,0:T(8,128)S(1)}, f32[29,8,128]{2,1,0:T(8,128)S(1)}, u32[]{:S(2)}, u32[]{:S(2)}) collective-permute-start(f32[29,8,128]{2,1,0:T(8,128)S(1)} %get-tuple-element.34), channel_id=1, source_target_pairs={{0,1},{2,3},{4,5},{6,7},{1,0},{3,2},{5,4},{7,6},{8,9},{10,11},{12,... | collective-permute-start | bytes 356360 | tf_op jit(solution)/shard_map/ppermute | solution.py:566
  23.5 6.4 %collective-permute-start.5 = (f32[29,8,128]{2,1,0:T(8,128)S(1)}, f32[29,8,128]{2,1,0:T(8,128)S(1)}, u32[]{:S(2)}, u32[]{:S(2)}) collective-permute-start(f32[29,8,128]{2,1,0:T(8,128)S(1)} %get-tuple-element.35), channel_id=1, source_target_pairs={{1,2},{3,4},{5,6},{2,1},{4,3},{6,5},{9,10},{11,12},{13,14},{10,9},... | collective-permute-start | bytes 356360 | tf_op jit(solution)/shard_map/ppermute | solution.py:566
  29.9 9.2 %collective-permute-start.6 = (f32[3,64,256]{2,1,0:T(8,128)S(1)}, f32[3,64,256]{2,1,0:T(8,128)S(1)}, u32[]{:S(2)}, u32[]{:S(2)}) collective-permute-start(f32[3,64,256]{2,1,0:T(8,128)S(1)} %get-tuple-element.36.a_ref), channel_id=1, source_target_pairs={{0,8},{8,0},{16,24},{24,16},{1,9},{9,1},{17,25},{25,17},{2,10},{10... | collective-permute-start | bytes 589832 | tf_op jit(solution)/shard_map/ppermute | solution.py:543
  31.5 7.7 %collective-permute-start.7 = (f32[3,61,256]{2,1,0:T(8,128)S(1)}, f32[3,61,256]{2,1,0:T(8,128)S(1)}, u32[]{:S(2)}, u32[]{:S(2)}) collective-permute-start(f32[3,61,256]{2,1,0:T(8,128)S(1)} %get-tuple-element.37.b_ref), channel_id=1, source_target_pairs={{0,16},{8,24},{16,0},{24,8},{1,17},{9,25},{17,1},{25,9},{2,18},{10... | collective-permute-start | bytes 562184 | tf_op jit(solution)/shard_map/ppermute | solution.py:543
  39.2 8.2 %collective-permute-start.8 = (f32[3,64,256]{2,1,0:T(8,128)S(1)}, f32[3,64,256]{2,1,0:T(8,128)S(1)}, u32[]{:S(2)}, u32[]{:S(2)}) collective-permute-start(f32[3,64,256]{2,1,0:T(8,128)S(1)} %get-tuple-element.41.a_ref), channel_id=1, source_target_pairs={{0,16},{8,24},{16,0},{24,8},{1,17},{9,25},{17,1},{25,9},{2,18},{10... | collective-permute-start | bytes 589832 | tf_op jit(solution)/shard_map/ppermute | solution.py:543
  40.8 6.6 %collective-permute-start.9 = (f32[3,61,256]{2,1,0:T(8,128)S(1)}, f32[3,61,256]{2,1,0:T(8,128)S(1)}, u32[]{:S(2)}, u32[]{:S(2)}) collective-permute-start(f32[3,61,256]{2,1,0:T(8,128)S(1)} %get-tuple-element.42.b_ref), channel_id=1, source_target_pairs={{0,8},{8,0},{16,24},{24,16},{1,9},{9,1},{17,25},{25,17},{2,10},{10... | collective-permute-start | bytes 562184 | tf_op jit(solution)/shard_map/ppermute | solution.py:543
where the time goes:
time: 48.4 us; the launch traced here: 48.2 us
  Pallas kernels  24.8 us (51%)
  starting transfers between devices  15.3 us (32%)
  waiting for transfers between devices  6.74 us (14%)
  between operations  1.44 us (3%)
    ppermute x6, starting transfers between devices, exchange(): lax.ppermute(send, 'dom', link[3])  10.1 us
    pallas_call x1, Pallas kernels, shards(): call(first_kernel, [state_shape, grad_shape], [smem] + [vmem] * 3, 'first...  5.97 us
    ppermute x4, starting transfers between devices, swapped(): return lax.ppermute(block, axis, route)  5.2 us
    ppermute x4, waiting for transfers between devices, swapped(): return lax.ppermute(block, axis, route)  4.64 us
    pallas_call x1, Pallas kernels, shards(): call(second_volume_kernel, [state_shape, grad_shape], [smem] + [vmem] * 4...  3.43 us
    pallas_call x1, Pallas kernels, shards(): call(second_faces_kernel, [state_shape], [smem] + [vmem] * 4, 'second_fac...  3.1 us
    pallas_call x1, Pallas kernels, shards(): call(load_kernel, [pltpu.VMEM(apart, f32), med_shape], [hbm] * 3, 'load',...  2.98 us
    pallas_call x1, Pallas kernels, shards(): call(middle_kernel, [state_shape] + [send_shape] * count, [smem] + [vmem]...  2.93 us
  transfers between devices with their start and end apart: 10, of which 3 were waited for; matrix products, arithmetic and copies ran while one was open for 0% of the time, Pallas kernels for 35%

commit v1 on v0

--- a/solution.py
+++ b/solution.py
@@ -66,7 +66,7 @@
 
 def live_tile(counts_ref):
     lane = lax.broadcasted_iota(jnp.int32, (SUBS, LANES), 1)
-    return half_of() * LANES + lane < counts_ref[0]
+    return half_of() * LANES + lane < jnp.broadcast_to(counts_ref[...], (SUBS, LANES))
 
 
 def swap_halves(x):
@@ -406,8 +406,8 @@
     mat_copy = pltpu.make_async_copy(mat_hbm, mat_ref, mat_sem)
     mat_copy.start()
     copies = []
-    for k in range(FIELDS):
-        span = pl.ds(k * NODES, NODES)
+    for k in range(FIELDS * ORDER):
+        span = pl.ds(k * FACE, FACE)
         for n, far in enumerate((fwd_hbm, adj_hbm)):
             copies.append(pltpu.make_async_copy(far.at[span], state_ref.at[span, :, n], sems.at[n, k]))
             copies[-1].start()
@@ -417,10 +417,19 @@
         copy.wait()
 
 
-def pack_kernel(slots, links, place_ref, state_ref, list_ref, *sends):
+def pack_links(slots, links, place_ref, state_ref, list_ref, sends, line):
     ups = link_ups(place_ref, links)
-    for n, link in enumerate(links):
-        pack_side(state_ref, list_ref, sends[n], link[0], ups[n], slots)
+    chosen = [n for n, link in enumerate(links) if link[0] == line]
+    for n, send in zip(chosen, sends):
+        pack_side(state_ref, list_ref, send, line, ups[n], slots)
+
+
+def pack_kernel(line, slots, links, place_ref, state_ref, list_ref, *sends):
+    pack_links(slots, links, place_ref, state_ref, list_ref, sends, line)
+
+
+def late_pack_kernel(line, slots, links, place_ref, state_ref, list_ref, grad_ref, *sends):
+    pack_links(slots, links, place_ref, state_ref, list_ref, sends, line)
 
 
 def spread_material(mat_ref, med_ref):
@@ -439,18 +448,24 @@
 
 def first_kernel(slots, links, counts_ref, state_ref, med_ref, codes_ref, acc_ref, grad_ref, products):
     volume_pass(state_ref, acc_ref, med_ref, products, lambda own, row: own, lambda value: value)
-    shot_sums(products, store_gradient(counts_ref, grad_ref, None))
+    shot_sums(products, store_gradient(counts_ref, [grad_ref], None))
     local_pass(state_ref, acc_ref, med_ref, codes_ref, slots, 0.5 * lift_weight)
 
 
-def store_gradient(counts_ref, grad_ref, earlier_ref):
+def store_gradient(counts_ref, grad_refs, earlier_ref):
     lane = lax.broadcasted_iota(jnp.int32, (SUBS, LANES), 1)
+    count = jnp.broadcast_to(counts_ref[...], (SUBS, LANES))
 
     def emit(m, start, rows, h, value):
         at = (m, slice(start, start + rows), slice(h * LANES, (h + 1) * LANES))
         if earlier_ref is not None:
             value = (0.5 * step_size) * (earlier_ref[at] + value)
-        grad_ref[at] = jnp.where((h * LANES + lane < counts_ref[0])[:rows], value, 0.0)
+        value = jnp.where((h * LANES + lane < count)[:rows], value, 0.0)
+        for grad_ref in grad_refs:
+            size = grad_ref.shape[1]
+            if 0 <= start < size:
+                grad_ref[m, start : start + rows, h * LANES : (h + 1) * LANES] = value
+            start -= size
 
     return emit
 
@@ -464,20 +479,19 @@
 
 def middle_kernel(slots, links, place_ref, acc_in, state_ref, med_ref, codes_ref, list_ref, *rest):
     count = len(links)
-    ghosts, mid_ref, sends, outer = rest[:count], rest[count], rest[count + 1 : 2 * count + 1], rest[-1]
+    ghosts, mid_ref, sends, outer = rest[:count], rest[count], rest[count + 1 : -1], rest[-1]
     ups = link_ups(place_ref, links)
     ghost_stage(slots, links, ups, state_ref, mid_ref, med_ref, codes_ref, ghosts, outer, 0.5 * lift_weight)
-    for n, link in enumerate(links):
-        pack_side(mid_ref, list_ref, sends[n], link[0], ups[n], slots)
-
-
-def second_volume_kernel(slots, links, counts_ref, mid_ref, state_ref, med_ref, first_ref, acc_ref, grad_ref, products):
+    pack_links(slots, links, place_ref, mid_ref, list_ref, sends, 0)
+
+
+def second_volume_kernel(slots, links, counts_ref, mid_ref, state_ref, med_ref, first_ref, acc_ref, near_ref, far_ref, products):
     share = jnp.where(live_tile(counts_ref), 0.5, 0.0)
     volume_pass(
         mid_ref, acc_ref, med_ref, products,
         lambda own, row: share * (own + state_ref[row]), lambda value: share * value,
     )
-    shot_sums(products, store_gradient(counts_ref, grad_ref, first_ref))
+    shot_sums(products, store_gradient(counts_ref, [near_ref, far_ref], first_ref))
 
 
 def second_faces_kernel(slots, links, counts_ref, acc_in, mid_ref, med_ref, codes_ref, acc_ref):
@@ -497,13 +511,6 @@
     ups = link_ups(place_ref, links)
     axes = [link[0] for link in links]
     other_sources(mid_ref, acc_ref, med_ref, codes_ref, ghosts, ups, axes, outer, slots, 0.25 * lift_weight)
-
-
-def split_kernel(slots, links, grad_ref, *rest):
-    first_ref, second_ref = rest[len(links) :]
-    cut = first_ref.shape[1]
-    first_ref[...] = grad_ref[:, :cut]
-    second_ref[...] = grad_ref[:, cut:]
 
 
 def partial_kernel(slots, links, acc_in, a_ref, b_ref, near_ref, far_ref, acc_ref, first_ref, second_ref):
@@ -561,9 +568,11 @@
     links = tree_links(lax.axis_size("dom"))
     axes = tuple(link[:3] for link in links)
     place = lax.axis_index("dom").astype(jnp.int32).reshape(1)
-
-    def exchange(sends):
-        return [lax.ppermute(send, "dom", link[3]) for send, link in zip(sends, links)]
+    counts = counts.reshape(1, 1)
+
+    def exchange(sends, line):
+        routes = [link[3] for link in links if link[0] == line]
+        return [lax.ppermute(send, "dom", route) for send, route in zip(sends, routes)]
 
     vmem = pl.BlockSpec(memory_space=pltpu.VMEM)
     smem = pl.BlockSpec(memory_space=pltpu.SMEM)
@@ -588,56 +597,64 @@
             scratch_shapes=list(scratch),
             input_output_aliases=aliases or {},
             compiler_params=pltpu.CompilerParams(vmem_limit_bytes=VMEM_BYTES),
-            cost_estimate=pl.CostEstimate(flops=0, bytes_accessed=micros * 3000000, transcendentals=0),
+            cost_estimate=pl.CostEstimate(flops=int(micros * 10**9), bytes_accessed=0, transcendentals=0),
             name=name,
         )
 
     count = len(links)
     state, med = call(
         load_kernel, [pltpu.VMEM(apart, f32), med_shape], [hbm] * 3, "load", 4,
-        [pltpu.VMEM(material.shape, f32), field_sems, pltpu.SemaphoreType.DMA],
+        [pltpu.VMEM(material.shape, f32), pltpu.SemaphoreType.DMA((2, FIELDS * ORDER)), pltpu.SemaphoreType.DMA],
     )(pltpu.with_memory_space_constraint(material, pltpu.HBM), dense(forward), dense(adjoint))
     state = state.reshape(rows, SUBS, LANES)
-    sends = call(pack_kernel, [send_shape] * count, [smem, vmem, vmem], "pack", 2)(place, state, send_list)
-    ghosts = exchange(sends)
+    by_line = [[send_shape for link in links if link[0] == line] for line in range(2)]
+    across = len(by_line[0])
+    ghosts = []
+    for line in range(2):
+        sends = call(functools.partial(pack_kernel, line), by_line[line], [smem, vmem, vmem], "pack", 0)(
+            place, state, send_list
+        )
+        ghosts += exchange(sends, line)
     acc, grad_first = call(
-        first_kernel, [state_shape, grad_shape], [smem] + [vmem] * 3, "first_section", 8, [products]
+        first_kernel, [state_shape, grad_shape], [vmem] + [vmem] * 3, "first_section", 8, [products]
     )(counts, state, med, neighbours)
     mid, *sends = call(
-        middle_kernel, [state_shape] + [send_shape] * count, [smem] + [vmem] * (5 + count), "first_ghosts", 4,
+        middle_kernel, [state_shape] + by_line[0], [smem] + [vmem] * (5 + count), "first_ghosts", 4,
         [outer], aliases={1: 0},
     )(place, acc, state, med, neighbours, send_list, *ghosts)
-    ghosts = exchange(sends)
-    acc, grad = call(
-        second_volume_kernel, [state_shape, grad_shape], [smem] + [vmem] * 4, "second_volume", 4, [products]
+    ghosts = exchange(sends, 0)
+    cut = (nodes // 2 + SUBS // 2) // SUBS * SUBS
+    part_shapes = [pltpu.VMEM((3, size, slots), f32) for size in (cut, nodes - cut)]
+    acc, *halved = call(
+        second_volume_kernel, [state_shape] + part_shapes, [vmem] + [vmem] * 4, "second_volume", 0, [products]
     )(counts, mid, state, med, grad_first)
-    shot_devices = lax.axis_size("shot")
-    doubling = shot_devices == 4
+    sends = call(
+        functools.partial(late_pack_kernel, 1), by_line[1], [smem] + [vmem] * 3, "pack", 0.5
+    )(place, mid, send_list, halved[0])
+    ghosts += exchange(sends, 1)
+    doubling = lax.axis_size("shot") == 4
     if doubling:
-        cut = (nodes // 2 + SUBS // 2) // SUBS * SUBS
-        part_shapes = [pltpu.VMEM((3, size, slots), f32) for size in (cut, nodes - cut)]
-        halved = call(split_kernel, part_shapes, [vmem] * (1 + count), "gradient_split", 0)(grad, *ghosts)
         pieces = [swapped(halved[0], "shot", 1), swapped(halved[1], "shot", 2)]
     (acc,) = call(
-        second_faces_kernel, [state_shape], [smem] + [vmem] * 4, "second_faces", 4, aliases={1: 0}
+        second_faces_kernel, [state_shape], [vmem] + [vmem] * 4, "second_faces", 0.5, aliases={1: 0}
     )(counts, acc, mid, med, neighbours)
 
-    def add_ghosts(acc, chosen):
+    def add_ghosts(acc, chosen, micros):
         (acc,) = call(
             functools.partial(second_ghosts_kernel, chosen), [state_shape], [smem] + [vmem] * (3 + len(chosen)),
-            "second_ghosts", 2, aliases={1: 0},
+            "second_ghosts", micros, aliases={1: 0},
         )(place, acc, med, neighbours, *[ghosts[n] for n in chosen])
         return acc
 
-    acc = add_ghosts(acc, range(1))
+    acc = add_ghosts(acc, range(across), 1)
     if doubling:
         acc, *parts = call(
             partial_kernel, [state_shape] + part_shapes, [vmem] * 5, "gradient_partial", 0, aliases={0: 0}
         )(acc, *halved, *pieces)
         pieces = [swapped(parts[0], "shot", 2), swapped(parts[1], "shot", 1)]
     else:
-        gradient = lax.psum(grad, "shot")
-    acc = add_ghosts(acc, range(1, count))
+        gradient = lax.psum(jnp.concatenate(halved, axis=1), "shot")
+    acc = add_ghosts(acc, range(across, count), 1)
     (acc,) = call(
         other_sources_kernel, [state_shape], [smem] + [vmem] * (4 + count), "other_sources", 0, [outer], aliases={1: 0}
     )(place, acc, mid, med, neighbours, *ghosts)

time: 48.4 us -> 44.9 us (0.928)
  the two profiles are of different devices: /device:TPU:0 before, /device:TPU:1 now
where the time goes in v1:
time: 44.9 us; the launch traced here: 44.5 us
  Pallas kernels  25.8 us (57%)
  starting transfers between devices  15.1 us (34%)
  waiting for transfers between devices  2.07 us (5%)
  between operations  1.46 us (3%)
    ppermute x6, starting transfers between devices, exchange(): lax.ppermute(send, 'dom', route)  12.1 us
    pallas_call x1, Pallas kernels, shards(): call(first_kernel, [state_shape, grad_shape], [vmem] + [vmem] * 3, 'first...  6.02 us
    pallas_call x1, Pallas kernels, shards(): call(load_kernel, [pltpu.VMEM(apart, f32), med_shape], [hbm] * 3, 'load',...  3.78 us
    pallas_call x1, Pallas kernels, shards(): call(second_volume_kernel, [state_shape] + part_shapes, [vmem] + [vmem] *...  3.56 us
    pallas_call x1, Pallas kernels, shards(): call(second_faces_kernel, [state_shape], [vmem] + [vmem] * 4, 'second_fac...  3.06 us
    ppermute x4, starting transfers between devices, swapped(): return lax.ppermute(block, axis, route)  3.06 us
    pallas_call x1, Pallas kernels, shards(): call(middle_kernel, [state_shape] + by_line[0], [smem] + [vmem] * (5 + co...  2.3 us
    pallas_call x1, Pallas kernels, shards(): call(store_kernel, [part_shape, part_shape], [vmem], 'store', 4, [field_s...  2.29 us
  transfers between devices with their start and end apart: 10, of which 1 were waited for; matrix products, arithmetic and copies ran while one was open for 0% of the time, Pallas kernels for 42%

profile of v1, /device:TPU:1, one launch (start us, length us, event | category | flops | bytes accessed | tf_op | source)
XLA Modules:
  0.0 44.5 jit_solution(5363804572735789341)
XLA Ops:
  0.6 0.0 copy-start.1
  0.6 3.8 %load.1 = (f32[1125,2,2,2,128]{4,3,2,1,0:T(2,128)S(1)}, f32[500,8,128]{2,1,0:T(8,128)S(1)}) custom-call(f32[3,125,256]{2,1,0:T(8,128)} %mat_hbm.1, f32[1125,2,2,128]{3,2,1,0:T(2,128)} %bitcast.33, f32[1125,2,2,128]{3,2,1,0:T(2,128)} %bitcast.34), custom_call_target="tpu_custom_call" | custom-call | flops 4000000000 | tf_op jit(solution)/shard_map/load/pallas_call | solution.py:605
  4.4 0.0 copy-done.1
  4.4 0.0 copy-start
  4.5 0.4 pack.3
  4.9 3.2 %collective-permute-start = (f32[29,8,128]{2,1,0:T(8,128)S(1)}, f32[29,8,128]{2,1,0:T(8,128)S(1)}, u32[]{:S(2)}, u32[]{:S(2)}) collective-permute-start(f32[29,8,128]{2,1,0:T(8,128)S(1)} %pack.3), channel_id=1, source_target_pairs={{0,4},{1,5},{2,6},{3,7},{4,0},{5,1},{6,2},{7,3},{8,12},{9,13},{10,... | collective-permute-start | bytes 356360 | tf_op jit(solution)/shard_map/ppermute | solution.py:575
  8.1 0.7 %pack.4 = (f32[29,8,128]{2,1,0:T(8,128)S(1)}, f32[29,8,128]{2,1,0:T(8,128)S(1)}) custom-call(s32[1]{0:T(128)} %bitcast.place_ref, f32[1125,8,128]{2,1,0:T(8,128)S(1)} %bitcast.29, s32[1,4,32]{2,1,0:T(4,128)S(1)} %copy-done.1), custom_call_target="tpu_custom_call" | custom-call | tf_op jit(solution)/shard_map/pack/pallas_call | solution.py:614
  8.8 1.0 %collective-permute-start.1 = (f32[29,8,128]{2,1,0:T(8,128)S(1)}, f32[29,8,128]{2,1,0:T(8,128)S(1)}, u32[]{:S(2)}, u32[]{:S(2)}) collective-permute-start(f32[29,8,128]{2,1,0:T(8,128)S(1)} %get-tuple-element.24), channel_id=1, source_target_pairs={{0,1},{2,3},{4,5},{6,7},{1,0},{3,2},{5,4},{7,6},{8,9},{10,11},{12,... | collective-permute-start | bytes 356360 | tf_op jit(solution)/shard_map/ppermute | solution.py:575
  9.8 3.1 %collective-permute-start.2 = (f32[29,8,128]{2,1,0:T(8,128)S(1)}, f32[29,8,128]{2,1,0:T(8,128)S(1)}, u32[]{:S(2)}, u32[]{:S(2)}) collective-permute-start(f32[29,8,128]{2,1,0:T(8,128)S(1)} %get-tuple-element.25), channel_id=1, source_target_pairs={{1,2},{3,4},{5,6},{2,1},{4,3},{6,5},{9,10},{11,12},{13,14},{10,9},... | collective-permute-start | bytes 356360 | tf_op jit(solution)/shard_map/ppermute | solution.py:575
  13.5 0.0 copy-done
  13.6 6.0 %first_section.1 = (f32[1125,8,128]{2,1,0:T(8,128)S(1)}, f32[3,125,256]{2,1,0:T(8,128)S(1)}) custom-call(s32[1,1]{1,0:T(1,128)} %bitcast.24.counts_ref, f32[1125,8,128]{2,1,0:T(8,128)S(1)} %bitcast.30, f32[500,8,128]{2,1,0:T(8,128)S(1)} %get-tuple-element.22.med_ref, s32[1,1536]{1,0:T(1,128)S(1)} %copy-done), custom_call_target="tpu_custom_call" | custom-call | flops 8000000000 | tf_op jit(solution)/shard_map/first_section/pallas_call | solution.py:618
  19.6 0.0 collective-permute-done.rest_0_
  19.6 0.0 collective-permute-done.1.rest_1_
  19.6 0.0 collective-permute-done.2.rest_2_
  19.6 2.3 %first_ghosts.1 = (f32[1125,8,128]{2,1,0:T(8,128)S(1)}, f32[29,8,128]{2,1,0:T(8,128)S(1)}) custom-call(s32[1]{0:T(128)} %bitcast.place_ref, f32[1125,8,128]{2,1,0:T(8,128)S(1)} %get-tuple-element.23.acc_in, f32[1125,8,128]{2,1,0:T(8,128)S(1)} %bitcast.31, f32[500,8,128]{2,1,0:T(8,128)S(1)} %get-tuple-element.22.med_ref, ...), custom_call_target="tpu_custom_call", output_to_operand_aliasing={{0}: (1, {})} | custom-call | flops 4000000000 | tf_op jit(solution)/shard_map/first_ghosts/pallas_call | solution.py:621
  21.9 0.1 collective-permute-start.3
  22.0 3.6 %second_volume.1 = (f32[1125,8,128]{2,1,0:T(8,128)S(1)}, f32[3,64,256]{2,1,0:T(8,128)S(1)}, f32[3,61,256]{2,1,0:T(8,128)S(1)}) custom-call(s32[1,1]{1,0:T(1,128)} %bitcast.25.counts_ref, f32[1125,8,128]{2,1,0:T(8,128)S(1)} %get-tuple-element.26.mid_ref.state_ref, f32[1125,8,128]{2,1,0:T(8,128)S(1)} %bitcast.32, ...), custom_call_target="tpu_custom_call" | custom-call | tf_op jit(solution)/shard_map/second_volume/pallas_call | solution.py:628
  25.6 1.3 %collective-permute-start.4 = (f32[3,64,256]{2,1,0:T(8,128)S(1)}, f32[3,64,256]{2,1,0:T(8,128)S(1)}, u32[]{:S(2)}, u32[]{:S(2)}) collective-permute-start(f32[3,64,256]{2,1,0:T(8,128)S(1)} %get-tuple-element.30.a_ref.grad_ref), channel_id=1, source_target_pairs={{0,8},{8,0},{16,24},{24,16},{1,9},{9,1},{17,25},{25,17},{2,10},{10... | collective-permute-start | bytes 589832 | tf_op jit(solution)/shard_map/ppermute | solution.py:550
  26.9 1.2 %collective-permute-start.5 = (f32[3,61,256]{2,1,0:T(8,128)S(1)}, f32[3,61,256]{2,1,0:T(8,128)S(1)}, u32[]{:S(2)}, u32[]{:S(2)}) collective-permute-start(f32[3,61,256]{2,1,0:T(8,128)S(1)} %get-tuple-element.31.b_ref), channel_id=1, source_target_pairs={{0,16},{8,24},{16,0},{24,8},{1,17},{9,25},{17,1},{25,9},{2,18},{10... | collective-permute-start | bytes 562184 | tf_op jit(solution)/shard_map/ppermute | solution.py:550
  28.1 0.7 %pack.5 = (f32[29,8,128]{2,1,0:T(8,128)S(1)}, f32[29,8,128]{2,1,0:T(8,128)S(1)}) custom-call(s32[1]{0:T(128)} %bitcast.place_ref, f32[1125,8,128]{2,1,0:T(8,128)S(1)} %get-tuple-element.26.mid_ref.state_ref, s32[1,4,32]{2,1,0:T(4,128)S(1)} %copy-done.1, f32[3,64,256]{2,1,0:T(8,128)S(1)} %get-tuple-element.30.a_ref.grad_ref), custom_call_target="tpu_custom_call" | custom-call | flops 500000000 | tf_op jit(solution)/shard_map/pack/pallas_call | solution.py:631
  28.8 2.5 %collective-permute-start.6 = (f32[29,8,128]{2,1,0:T(8,128)S(1)}, f32[29,8,128]{2,1,0:T(8,128)S(1)}, u32[]{:S(2)}, u32[]{:S(2)}) collective-permute-start(f32[29,8,128]{2,1,0:T(8,128)S(1)} %get-tuple-element.33), channel_id=1, source_target_pairs={{0,1},{2,3},{4,5},{6,7},{1,0},{3,2},{5,4},{7,6},{8,9},{10,11},{12,... | collective-permute-start | bytes 356360 | tf_op jit(solution)/shard_map/ppermute | solution.py:575
  31.3 2.1 %collective-permute-start.7 = (f32[29,8,128]{2,1,0:T(8,128)S(1)}, f32[29,8,128]{2,1,0:T(8,128)S(1)}, u32[]{:S(2)}, u32[]{:S(2)}) collective-permute-start(f32[29,8,128]{2,1,0:T(8,128)S(1)} %get-tuple-element.34), channel_id=1, source_target_pairs={{1,2},{3,4},{5,6},{2,1},{4,3},{6,5},{9,10},{11,12},{13,14},{10,9},... | collective-permute-start | bytes 356360 | tf_op jit(solution)/shard_map/ppermute | solution.py:575
  33.4 3.1 %second_faces.1.acc_in = f32[1125,8,128]{2,1,0:T(8,128)S(1)} custom-call(s32[1,1]{1,0:T(1,128)} %bitcast.26.counts_ref, f32[1125,8,128]{2,1,0:T(8,128)S(1)} %get-tuple-element.28.acc_in, f32[1125,8,128]{2,1,0:T(8,128)S(1)} %get-tuple-element.26.mid_ref.state_ref, f32[500,8,128]{2,1,0:T(8,128)S(1)} %get-tuple-element.22.med_ref, ...), custom_call_target="tpu_custom_call", output_to_operand_aliasing={{}: (1, {})} | custom-call | flops 500000000 | tf_op jit(solution)/shard_map/second_faces/pallas_call | solution.py:638
  36.5 0.0 collective-permute-done.3.rest_0_
  36.5 0.7 %second_ghosts.2.acc_in = f32[1125,8,128]{2,1,0:T(8,128)S(1)} custom-call(s32[1]{0:T(128)} %bitcast.place_ref, f32[1125,8,128]{2,1,0:T(8,128)S(1)} %second_faces.1.acc_in, f32[500,8,128]{2,1,0:T(8,128)S(1)} %get-tuple-element.22.med_ref, s32[1,1536]{1,0:T(1,128)S(1)} %copy-done, ...), custom_call_target="tpu_custom_call", output_to_operand_aliasing={{}: (1, {})} | custom-call | flops 1000000000 | tf_op jit(solution)/shard_map/second_ghosts/pallas_call | solution.py:643
  37.2 0.0 collective-permute-done.5.far_ref
  37.2 0.0 collective-permute-done.4.near_ref
  37.3 0.3 collective-permute-start.8
  37.6 0.3 collective-permute-start.9
  37.8 0.0 collective-permute-done.6.rest_0_.rest_1_
  37.8 0.0 collective-permute-done.7.rest_1_.rest_2_
  37.8 1.3 %second_ghosts.3.acc_in = f32[1125,8,128]{2,1,0:T(8,128)S(1)} custom-call(s32[1]{0:T(128)} %bitcast.place_ref, f32[1125,8,128]{2,1,0:T(8,128)S(1)} %get-tuple-element.32.acc_in, f32[500,8,128]{2,1,0:T(8,128)S(1)} %get-tuple-element.22.med_ref, s32[1,1536]{1,0:T(1,128)S(1)} %copy-done, ...), custom_call_target="tpu_custom_call", output_to_operand_aliasing={{}: (1, {})} | custom-call | flops 1000000000 | tf_op jit(solution)/shard_map/second_ghosts/pallas_call | solution.py:643
  39.1 0.2 other_sources.1
  39.4 2.3 %store.1 = (f32[1125,2,2,128]{3,2,1,0:T(2,128)}, f32[1125,2,2,128]{3,2,1,0:T(2,128)}) custom-call(f32[1125,2,2,2,128]{4,3,2,1,0:T(2,128)S(1)} %bitcast.27), custom_call_target="tpu_custom_call" | custom-call | flops 4000000000 | tf_op jit(solution)/shard_map/store/pallas_call | solution.py:661
  41.7 2.0 %collective-permute-done.9.d_ref = f32[3,61,256]{2,1,0:T(8,128)S(1)} collective-permute-done((f32[3,61,256]{2,1,0:T(8,128)S(1)}, f32[3,61,256]{2,1,0:T(8,128)S(1)}, u32[]{:S(2)}, u32[]{:S(2)}) %collective-permute-start.9) | collective-permute-done | bytes 187424 | tf_op jit(solution)/shard_map/ppermute | solution.py:550
  43.7 0.0 collective-permute-done.8.c_ref
  43.7 0.8 %gradient_total.1 = f32[3,125,256]{2,1,0:T(8,128)} custom-call(f32[3,64,256]{2,1,0:T(8,128)S(1)} %get-tuple-element.37.a_ref, f32[3,61,256]{2,1,0:T(8,128)S(1)} %get-tuple-element.38.b_ref, f32[3,64,256]{2,1,0:T(8,128)S(1)} %collective-permute-done.8.c_ref, f32[3,61,256]{2,1,0:T(8,128)S(1)} %collective-permute-done.9.d_ref), custom_call_target="tpu_custom_call" | custom-call | tf_op jit(solution)/shard_map/gradient_total/pallas_call | solution.py:665
  (1 shorter events, 0.0 us)
Async XLA Ops:
  0.6 3.8 %copy-start.1 = (s32[1,4,32]{2,1,0:T(4,128)S(1)}, s32[1,4,32]{2,1,0:T(4,128)}, u32[]{:S(2)}) copy-start(s32[1,4,32]{2,1,0:T(4,128)} %list_ref.7) | copy-start | bytes 1540
  4.4 9.1 %copy-start = (s32[1,1536]{1,0:T(1,128)S(1)}, s32[1,1536]{1,0:T(1,128)}, u32[]{:S(2)}) copy-start(s32[1,1536]{1,0:T(1,128)} %codes_ref.11) | copy-start | bytes 18436
  4.9 14.7 %collective-permute-start = (f32[29,8,128]{2,1,0:T(8,128)S(1)}, f32[29,8,128]{2,1,0:T(8,128)S(1)}, u32[]{:S(2)}, u32[]{:S(2)}) collective-permute-start(f32[29,8,128]{2,1,0:T(8,128)S(1)} %pack.3), channel_id=1, source_target_pairs={{0,4},{1,5},{2,6},{3,7},{4,0},{5,1},{6,2},{7,3},{8,12},{9,13},{10,... | collective-permute-start | bytes 356360 | tf_op jit(solution)/shard_map/ppermute | solution.py:575
  8.8 10.8 %collective-permute-start.1 = (f32[29,8,128]{2,1,0:T(8,128)S(1)}, f32[29,8,128]{2,1,0:T(8,128)S(1)}, u32[]{:S(2)}, u32[]{:S(2)}) collective-permute-start(f32[29,8,128]{2,1,0:T(8,128)S(1)} %get-tuple-element.24), channel_id=1, source_target_pairs={{0,1},{2,3},{4,5},{6,7},{1,0},{3,2},{5,4},{7,6},{8,9},{10,11},{12,... | collective-permute-start | bytes 356360 | tf_op jit(solution)/shard_map/ppermute | solution.py:575
  9.8 9.8 %collective-permute-start.2 = (f32[29,8,128]{2,1,0:T(8,128)S(1)}, f32[29,8,128]{2,1,0:T(8,128)S(1)}, u32[]{:S(2)}, u32[]{:S(2)}) collective-permute-start(f32[29,8,128]{2,1,0:T(8,128)S(1)} %get-tuple-element.25), channel_id=1, source_target_pairs={{1,2},{3,4},{5,6},{2,1},{4,3},{6,5},{9,10},{11,12},{13,14},{10,9},... | collective-permute-start | bytes 356360 | tf_op jit(solution)/shard_map/ppermute | solution.py:575
  21.9 14.6 %collective-permute-start.3 = (f32[29,8,128]{2,1,0:T(8,128)S(1)}, f32[29,8,128]{2,1,0:T(8,128)S(1)}, u32[]{:S(2)}, u32[]{:S(2)}) collective-permute-start(f32[29,8,128]{2,1,0:T(8,128)S(1)} %get-tuple-element.29), channel_id=1, source_target_pairs={{0,4},{1,5},{2,6},{3,7},{4,0},{5,1},{6,2},{7,3},{8,12},{9,13},{10,... | collective-permute-start | bytes 356360 | tf_op jit(solution)/shard_map/ppermute | solution.py:575
  25.6 11.6 %collective-permute-start.4 = (f32[3,64,256]{2,1,0:T(8,128)S(1)}, f32[3,64,256]{2,1,0:T(8,128)S(1)}, u32[]{:S(2)}, u32[]{:S(2)}) collective-permute-start(f32[3,64,256]{2,1,0:T(8,128)S(1)} %get-tuple-element.30.a_ref.grad_ref), channel_id=1, source_target_pairs={{0,8},{8,0},{16,24},{24,16},{1,9},{9,1},{17,25},{25,17},{2,10},{10... | collective-permute-start | bytes 589832 | tf_op jit(solution)/shard_map/ppermute | solution.py:550
  26.9 10.3 %collective-permute-start.5 = (f32[3,61,256]{2,1,0:T(8,128)S(1)}, f32[3,61,256]{2,1,0:T(8,128)S(1)}, u32[]{:S(2)}, u32[]{:S(2)}) collective-permute-start(f32[3,61,256]{2,1,0:T(8,128)S(1)} %get-tuple-element.31.b_ref), channel_id=1, source_target_pairs={{0,16},{8,24},{16,0},{24,8},{1,17},{9,25},{17,1},{25,9},{2,18},{10... | collective-permute-start | bytes 562184 | tf_op jit(solution)/shard_map/ppermute | solution.py:550
  28.8 9.0 %collective-permute-start.6 = (f32[29,8,128]{2,1,0:T(8,128)S(1)}, f32[29,8,128]{2,1,0:T(8,128)S(1)}, u32[]{:S(2)}, u32[]{:S(2)}) collective-permute-start(f32[29,8,128]{2,1,0:T(8,128)S(1)} %get-tuple-element.33), channel_id=1, source_target_pairs={{0,1},{2,3},{4,5},{6,7},{1,0},{3,2},{5,4},{7,6},{8,9},{10,11},{12,... | collective-permute-start | bytes 356360 | tf_op jit(solution)/shard_map/ppermute | solution.py:575
  31.3 6.5 %collective-permute-start.7 = (f32[29,8,128]{2,1,0:T(8,128)S(1)}, f32[29,8,128]{2,1,0:T(8,128)S(1)}, u32[]{:S(2)}, u32[]{:S(2)}) collective-permute-start(f32[29,8,128]{2,1,0:T(8,128)S(1)} %get-tuple-element.34), channel_id=1, source_target_pairs={{1,2},{3,4},{5,6},{2,1},{4,3},{6,5},{9,10},{11,12},{13,14},{10,9},... | collective-permute-start | bytes 356360 | tf_op jit(solution)/shard_map/ppermute | solution.py:575
  37.3 6.4 %collective-permute-start.8 = (f32[3,64,256]{2,1,0:T(8,128)S(1)}, f32[3,64,256]{2,1,0:T(8,128)S(1)}, u32[]{:S(2)}, u32[]{:S(2)}) collective-permute-start(f32[3,64,256]{2,1,0:T(8,128)S(1)} %get-tuple-element.37.a_ref), channel_id=1, source_target_pairs={{0,16},{8,24},{16,0},{24,8},{1,17},{9,25},{17,1},{25,9},{2,18},{10... | collective-permute-start | bytes 589832 | tf_op jit(solution)/shard_map/ppermute | solution.py:550
  37.6 6.1 %collective-permute-start.9 = (f32[3,61,256]{2,1,0:T(8,128)S(1)}, f32[3,61,256]{2,1,0:T(8,128)S(1)}, u32[]{:S(2)}, u32[]{:S(2)}) collective-permute-start(f32[3,61,256]{2,1,0:T(8,128)S(1)} %get-tuple-element.38.b_ref), channel_id=1, source_target_pairs={{0,8},{8,0},{16,24},{24,16},{1,9},{9,1},{17,25},{25,17},{2,10},{10... | collective-permute-start | bytes 562184 | tf_op jit(solution)/shard_map/ppermute | solution.py:550

commit v2 on v1

--- a/solution.py
+++ b/solution.py
@@ -62,11 +62,6 @@
 
 def half_of():
     return sub_iota() >> 2
-
-
-def live_tile(counts_ref):
-    lane = lax.broadcasted_iota(jnp.int32, (SUBS, LANES), 1)
-    return half_of() * LANES + lane < jnp.broadcast_to(counts_ref[...], (SUBS, LANES))
 
 
 def swap_halves(x):
@@ -156,7 +151,7 @@
     return [med[m * NODES + node] for m in range(4)]
 
 
-def volume_pass(state, acc, med, products, average, scaled):
+def volume_pass(state, turned, acc, med, products, average, scaled):
     def x_lines(j, carry):
         for k in range(5):
             for field, row in ((0, 3), (1, 8), (2, 7), (3, 0), (8, 1), (7, 2)):
@@ -199,6 +194,7 @@
             volume += [mu * r for r in (r23, r13, r12)]
             own = [state[row * NODES + node] for row in range(FIELDS)]
             for row in range(FIELDS):
+                turned[row * NODES + node] = swap_halves(own[row])
                 acc[row * NODES + node] = average(own[row], row * NODES + node) + volume[row]
             dual = [pltpu.roll(x, SUBS - 2, axis=0) for x in own]
             pressure = div * (dual[3] + dual[4] + dual[5])
@@ -227,7 +223,7 @@
                 emit(m, 8 * g, rows, h, (first + second)[:rows])
 
 
-def local_pass(state, acc, med, codes_ref, slots, weight):
+def local_pass(state, turned, acc, med, codes_ref, slots, weight):
     half = half_of()
     low = half == 0
     free_code = 6 * slots + 4 * 32
@@ -252,7 +248,7 @@
                 for k in range(FIELDS):
                     there = state[k * NODES + source]
                     outer = jnp.where(same, lane_pick(there, idx), 0.0)
-                    outer = jnp.where(cross, lane_pick(swap_halves(there), idx), outer)
+                    outer = jnp.where(cross, lane_pick(turned[k * NODES + source], idx), outer)
                     jump = outer - state[k * NODES + node]
                     jumps.append(jump * (factor_v if k < 3 else factor_s))
                 add_rows(acc, node, jumps, coefs(med, node), face // 2, 2 * (face % 2) - 1)
@@ -406,8 +402,8 @@
     mat_copy = pltpu.make_async_copy(mat_hbm, mat_ref, mat_sem)
     mat_copy.start()
     copies = []
-    for k in range(FIELDS * ORDER):
-        span = pl.ds(k * FACE, FACE)
+    for k in range(FIELDS):
+        span = pl.ds(k * NODES, NODES)
         for n, far in enumerate((fwd_hbm, adj_hbm)):
             copies.append(pltpu.make_async_copy(far.at[span], state_ref.at[span, :, n], sems.at[n, k]))
             copies[-1].start()
@@ -428,8 +424,10 @@
     pack_links(slots, links, place_ref, state_ref, list_ref, sends, line)
 
 
-def late_pack_kernel(line, slots, links, place_ref, state_ref, list_ref, grad_ref, *sends):
-    pack_links(slots, links, place_ref, state_ref, list_ref, sends, line)
+def late_pack_kernel(slots, links, place_ref, state_ref, list_ref, grad_ref, *sends):
+    across = sum(link[0] == 0 for link in links)
+    pack_links(slots, links, place_ref, state_ref, list_ref, sends[:across], 0)
+    pack_links(slots, links, place_ref, state_ref, list_ref, sends[across:], 1)
 
 
 def spread_material(mat_ref, med_ref):
@@ -446,21 +444,23 @@
             med_ref[m * NODES + node] = step_size * value
 
 
-def first_kernel(slots, links, counts_ref, state_ref, med_ref, codes_ref, acc_ref, grad_ref, products):
-    volume_pass(state_ref, acc_ref, med_ref, products, lambda own, row: own, lambda value: value)
-    shot_sums(products, store_gradient(counts_ref, [grad_ref], None))
-    local_pass(state_ref, acc_ref, med_ref, codes_ref, slots, 0.5 * lift_weight)
-
-
-def store_gradient(counts_ref, grad_refs, earlier_ref):
+def first_kernel(slots, links, counts_ref, state_ref, med_ref, codes_ref, acc_ref, grad_ref, live_ref, products, turned):
     lane = lax.broadcasted_iota(jnp.int32, (SUBS, LANES), 1)
-    count = jnp.broadcast_to(counts_ref[...], (SUBS, LANES))
+    count = jnp.broadcast_to(counts_ref[...].reshape(1, 1), (SUBS, LANES))
+    live_ref[...] = jnp.where(half_of() * LANES + lane < count, 1.0, 0.0)
+    volume_pass(state_ref, turned, acc_ref, med_ref, products, lambda own, row: own, lambda value: value)
+    shot_sums(products, store_gradient(live_ref, [grad_ref], None))
+    local_pass(state_ref, turned, acc_ref, med_ref, codes_ref, slots, 0.5 * lift_weight)
+
+
+def store_gradient(live_ref, grad_refs, earlier_ref):
+    alive = [jnp.broadcast_to(live_ref[4 * h : 4 * h + 1, :], (SUBS, LANES)) > 0.0 for h in range(2)]
 
     def emit(m, start, rows, h, value):
         at = (m, slice(start, start + rows), slice(h * LANES, (h + 1) * LANES))
         if earlier_ref is not None:
             value = (0.5 * step_size) * (earlier_ref[at] + value)
-        value = jnp.where((h * LANES + lane < count)[:rows], value, 0.0)
+        value = jnp.where(alive[h][:rows], value, 0.0)
         for grad_ref in grad_refs:
             size = grad_ref.shape[1]
             if 0 <= start < size:
@@ -477,26 +477,26 @@
     other_sources(state_ref, acc_ref, med_ref, codes_ref, ghosts, ups, axes, outer, slots, scale)
 
 
-def middle_kernel(slots, links, place_ref, acc_in, state_ref, med_ref, codes_ref, list_ref, *rest):
-    count = len(links)
-    ghosts, mid_ref, sends, outer = rest[:count], rest[count], rest[count + 1 : -1], rest[-1]
+def middle_kernel(slots, links, place_ref, acc_in, state_ref, med_ref, codes_ref, *rest):
+    ghosts, (mid_ref, outer) = rest[: len(links)], rest[len(links) :]
     ups = link_ups(place_ref, links)
     ghost_stage(slots, links, ups, state_ref, mid_ref, med_ref, codes_ref, ghosts, outer, 0.5 * lift_weight)
-    pack_links(slots, links, place_ref, mid_ref, list_ref, sends, 0)
-
-
-def second_volume_kernel(slots, links, counts_ref, mid_ref, state_ref, med_ref, first_ref, acc_ref, near_ref, far_ref, products):
-    share = jnp.where(live_tile(counts_ref), 0.5, 0.0)
+
+
+def second_volume_kernel(
+    slots, links, live_ref, mid_ref, state_ref, med_ref, first_ref, acc_ref, turned, near_ref, far_ref, products
+):
+    share = 0.5 * live_ref[...]
     volume_pass(
-        mid_ref, acc_ref, med_ref, products,
+        mid_ref, turned, acc_ref, med_ref, products,
         lambda own, row: share * (own + state_ref[row]), lambda value: share * value,
     )
-    shot_sums(products, store_gradient(counts_ref, [near_ref, far_ref], first_ref))
-
-
-def second_faces_kernel(slots, links, counts_ref, acc_in, mid_ref, med_ref, codes_ref, acc_ref):
-    weight = jnp.where(live_tile(counts_ref), 0.25 * lift_weight, 0.0)
-    local_pass(mid_ref, acc_ref, med_ref, codes_ref, slots, weight)
+    shot_sums(products, store_gradient(live_ref, [near_ref, far_ref], first_ref))
+
+
+def second_faces_kernel(slots, links, live_ref, acc_in, mid_ref, turned, med_ref, codes_ref, acc_ref):
+    weight = (0.25 * lift_weight) * live_ref[...]
+    local_pass(mid_ref, turned, acc_ref, med_ref, codes_ref, slots, weight)
 
 
 def second_ghosts_kernel(chosen, slots, links, place_ref, acc_in, med_ref, codes_ref, *rest):
@@ -568,7 +568,6 @@
     links = tree_links(lax.axis_size("dom"))
     axes = tuple(link[:3] for link in links)
     place = lax.axis_index("dom").astype(jnp.int32).reshape(1)
-    counts = counts.reshape(1, 1)
 
     def exchange(sends, line):
         routes = [link[3] for link in links if link[0] == line]
@@ -604,8 +603,10 @@
     count = len(links)
     state, med = call(
         load_kernel, [pltpu.VMEM(apart, f32), med_shape], [hbm] * 3, "load", 4,
-        [pltpu.VMEM(material.shape, f32), pltpu.SemaphoreType.DMA((2, FIELDS * ORDER)), pltpu.SemaphoreType.DMA],
-    )(pltpu.with_memory_space_constraint(material, pltpu.HBM), dense(forward), dense(adjoint))
+        [pltpu.VMEM(material.shape, f32), field_sems, pltpu.SemaphoreType.DMA],
+    )(
+        pltpu.with_memory_space_constraint(material, pltpu.HBM), dense(forward), dense(adjoint),
+    )
     state = state.reshape(rows, SUBS, LANES)
     by_line = [[send_shape for link in links if link[0] == line] for line in range(2)]
     across = len(by_line[0])
@@ -615,29 +616,27 @@
             place, state, send_list
         )
         ghosts += exchange(sends, line)
-    acc, grad_first = call(
-        first_kernel, [state_shape, grad_shape], [vmem] + [vmem] * 3, "first_section", 8, [products]
+    acc, grad_first, live = call(
+        first_kernel, [state_shape, grad_shape, pltpu.VMEM((SUBS, LANES), f32)], [vmem] + [vmem] * 3, "first_section", 8, [products, pltpu.VMEM((rows, SUBS, LANES), f32)]
     )(counts, state, med, neighbours)
-    mid, *sends = call(
-        middle_kernel, [state_shape] + by_line[0], [smem] + [vmem] * (5 + count), "first_ghosts", 4,
-        [outer], aliases={1: 0},
-    )(place, acc, state, med, neighbours, send_list, *ghosts)
-    ghosts = exchange(sends, 0)
+    (mid,) = call(
+        middle_kernel, [state_shape], [smem] + [vmem] * (4 + count), "first_ghosts", 4, [outer], aliases={1: 0}
+    )(place, acc, state, med, neighbours, *ghosts)
     cut = (nodes // 2 + SUBS // 2) // SUBS * SUBS
     part_shapes = [pltpu.VMEM((3, size, slots), f32) for size in (cut, nodes - cut)]
-    acc, *halved = call(
-        second_volume_kernel, [state_shape] + part_shapes, [vmem] + [vmem] * 4, "second_volume", 0, [products]
-    )(counts, mid, state, med, grad_first)
-    sends = call(
-        functools.partial(late_pack_kernel, 1), by_line[1], [smem] + [vmem] * 3, "pack", 0.5
-    )(place, mid, send_list, halved[0])
-    ghosts += exchange(sends, 1)
+    acc, turned, *halved = call(
+        second_volume_kernel, [state_shape] * 2 + part_shapes, [vmem] + [vmem] * 4, "second_volume", 0, [products]
+    )(live, mid, state, med, grad_first)
+    sends = call(late_pack_kernel, [send_shape] * count, [smem] + [vmem] * 3, "pack", 0.5)(
+        place, mid, send_list, halved[0]
+    )
+    ghosts = exchange(sends[:across], 0) + exchange(sends[across:], 1)
     doubling = lax.axis_size("shot") == 4
     if doubling:
         pieces = [swapped(halved[0], "shot", 1), swapped(halved[1], "shot", 2)]
     (acc,) = call(
-        second_faces_kernel, [state_shape], [vmem] + [vmem] * 4, "second_faces", 0.5, aliases={1: 0}
-    )(counts, acc, mid, med, neighbours)
+        second_faces_kernel, [state_shape], [vmem] * 6, "second_faces", 0.5, aliases={1: 0}
+    )(live, acc, mid, turned, med, neighbours)
 
     def add_ghosts(acc, chosen, micros):
         (acc,) = call(
@@ -646,7 +645,6 @@
         )(place, acc, med, neighbours, *[ghosts[n] for n in chosen])
         return acc
 
-    acc = add_ghosts(acc, range(across), 1)
     if doubling:
         acc, *parts = call(
             partial_kernel, [state_shape] + part_shapes, [vmem] * 5, "gradient_partial", 0, aliases={0: 0}
@@ -654,7 +652,7 @@
         pieces = [swapped(parts[0], "shot", 2), swapped(parts[1], "shot", 1)]
     else:
         gradient = lax.psum(jnp.concatenate(halved, axis=1), "shot")
-    acc = add_ghosts(acc, range(across, count), 1)
+    acc = add_ghosts(acc, range(count), 1)
     (acc,) = call(
         other_sources_kernel, [state_shape], [smem] + [vmem] * (4 + count), "other_sources", 0, [outer], aliases={1: 0}
     )(place, acc, mid, med, neighbours, *ghosts)

time: 44.9 us -> 44 us (0.980)
  waiting for transfers between devices: 2.07 us -> 1.33 us
    ppermute x4, waiting for transfers between devices: 2.05 us -> 0.32 us  [swapped(): return lax.ppermute(block, axis, route)]
    ppermute x6, waiting for transfers between devices: 0.02 us -> 1.01 us  [exchange(): lax.ppermute(send, 'dom', route)]
    pallas_call x1, Pallas kernels: 3.78 us -> 2.98 us  [shards(): call(load_kernel, [pltpu.VMEM(apart, f32), med_shape], [hbm] * 3, 'load',...]
    pallas_call x5, Pallas kernels: 15.6 us -> 16.3 us  [the longest x1 6.43 us: shards(): call(first_kernel, [state_shape, grad_shape, pltpu.VMEM((SUBS, LANES), f3...]
    pallas_call x2 -> x1, Pallas kernels: 1.98 us -> 2.02 us  [add_ghosts(): call(functools.partial(second_ghosts_kernel, chosen), [state_shape], [sme...]
  transfers between devices with their start and end apart: 10 -> 10, of which waited for: 1 -> 2; matrix products, arithmetic and copies ran while one was open for 0% -> 0% of each run, Pallas kernels for 42% -> 37%
where the time goes in v2:
time: 44 us; the launch traced here: 43.6 us
  Pallas kernels  25.8 us (59%)
  starting transfers between devices  15.1 us (34%)
  between operations  1.45 us (3%)
  waiting for transfers between devices  1.33 us (3%)
    ppermute x6, starting transfers between devices, exchange(): lax.ppermute(send, 'dom', route)  12 us
    pallas_call x1, Pallas kernels, shards(): call(first_kernel, [state_shape, grad_shape, pltpu.VMEM((SUBS, LANES), f3...  6.43 us
    pallas_call x1, Pallas kernels, shards(): call(second_volume_kernel, [state_shape] * 2 + part_shapes, [vmem] + [vme...  3.73 us
    pallas_call x1, Pallas kernels, shards(): call(second_faces_kernel, [state_shape], [vmem] * 6, 'second_faces', 0.5,...  3.25 us
    ppermute x4, starting transfers between devices, swapped(): return lax.ppermute(block, axis, route)  3.06 us
    pallas_call x1, Pallas kernels, shards(): call(load_kernel, [pltpu.VMEM(apart, f32), med_shape], [hbm] * 3, 'load',...  2.98 us
    pallas_call x1, Pallas kernels, shards(): call(store_kernel, [part_shape, part_shape], [vmem], 'store', 4, [field_s...  2.29 us
    pallas_call x1, Pallas kernels, add_ghosts(): call(functools.partial(second_ghosts_kernel, chosen), [state_shape], [sme...  2.02 us
  transfers between devices with their start and end apart: 10, of which 2 were waited for; matrix products, arithmetic and copies ran while one was open for 0% of the time, Pallas kernels for 37%

profile of v2, /device:TPU:1, one launch (start us, length us, event | category | flops | bytes accessed | tf_op | source)
XLA Modules:
  0.0 43.6 jit_solution(18019288650748427961)
XLA Ops:
  0.6 0.0 copy-start.1
  0.6 3.0 %load.1 = (f32[1125,2,2,2,128]{4,3,2,1,0:T(2,128)S(1)}, f32[500,8,128]{2,1,0:T(8,128)S(1)}) custom-call(f32[3,125,256]{2,1,0:T(8,128)} %mat_hbm.1, f32[1125,2,2,128]{3,2,1,0:T(2,128)} %bitcast.29, f32[1125,2,2,128]{3,2,1,0:T(2,128)} %bitcast.30), custom_call_target="tpu_custom_call" | custom-call | flops 4000000000 | tf_op jit(solution)/shard_map/load/pallas_call | solution.py:604
  3.6 0.0 copy-done.1
  3.6 0.0 copy-start
  3.7 0.4 pack.3
  4.1 3.2 %collective-permute-start = (f32[29,8,128]{2,1,0:T(8,128)S(1)}, f32[29,8,128]{2,1,0:T(8,128)S(1)}, u32[]{:S(2)}, u32[]{:S(2)}) collective-permute-start(f32[29,8,128]{2,1,0:T(8,128)S(1)} %pack.3), channel_id=1, source_target_pairs={{0,4},{1,5},{2,6},{3,7},{4,0},{5,1},{6,2},{7,3},{8,12},{9,13},{10,... | collective-permute-start | bytes 356360 | tf_op jit(solution)/shard_map/ppermute | solution.py:574
  7.3 0.7 %pack.4 = (f32[29,8,128]{2,1,0:T(8,128)S(1)}, f32[29,8,128]{2,1,0:T(8,128)S(1)}) custom-call(s32[1]{0:T(128)} %bitcast.place_ref, f32[1125,8,128]{2,1,0:T(8,128)S(1)} %bitcast.24, s32[1,4,32]{2,1,0:T(4,128)S(1)} %copy-done.1), custom_call_target="tpu_custom_call" | custom-call | tf_op jit(solution)/shard_map/pack/pallas_call | solution.py:615
  8.0 1.0 %collective-permute-start.1 = (f32[29,8,128]{2,1,0:T(8,128)S(1)}, f32[29,8,128]{2,1,0:T(8,128)S(1)}, u32[]{:S(2)}, u32[]{:S(2)}) collective-permute-start(f32[29,8,128]{2,1,0:T(8,128)S(1)} %get-tuple-element.26), channel_id=1, source_target_pairs={{0,1},{2,3},{4,5},{6,7},{1,0},{3,2},{5,4},{7,6},{8,9},{10,11},{12,... | collective-permute-start | bytes 356360 | tf_op jit(solution)/shard_map/ppermute | solution.py:574
  9.0 3.1 %collective-permute-start.2 = (f32[29,8,128]{2,1,0:T(8,128)S(1)}, f32[29,8,128]{2,1,0:T(8,128)S(1)}, u32[]{:S(2)}, u32[]{:S(2)}) collective-permute-start(f32[29,8,128]{2,1,0:T(8,128)S(1)} %get-tuple-element.27), channel_id=1, source_target_pairs={{1,2},{3,4},{5,6},{2,1},{4,3},{6,5},{9,10},{11,12},{13,14},{10,9},... | collective-permute-start | bytes 356360 | tf_op jit(solution)/shard_map/ppermute | solution.py:574
  12.7 0.0 copy-done
  12.7 6.4 %first_section.1 = (f32[1125,8,128]{2,1,0:T(8,128)S(1)}, f32[3,125,256]{2,1,0:T(8,128)S(1)}, f32[8,128]{1,0:T(8,128)S(1)}) custom-call(s32[1]{0:T(128)S(6)} %copy.23.counts_ref, f32[1125,8,128]{2,1,0:T(8,128)S(1)} %bitcast.25, f32[500,8,128]{2,1,0:T(8,128)S(1)} %get-tuple-element.23.med_ref, s32[1,1536]{1,0:T(1,128)S(1)} %copy-done), custom_call_target="tpu_custom_call" | custom-call | flops 8000000000 | tf_op jit(solution)/shard_map/first_section/pallas_call | solution.py:619
  19.2 0.0 collective-permute-done.rest_0_
  19.2 0.0 collective-permute-done.1.rest_1_
  19.2 0.0 collective-permute-done.2.rest_2_
  19.2 1.9 %first_ghosts.1.mid_ref.state_ref = f32[1125,8,128]{2,1,0:T(8,128)S(1)} custom-call(s32[1]{0:T(128)} %bitcast.place_ref, f32[1125,8,128]{2,1,0:T(8,128)S(1)} %get-tuple-element.25.acc_in, f32[1125,8,128]{2,1,0:T(8,128)S(1)} %bitcast.26, f32[500,8,128]{2,1,0:T(8,128)S(1)} %get-tuple-element.23.med_ref, ...), custom_call_target="tpu_custom_call", output_to_operand_aliasing={{}: (1, {})} | custom-call | flops 4000000000 | tf_op jit(solution)/shard_map/first_ghosts/pallas_call | solution.py:622
  21.1 3.7 %second_volume.1 = (f32[1125,8,128]{2,1,0:T(8,128)S(1)}, f32[1125,8,128]{2,1,0:T(8,128)S(1)}, f32[3,64,256]{2,1,0:T(8,128)S(1)}, f32[3,61,256]{2,1,0:T(8,128)S(1)}) custom-call(f32[8,128]{1,0:T(8,128)S(1)} %get-tuple-element.24.live_ref, f32[1125,8,128]{2,1,0:T(8,128)S(1)} %first_ghosts.1.mid_ref.state_ref, f32[1125,8,128]{2,1,0:T(8,128)S(1)} %bitcast.27, ...), custom_call_target="tpu_custom_call" | custom-call | tf_op jit(solution)/shard_map/second_volume/pallas_call | solution.py:627
  24.9 1.3 %collective-permute-start.3 = (f32[3,64,256]{2,1,0:T(8,128)S(1)}, f32[3,64,256]{2,1,0:T(8,128)S(1)}, u32[]{:S(2)}, u32[]{:S(2)}) collective-permute-start(f32[3,64,256]{2,1,0:T(8,128)S(1)} %get-tuple-element.31.a_ref.grad_ref), channel_id=1, source_target_pairs={{0,8},{8,0},{16,24},{24,16},{1,9},{9,1},{17,25},{25,17},{2,10},{10... | collective-permute-start | bytes 589832 | tf_op jit(solution)/shard_map/ppermute | solution.py:550
  26.1 1.2 %collective-permute-start.4 = (f32[3,61,256]{2,1,0:T(8,128)S(1)}, f32[3,61,256]{2,1,0:T(8,128)S(1)}, u32[]{:S(2)}, u32[]{:S(2)}) collective-permute-start(f32[3,61,256]{2,1,0:T(8,128)S(1)} %get-tuple-element.32.b_ref), channel_id=1, source_target_pairs={{0,16},{8,24},{16,0},{24,8},{1,17},{9,25},{17,1},{25,9},{2,18},{10... | collective-permute-start | bytes 562184 | tf_op jit(solution)/shard_map/ppermute | solution.py:550
  27.4 1.0 %pack.5 = (f32[29,8,128]{2,1,0:T(8,128)S(1)}, f32[29,8,128]{2,1,0:T(8,128)S(1)}, f32[29,8,128]{2,1,0:T(8,128)S(1)}) custom-call(s32[1]{0:T(128)} %bitcast.place_ref, f32[1125,8,128]{2,1,0:T(8,128)S(1)} %first_ghosts.1.mid_ref.state_ref, s32[1,4,32]{2,1,0:T(4,128)S(1)} %copy-done.1, f32[3,64,256]{2,1,0:T(8,128)S(1)} %get-tuple-element.31.a_ref.grad_ref), custom_call_target="tpu_custom_call" | custom-call | flops 500000000 | tf_op jit(solution)/shard_map/pack/pallas_call | solution.py:630
  28.4 0.1 collective-permute-start.5
  28.5 2.5 %collective-permute-start.6 = (f32[29,8,128]{2,1,0:T(8,128)S(1)}, f32[29,8,128]{2,1,0:T(8,128)S(1)}, u32[]{:S(2)}, u32[]{:S(2)}) collective-permute-start(f32[29,8,128]{2,1,0:T(8,128)S(1)} %get-tuple-element.35), channel_id=1, source_target_pairs={{0,1},{2,3},{4,5},{6,7},{1,0},{3,2},{5,4},{7,6},{8,9},{10,11},{12,... | collective-permute-start | bytes 356360 | tf_op jit(solution)/shard_map/ppermute | solution.py:574
  31.0 2.1 %collective-permute-start.7 = (f32[29,8,128]{2,1,0:T(8,128)S(1)}, f32[29,8,128]{2,1,0:T(8,128)S(1)}, u32[]{:S(2)}, u32[]{:S(2)}) collective-permute-start(f32[29,8,128]{2,1,0:T(8,128)S(1)} %get-tuple-element.36), channel_id=1, source_target_pairs={{1,2},{3,4},{5,6},{2,1},{4,3},{6,5},{9,10},{11,12},{13,14},{10,9},... | collective-permute-start | bytes 356360 | tf_op jit(solution)/shard_map/ppermute | solution.py:574
  33.1 3.3 %second_faces.1.acc_in = f32[1125,8,128]{2,1,0:T(8,128)S(1)} custom-call(f32[8,128]{1,0:T(8,128)S(1)} %get-tuple-element.24.live_ref, f32[1125,8,128]{2,1,0:T(8,128)S(1)} %get-tuple-element.29.acc_in, f32[1125,8,128]{2,1,0:T(8,128)S(1)} %first_ghosts.1.mid_ref.state_ref, ...), custom_call_target="tpu_custom_call", output_to_operand_aliasing={{}: (1, {})} | custom-call | flops 500000000 | tf_op jit(solution)/shard_map/second_faces/pallas_call | solution.py:637
  36.3 0.0 collective-permute-done.4.far_ref
  36.3 0.0 collective-permute-done.3.near_ref
  36.4 0.3 collective-permute-start.8
  36.7 0.3 collective-permute-start.9
  37.0 0.0 collective-permute-done.5.rest_0_
  37.0 0.0 collective-permute-done.6.rest_1_
  37.0 1.0 %collective-permute-done.7.rest_2_ = f32[29,8,128]{2,1,0:T(8,128)S(1)} collective-permute-done((f32[29,8,128]{2,1,0:T(8,128)S(1)}, f32[29,8,128]{2,1,0:T(8,128)S(1)}, u32[]{:S(2)}, u32[]{:S(2)}) %collective-permute-start.7) | collective-permute-done | bytes 118816 | tf_op jit(solution)/shard_map/ppermute | solution.py:574
  38.0 2.0 %second_ghosts.1.acc_in = f32[1125,8,128]{2,1,0:T(8,128)S(1)} custom-call(s32[1]{0:T(128)} %bitcast.place_ref, f32[1125,8,128]{2,1,0:T(8,128)S(1)} %get-tuple-element.33.acc_in, f32[500,8,128]{2,1,0:T(8,128)S(1)} %get-tuple-element.23.med_ref, s32[1,1536]{1,0:T(1,128)S(1)} %copy-done, ...), custom_call_target="tpu_custom_call", output_to_operand_aliasing={{}: (1, {})} | custom-call | flops 1000000000 | tf_op jit(solution)/shard_map/second_ghosts/pallas_call | solution.py:642
  40.0 0.2 other_sources.1
  40.2 2.3 %store.1 = (f32[1125,2,2,128]{3,2,1,0:T(2,128)}, f32[1125,2,2,128]{3,2,1,0:T(2,128)}) custom-call(f32[1125,2,2,2,128]{4,3,2,1,0:T(2,128)S(1)} %bitcast.28), custom_call_target="tpu_custom_call" | custom-call | flops 4000000000 | tf_op jit(solution)/shard_map/store/pallas_call | solution.py:659
  42.5 0.3 collective-permute-done.9.d_ref
  42.8 0.0 collective-permute-done.8.c_ref
  42.8 0.8 %gradient_total.1 = f32[3,125,256]{2,1,0:T(8,128)} custom-call(f32[3,64,256]{2,1,0:T(8,128)S(1)} %get-tuple-element.39.a_ref, f32[3,61,256]{2,1,0:T(8,128)S(1)} %get-tuple-element.40.b_ref, f32[3,64,256]{2,1,0:T(8,128)S(1)} %collective-permute-done.8.c_ref, f32[3,61,256]{2,1,0:T(8,128)S(1)} %collective-permute-done.9.d_ref), custom_call_target="tpu_custom_call" | custom-call | tf_op jit(solution)/shard_map/gradient_total/pallas_call | solution.py:663
  (1 shorter events, 0.0 us)
Async XLA Ops:
  0.6 3.0 %copy-start.1 = (s32[1,4,32]{2,1,0:T(4,128)S(1)}, s32[1,4,32]{2,1,0:T(4,128)}, u32[]{:S(2)}) copy-start(s32[1,4,32]{2,1,0:T(4,128)} %list_ref.5) | copy-start | bytes 1540
  3.6 9.1 %copy-start = (s32[1,1536]{1,0:T(1,128)S(1)}, s32[1,1536]{1,0:T(1,128)}, u32[]{:S(2)}) copy-start(s32[1,1536]{1,0:T(1,128)} %codes_ref.9) | copy-start | bytes 18436
  4.1 15.1 %collective-permute-start = (f32[29,8,128]{2,1,0:T(8,128)S(1)}, f32[29,8,128]{2,1,0:T(8,128)S(1)}, u32[]{:S(2)}, u32[]{:S(2)}) collective-permute-start(f32[29,8,128]{2,1,0:T(8,128)S(1)} %pack.3), channel_id=1, source_target_pairs={{0,4},{1,5},{2,6},{3,7},{4,0},{5,1},{6,2},{7,3},{8,12},{9,13},{10,... | collective-permute-start | bytes 356360 | tf_op jit(solution)/shard_map/ppermute | solution.py:574
  8.0 11.2 %collective-permute-start.1 = (f32[29,8,128]{2,1,0:T(8,128)S(1)}, f32[29,8,128]{2,1,0:T(8,128)S(1)}, u32[]{:S(2)}, u32[]{:S(2)}) collective-permute-start(f32[29,8,128]{2,1,0:T(8,128)S(1)} %get-tuple-element.26), channel_id=1, source_target_pairs={{0,1},{2,3},{4,5},{6,7},{1,0},{3,2},{5,4},{7,6},{8,9},{10,11},{12,... | collective-permute-start | bytes 356360 | tf_op jit(solution)/shard_map/ppermute | solution.py:574
  9.0 10.2 %collective-permute-start.2 = (f32[29,8,128]{2,1,0:T(8,128)S(1)}, f32[29,8,128]{2,1,0:T(8,128)S(1)}, u32[]{:S(2)}, u32[]{:S(2)}) collective-permute-start(f32[29,8,128]{2,1,0:T(8,128)S(1)} %get-tuple-element.27), channel_id=1, source_target_pairs={{1,2},{3,4},{5,6},{2,1},{4,3},{6,5},{9,10},{11,12},{13,14},{10,9},... | collective-permute-start | bytes 356360 | tf_op jit(solution)/shard_map/ppermute | solution.py:574
  24.9 11.5 %collective-permute-start.3 = (f32[3,64,256]{2,1,0:T(8,128)S(1)}, f32[3,64,256]{2,1,0:T(8,128)S(1)}, u32[]{:S(2)}, u32[]{:S(2)}) collective-permute-start(f32[3,64,256]{2,1,0:T(8,128)S(1)} %get-tuple-element.31.a_ref.grad_ref), channel_id=1, source_target_pairs={{0,8},{8,0},{16,24},{24,16},{1,9},{9,1},{17,25},{25,17},{2,10},{10... | collective-permute-start | bytes 589832 | tf_op jit(solution)/shard_map/ppermute | solution.py:550
  26.1 10.2 %collective-permute-start.4 = (f32[3,61,256]{2,1,0:T(8,128)S(1)}, f32[3,61,256]{2,1,0:T(8,128)S(1)}, u32[]{:S(2)}, u32[]{:S(2)}) collective-permute-start(f32[3,61,256]{2,1,0:T(8,128)S(1)} %get-tuple-element.32.b_ref), channel_id=1, source_target_pairs={{0,16},{8,24},{16,0},{24,8},{1,17},{9,25},{17,1},{25,9},{2,18},{10... | collective-permute-start | bytes 562184 | tf_op jit(solution)/shard_map/ppermute | solution.py:550
  28.4 8.6 %collective-permute-start.5 = (f32[29,8,128]{2,1,0:T(8,128)S(1)}, f32[29,8,128]{2,1,0:T(8,128)S(1)}, u32[]{:S(2)}, u32[]{:S(2)}) collective-permute-start(f32[29,8,128]{2,1,0:T(8,128)S(1)} %get-tuple-element.34), channel_id=1, source_target_pairs={{0,4},{1,5},{2,6},{3,7},{4,0},{5,1},{6,2},{7,3},{8,12},{9,13},{10,... | collective-permute-start | bytes 356360 | tf_op jit(solution)/shard_map/ppermute | solution.py:574
  28.5 8.5 %collective-permute-start.6 = (f32[29,8,128]{2,1,0:T(8,128)S(1)}, f32[29,8,128]{2,1,0:T(8,128)S(1)}, u32[]{:S(2)}, u32[]{:S(2)}) collective-permute-start(f32[29,8,128]{2,1,0:T(8,128)S(1)} %get-tuple-element.35), channel_id=1, source_target_pairs={{0,1},{2,3},{4,5},{6,7},{1,0},{3,2},{5,4},{7,6},{8,9},{10,11},{12,... | collective-permute-start | bytes 356360 | tf_op jit(solution)/shard_map/ppermute | solution.py:574
  31.0 7.0 %collective-permute-start.7 = (f32[29,8,128]{2,1,0:T(8,128)S(1)}, f32[29,8,128]{2,1,0:T(8,128)S(1)}, u32[]{:S(2)}, u32[]{:S(2)}) collective-permute-start(f32[29,8,128]{2,1,0:T(8,128)S(1)} %get-tuple-element.36), channel_id=1, source_target_pairs={{1,2},{3,4},{5,6},{2,1},{4,3},{6,5},{9,10},{11,12},{13,14},{10,9},... | collective-permute-start | bytes 356360 | tf_op jit(solution)/shard_map/ppermute | solution.py:574
  36.4 6.4 %collective-permute-start.8 = (f32[3,64,256]{2,1,0:T(8,128)S(1)}, f32[3,64,256]{2,1,0:T(8,128)S(1)}, u32[]{:S(2)}, u32[]{:S(2)}) collective-permute-start(f32[3,64,256]{2,1,0:T(8,128)S(1)} %get-tuple-element.39.a_ref), channel_id=1, source_target_pairs={{0,16},{8,24},{16,0},{24,8},{1,17},{9,25},{17,1},{25,9},{2,18},{10... | collective-permute-start | bytes 589832 | tf_op jit(solution)/shard_map/ppermute | solution.py:550
  36.7 6.1 %collective-permute-start.9 = (f32[3,61,256]{2,1,0:T(8,128)S(1)}, f32[3,61,256]{2,1,0:T(8,128)S(1)}, u32[]{:S(2)}, u32[]{:S(2)}) collective-permute-start(f32[3,61,256]{2,1,0:T(8,128)S(1)} %get-tuple-element.40.b_ref), channel_id=1, source_target_pairs={{0,8},{8,0},{16,24},{24,16},{1,9},{9,1},{17,25},{25,17},{2,10},{10... | collective-permute-start | bytes 562184 | tf_op jit(solution)/shard_map/ppermute | solution.py:550

commit v3 on v2

--- a/solution.py
+++ b/solution.py
@@ -123,7 +123,7 @@
         out[FACE + g] = combine(parts)
 
 
-def add_rows(acc, node, jumps, coef, direction, sign):
+def correction(jumps, coef, direction, sign):
     lam, mu, buoy, speed = coef
     a, b, c = direction, (direction + 1) % 3, (direction + 2) % 3
     s_aa, s_bb, s_cc = 3 + a, 3 + b, 3 + c
@@ -139,20 +139,31 @@
         s_ab: mu * jumps[b],
         s_ac: mu * jumps[c],
     }
+    rows = []
     for k in range(FIELDS):
-        row = k * NODES + node
         total = speed * jumps[k]
         if k in flux:
             total = total + flux[k] if sign > 0 else total - flux[k]
-        acc[row] = acc[row] + total
+        rows.append(total)
+    return rows
+
+
+def add_rows(acc, node, rows):
+    for k in range(FIELDS):
+        row = k * NODES + node
+        acc[row] = acc[row] + rows[k]
 
 
 def coefs(med, node):
     return [med[m * NODES + node] for m in range(4)]
 
 
-def volume_pass(state, turned, acc, med, products, average, scaled):
-    def x_lines(j, carry):
+def volume_pass(state, of_face, acc, med, products, average, scaled):
+    lines = [of_face(face) for face in (0, 1)]
+
+    def x_lines(j, carry, lines=lines):
+        for line in lines:
+            line(j)
         for k in range(5):
             for field, row in ((0, 3), (1, 8), (2, 7), (3, 0), (8, 1), (7, 2)):
                 out = derivative([state[field * NODES + 25 * i + 5 * j + k] for i in range(5)])
@@ -162,7 +173,11 @@
 
     lax.fori_loop(0, ORDER, x_lines, 0)
 
-    def y_lines(i, carry):
+    lines = [of_face(face) for face in (2, 3)]
+
+    def y_lines(i, carry, lines=lines):
+        for line in lines:
+            line(i)
         for k in range(5):
             for field, row, more in ((0, 8, 1), (1, 4, 0), (2, 6, 0), (8, 0, 1), (4, 1, 1), (6, 2, 1)):
                 out = derivative([state[field * NODES + 25 * i + 5 * j + k] for j in range(5)])
@@ -194,7 +209,6 @@
             volume += [mu * r for r in (r23, r13, r12)]
             own = [state[row * NODES + node] for row in range(FIELDS)]
             for row in range(FIELDS):
-                turned[row * NODES + node] = swap_halves(own[row])
                 acc[row * NODES + node] = average(own[row], row * NODES + node) + volume[row]
             dual = [pltpu.roll(x, SUBS - 2, axis=0) for x in own]
             pressure = div * (dual[3] + dual[4] + dual[5])
@@ -204,7 +218,11 @@
             for m, value in enumerate((pressure, shear, light)):
                 products[pl.ds((m * LANES + node) * SUBS, SUBS), :] = value
 
-    def z_lines(i, carry):
+    lines = [of_face(face) for face in (4, 5)]
+
+    def z_lines(i, carry, lines=lines):
+        for line in lines:
+            line(i)
         for j in range(5):
             z_line(25 * i + 5 * j)
         return carry
@@ -223,11 +241,11 @@
                 emit(m, 8 * g, rows, h, (first + second)[:rows])
 
 
-def local_pass(state, turned, acc, med, codes_ref, slots, weight):
+def face_jumps(state, jumps, codes_ref, slots, weight):
     half = half_of()
-    low = half == 0
     free_code = 6 * slots + 4 * 32
-    for face in range(6):
+
+    def of_face(face):
         codes = code_tile(codes_ref, face, slots)
         idx = codes & (LANES - 1)
         match = (codes >> 8) == (face ^ 1)
@@ -238,23 +256,35 @@
         factor_s = jnp.where(free, 2.0 * weight, weight)
         other = face ^ 1
 
-        def body(u, carry, face=face, other=other, idx=idx, same=same, cross=cross,
-                 factor_v=factor_v, factor_s=factor_s):
+        def line(u):
             for v in range(ORDER):
                 shift = FACE_U[face] * u + FACE_V[face] * v
-                node = FACE_OFF[face] + shift
-                source = FACE_OFF[other] + shift
-                jumps = []
                 for k in range(FIELDS):
-                    there = state[k * NODES + source]
+                    there = state[k * NODES + FACE_OFF[other] + shift]
                     outer = jnp.where(same, lane_pick(there, idx), 0.0)
-                    outer = jnp.where(cross, lane_pick(turned[k * NODES + source], idx), outer)
-                    jump = outer - state[k * NODES + node]
-                    jumps.append(jump * (factor_v if k < 3 else factor_s))
-                add_rows(acc, node, jumps, coefs(med, node), face // 2, 2 * (face % 2) - 1)
-            return carry
-
-        lax.fori_loop(0, ORDER, body, 0, unroll=True)
+                    outer = jnp.where(cross, lane_pick(swap_halves(there), idx), outer)
+                    jump = outer - state[k * NODES + FACE_OFF[face] + shift]
+                    at = (face * FIELDS + k) * FACE + ORDER * u + v
+                    jumps[at] = jump * (factor_v if k < 3 else factor_s)
+
+        return line
+
+    return of_face
+
+
+def local_pass(jumps, acc, med):
+    for node in range(NODES):
+        place = (node // 25, node // 5 % 5, node % 5)
+        total = None
+        for axis in range(3):
+            if place[axis] in (0, 4):
+                face = 2 * axis + place[axis] // 4
+                u, v = [place[n] for n in range(3) if n != axis]
+                found = [jumps[(face * FIELDS + k) * FACE + ORDER * u + v] for k in range(FIELDS)]
+                rows = correction(found, coefs(med, node), axis, 2 * (face % 2) - 1)
+                total = rows if total is None else [x + y for x, y in zip(total, rows)]
+        if total is not None:
+            add_rows(acc, node, total)
 
 
 def ghost_tiles(ghost, p, low):
@@ -287,7 +317,7 @@
                 jumps.append(lane_pick(first if k < 4 else second, shifted[k % 4]) * weight)
             jumps.append(lane_pick(nine, idx + 32 * (p & 3)) * weight)
             lam, mu, buoy, speed = coefs(med, node)
-            add_rows(acc, node, jumps, (sign * lam, sign * mu, sign * buoy, speed), axis, 1)
+            add_rows(acc, node, correction(jumps, (sign * lam, sign * mu, sign * buoy, speed), axis, 1))
         return carry
 
     lax.fori_loop(0, ORDER, body, 0, unroll=True)
@@ -444,13 +474,14 @@
             med_ref[m * NODES + node] = step_size * value
 
 
-def first_kernel(slots, links, counts_ref, state_ref, med_ref, codes_ref, acc_ref, grad_ref, live_ref, products, turned):
+def first_kernel(slots, links, counts_ref, state_ref, med_ref, codes_ref, acc_ref, grad_ref, live_ref, products, jumps):
     lane = lax.broadcasted_iota(jnp.int32, (SUBS, LANES), 1)
     count = jnp.broadcast_to(counts_ref[...].reshape(1, 1), (SUBS, LANES))
     live_ref[...] = jnp.where(half_of() * LANES + lane < count, 1.0, 0.0)
-    volume_pass(state_ref, turned, acc_ref, med_ref, products, lambda own, row: own, lambda value: value)
+    of_face = face_jumps(state_ref, jumps, codes_ref, slots, 0.5 * lift_weight)
+    volume_pass(state_ref, of_face, acc_ref, med_ref, products, lambda own, row: own, lambda value: value)
     shot_sums(products, store_gradient(live_ref, [grad_ref], None))
-    local_pass(state_ref, turned, acc_ref, med_ref, codes_ref, slots, 0.5 * lift_weight)
+    local_pass(jumps, acc_ref, med_ref)
 
 
 def store_gradient(live_ref, grad_refs, earlier_ref):
@@ -484,19 +515,19 @@
 
 
 def second_volume_kernel(
-    slots, links, live_ref, mid_ref, state_ref, med_ref, first_ref, acc_ref, turned, near_ref, far_ref, products
+    slots, links, live_ref, mid_ref, state_ref, med_ref, codes_ref, first_ref, acc_ref, jumps, near_ref, far_ref, products
 ):
     share = 0.5 * live_ref[...]
+    of_face = face_jumps(mid_ref, jumps, codes_ref, slots, (0.25 * lift_weight) * live_ref[...])
     volume_pass(
-        mid_ref, turned, acc_ref, med_ref, products,
+        mid_ref, of_face, acc_ref, med_ref, products,
         lambda own, row: share * (own + state_ref[row]), lambda value: share * value,
     )
     shot_sums(products, store_gradient(live_ref, [near_ref, far_ref], first_ref))
 
 
-def second_faces_kernel(slots, links, live_ref, acc_in, mid_ref, turned, med_ref, codes_ref, acc_ref):
-    weight = (0.25 * lift_weight) * live_ref[...]
-    local_pass(mid_ref, turned, acc_ref, med_ref, codes_ref, slots, weight)
+def second_faces_kernel(slots, links, acc_in, jumps, med_ref, acc_ref):
+    local_pass(jumps, acc_ref, med_ref)
 
 
 def second_ghosts_kernel(chosen, slots, links, place_ref, acc_in, med_ref, codes_ref, *rest):
@@ -585,6 +616,7 @@
     part_shape = jax.ShapeDtypeStruct((rows, halves, shots, LANES), f32)
     products = pltpu.VMEM((3 * LANES * SUBS, LANES), f32)
     outer = pltpu.VMEM((FIELDS, SUBS, LANES), f32)
+    jumps_shape = pltpu.VMEM((6 * fields * FACE, SUBS, LANES), f32)
     field_sems = pltpu.SemaphoreType.DMA((2, FIELDS))
 
     def call(kernel, out_shape, in_specs, name, micros, scratch=(), out_specs=None, aliases=None):
@@ -617,16 +649,16 @@
         )
         ghosts += exchange(sends, line)
     acc, grad_first, live = call(
-        first_kernel, [state_shape, grad_shape, pltpu.VMEM((SUBS, LANES), f32)], [vmem] + [vmem] * 3, "first_section", 8, [products, pltpu.VMEM((rows, SUBS, LANES), f32)]
+        first_kernel, [state_shape, grad_shape, pltpu.VMEM((SUBS, LANES), f32)], [vmem] + [vmem] * 3, "first_section", 8, [products, jumps_shape]
     )(counts, state, med, neighbours)
     (mid,) = call(
         middle_kernel, [state_shape], [smem] + [vmem] * (4 + count), "first_ghosts", 4, [outer], aliases={1: 0}
     )(place, acc, state, med, neighbours, *ghosts)
     cut = (nodes // 2 + SUBS // 2) // SUBS * SUBS
     part_shapes = [pltpu.VMEM((3, size, slots), f32) for size in (cut, nodes - cut)]
-    acc, turned, *halved = call(
-        second_volume_kernel, [state_shape] * 2 + part_shapes, [vmem] + [vmem] * 4, "second_volume", 0, [products]
-    )(live, mid, state, med, grad_first)
+    acc, jumps, *halved = call(
+        second_volume_kernel, [state_shape, jumps_shape] + part_shapes, [vmem] * 6, "second_volume", 0, [products]
+    )(live, mid, state, med, neighbours, grad_first)
     sends = call(late_pack_kernel, [send_shape] * count, [smem] + [vmem] * 3, "pack", 0.5)(
         place, mid, send_list, halved[0]
     )
@@ -635,8 +667,8 @@
     if doubling:
         pieces = [swapped(halved[0], "shot", 1), swapped(halved[1], "shot", 2)]
     (acc,) = call(
-        second_faces_kernel, [state_shape], [vmem] * 6, "second_faces", 0.5, aliases={1: 0}
-    )(live, acc, mid, turned, med, neighbours)
+        second_faces_kernel, [state_shape], [vmem] * 3, "second_faces", 0.5, aliases={0: 0}
+    )(acc, jumps, med)
 
     def add_ghosts(acc, chosen, micros):
         (acc,) = call(

time: 44 us -> 48.3 us (1.098)
  waiting for transfers between devices: 1.33 us -> 3.97 us
  Pallas kernels: 25.8 us -> 27.8 us
    ppermute x6, waiting for transfers between devices: 1.01 us -> 3.95 us  [exchange(): lax.ppermute(send, 'dom', route)]
    pallas_call x1, Pallas kernels: 6.43 us -> 7.48 us  [shards(): call(first_kernel, [state_shape, grad_shape, pltpu.VMEM((SUBS, LANES), f3...]
    pallas_call x2, Pallas kernels: 6.98 us -> 8 us  [the longest x1 7.22 us: shards(): call(second_volume_kernel, [state_shape, jumps_shape] + part_shapes, [vme...]
  transfers between devices with their start and end apart: 10 -> 10, of which waited for: 2 -> 2; matrix products, arithmetic and copies ran while one was open for 0% -> 0% of each run, Pallas kernels for 37% -> 30%
where the time goes in v3:
time: 48.3 us; the launch traced here: 48.2 us
  Pallas kernels  27.8 us (58%)
  starting transfers between devices  14.9 us (31%)
  waiting for transfers between devices  3.97 us (8%)
  between operations  1.47 us (3%)
    ppermute x6, starting transfers between devices, exchange(): lax.ppermute(send, 'dom', route)  11.8 us
    pallas_call x1, Pallas kernels, shards(): call(first_kernel, [state_shape, grad_shape, pltpu.VMEM((SUBS, LANES), f3...  7.48 us
    pallas_call x1, Pallas kernels, shards(): call(second_volume_kernel, [state_shape, jumps_shape] + part_shapes, [vme...  7.22 us
    ppermute x6, waiting for transfers between devices, exchange(): lax.ppermute(send, 'dom', route)  3.95 us
    ppermute x4, starting transfers between devices, swapped(): return lax.ppermute(block, axis, route)  3.06 us
    pallas_call x1, Pallas kernels, shards(): call(load_kernel, [pltpu.VMEM(apart, f32), med_shape], [hbm] * 3, 'load',...  2.98 us
    pallas_call x1, Pallas kernels, shards(): call(store_kernel, [part_shape, part_shape], [vmem], 'store', 4, [field_s...  2.29 us
    pallas_call x1, Pallas kernels, add_ghosts(): call(functools.partial(second_ghosts_kernel, chosen), [state_shape], [sme...  2.02 us
  transfers between devices with their start and end apart: 10, of which 2 were waited for; matrix products, arithmetic and copies ran while one was open for 0% of the time, Pallas kernels for 30%

profile of v3, /device:TPU:1, one launch (start us, length us, event | category | flops | bytes accessed | tf_op | source)
XLA Modules:
  0.0 48.2 jit_solution(9772822219006178662)
XLA Ops:
  0.6 0.0 copy-start.1
  0.6 3.0 %load.1 = (f32[1125,2,2,2,128]{4,3,2,1,0:T(2,128)S(1)}, f32[500,8,128]{2,1,0:T(8,128)S(1)}) custom-call(f32[3,125,256]{2,1,0:T(8,128)} %mat_hbm.1, f32[1125,2,2,128]{3,2,1,0:T(2,128)} %bitcast.29, f32[1125,2,2,128]{3,2,1,0:T(2,128)} %bitcast.30), custom_call_target="tpu_custom_call" | custom-call | flops 4000000000 | tf_op jit(solution)/shard_map/load/pallas_call | solution.py:636
  3.6 0.0 copy-done.1
  3.6 0.0 copy-start
  3.7 0.4 pack.3
  4.1 3.2 %collective-permute-start = (f32[29,8,128]{2,1,0:T(8,128)S(1)}, f32[29,8,128]{2,1,0:T(8,128)S(1)}, u32[]{:S(2)}, u32[]{:S(2)}) collective-permute-start(f32[29,8,128]{2,1,0:T(8,128)S(1)} %pack.3), channel_id=1, source_target_pairs={{0,4},{1,5},{2,6},{3,7},{4,0},{5,1},{6,2},{7,3},{8,12},{9,13},{10,... | collective-permute-start | bytes 356360 | tf_op jit(solution)/shard_map/ppermute | solution.py:605
  7.3 0.7 %pack.4 = (f32[29,8,128]{2,1,0:T(8,128)S(1)}, f32[29,8,128]{2,1,0:T(8,128)S(1)}) custom-call(s32[1]{0:T(128)} %bitcast.place_ref, f32[1125,8,128]{2,1,0:T(8,128)S(1)} %bitcast.24, s32[1,4,32]{2,1,0:T(4,128)S(1)} %copy-done.1), custom_call_target="tpu_custom_call" | custom-call | tf_op jit(solution)/shard_map/pack/pallas_call | solution.py:647
  8.0 1.0 %collective-permute-start.1 = (f32[29,8,128]{2,1,0:T(8,128)S(1)}, f32[29,8,128]{2,1,0:T(8,128)S(1)}, u32[]{:S(2)}, u32[]{:S(2)}) collective-permute-start(f32[29,8,128]{2,1,0:T(8,128)S(1)} %get-tuple-element.26), channel_id=1, source_target_pairs={{0,1},{2,3},{4,5},{6,7},{1,0},{3,2},{5,4},{7,6},{8,9},{10,11},{12,... | collective-permute-start | bytes 356360 | tf_op jit(solution)/shard_map/ppermute | solution.py:605
  9.0 3.1 %collective-permute-start.2 = (f32[29,8,128]{2,1,0:T(8,128)S(1)}, f32[29,8,128]{2,1,0:T(8,128)S(1)}, u32[]{:S(2)}, u32[]{:S(2)}) collective-permute-start(f32[29,8,128]{2,1,0:T(8,128)S(1)} %get-tuple-element.27), channel_id=1, source_target_pairs={{1,2},{3,4},{5,6},{2,1},{4,3},{6,5},{9,10},{11,12},{13,14},{10,9},... | collective-permute-start | bytes 356360 | tf_op jit(solution)/shard_map/ppermute | solution.py:605
  12.7 0.0 copy-done
  12.7 7.5 %first_section.1 = (f32[1125,8,128]{2,1,0:T(8,128)S(1)}, f32[3,125,256]{2,1,0:T(8,128)S(1)}, f32[8,128]{1,0:T(8,128)S(1)}) custom-call(s32[1]{0:T(128)S(6)} %copy.23.counts_ref, f32[1125,8,128]{2,1,0:T(8,128)S(1)} %bitcast.25, f32[500,8,128]{2,1,0:T(8,128)S(1)} %get-tuple-element.23.med_ref, s32[1,1536]{1,0:T(1,128)S(1)} %copy-done), custom_call_target="tpu_custom_call" | custom-call | flops 8000000000 | tf_op jit(solution)/shard_map/first_section/pallas_call | solution.py:651
  20.2 0.0 collective-permute-done.rest_0_
  20.2 0.0 collective-permute-done.1.rest_1_
  20.3 0.0 collective-permute-done.2.rest_2_
  20.3 1.9 %first_ghosts.1.mid_ref.state_ref = f32[1125,8,128]{2,1,0:T(8,128)S(1)} custom-call(s32[1]{0:T(128)} %bitcast.place_ref, f32[1125,8,128]{2,1,0:T(8,128)S(1)} %get-tuple-element.25.acc_in, f32[1125,8,128]{2,1,0:T(8,128)S(1)} %bitcast.26, f32[500,8,128]{2,1,0:T(8,128)S(1)} %get-tuple-element.23.med_ref, ...), custom_call_target="tpu_custom_call", output_to_operand_aliasing={{}: (1, {})} | custom-call | flops 4000000000 | tf_op jit(solution)/shard_map/first_ghosts/pallas_call | solution.py:654
  22.2 7.2 %second_volume.1 = (f32[1125,8,128]{2,1,0:T(8,128)S(1)}, f32[1350,8,128]{2,1,0:T(8,128)S(1)}, f32[3,64,256]{2,1,0:T(8,128)S(1)}, f32[3,61,256]{2,1,0:T(8,128)S(1)}) custom-call(f32[8,128]{1,0:T(8,128)S(1)} %get-tuple-element.24.live_ref, f32[1125,8,128]{2,1,0:T(8,128)S(1)} %first_ghosts.1.mid_ref.state_ref, f32[1125,8,128]{2,1,0:T(8,128)S(1)} %bitcast.27, ...), custom_call_target="tpu_custom_call" | custom-call | tf_op jit(solution)/shard_map/second_volume/pallas_call | solution.py:659
  29.4 1.3 %collective-permute-start.3 = (f32[3,64,256]{2,1,0:T(8,128)S(1)}, f32[3,64,256]{2,1,0:T(8,128)S(1)}, u32[]{:S(2)}, u32[]{:S(2)}) collective-permute-start(f32[3,64,256]{2,1,0:T(8,128)S(1)} %get-tuple-element.31.a_ref.grad_ref), channel_id=1, source_target_pairs={{0,8},{8,0},{16,24},{24,16},{1,9},{9,1},{17,25},{25,17},{2,10},{10... | collective-permute-start | bytes 589832 | tf_op jit(solution)/shard_map/ppermute | solution.py:581
  30.7 1.2 %collective-permute-start.4 = (f32[3,61,256]{2,1,0:T(8,128)S(1)}, f32[3,61,256]{2,1,0:T(8,128)S(1)}, u32[]{:S(2)}, u32[]{:S(2)}) collective-permute-start(f32[3,61,256]{2,1,0:T(8,128)S(1)} %get-tuple-element.32.b_ref), channel_id=1, source_target_pairs={{0,16},{8,24},{16,0},{24,8},{1,17},{9,25},{17,1},{25,9},{2,18},{10... | collective-permute-start | bytes 562184 | tf_op jit(solution)/shard_map/ppermute | solution.py:581
  31.9 1.0 %pack.5 = (f32[29,8,128]{2,1,0:T(8,128)S(1)}, f32[29,8,128]{2,1,0:T(8,128)S(1)}, f32[29,8,128]{2,1,0:T(8,128)S(1)}) custom-call(s32[1]{0:T(128)} %bitcast.place_ref, f32[1125,8,128]{2,1,0:T(8,128)S(1)} %first_ghosts.1.mid_ref.state_ref, s32[1,4,32]{2,1,0:T(4,128)S(1)} %copy-done.1, f32[3,64,256]{2,1,0:T(8,128)S(1)} %get-tuple-element.31.a_ref.grad_ref), custom_call_target="tpu_custom_call" | custom-call | flops 500000000 | tf_op jit(solution)/shard_map/pack/pallas_call | solution.py:662
  32.9 0.1 collective-permute-start.5
  33.1 2.5 %collective-permute-start.6 = (f32[29,8,128]{2,1,0:T(8,128)S(1)}, f32[29,8,128]{2,1,0:T(8,128)S(1)}, u32[]{:S(2)}, u32[]{:S(2)}) collective-permute-start(f32[29,8,128]{2,1,0:T(8,128)S(1)} %get-tuple-element.35), channel_id=1, source_target_pairs={{0,1},{2,3},{4,5},{6,7},{1,0},{3,2},{5,4},{7,6},{8,9},{10,11},{12,... | collective-permute-start | bytes 356360 | tf_op jit(solution)/shard_map/ppermute | solution.py:605
  35.5 1.9 %collective-permute-start.7 = (f32[29,8,128]{2,1,0:T(8,128)S(1)}, f32[29,8,128]{2,1,0:T(8,128)S(1)}, u32[]{:S(2)}, u32[]{:S(2)}) collective-permute-start(f32[29,8,128]{2,1,0:T(8,128)S(1)} %get-tuple-element.36), channel_id=1, source_target_pairs={{1,2},{3,4},{5,6},{2,1},{4,3},{6,5},{9,10},{11,12},{13,14},{10,9},... | collective-permute-start | bytes 356360 | tf_op jit(solution)/shard_map/ppermute | solution.py:605
  37.4 0.8 %second_faces.1.acc_in = f32[1125,8,128]{2,1,0:T(8,128)S(1)} custom-call(f32[1125,8,128]{2,1,0:T(8,128)S(1)} %get-tuple-element.29.acc_in, f32[1350,8,128]{2,1,0:T(8,128)S(1)} %get-tuple-element.30.jumps, f32[500,8,128]{2,1,0:T(8,128)S(1)} %get-tuple-element.23.med_ref), custom_call_target="tpu_custom_call", output_to_operand_aliasing={{}: (0, {})} | custom-call | flops 500000000 | tf_op jit(solution)/shard_map/second_faces/pallas_call | solution.py:669
  38.2 0.0 collective-permute-done.4.far_ref
  38.2 0.0 collective-permute-done.3.near_ref
  38.3 0.3 collective-permute-start.8
  38.6 0.3 collective-permute-start.9
  38.8 2.7 %collective-permute-done.5.rest_0_ = f32[29,8,128]{2,1,0:T(8,128)S(1)} collective-permute-done((f32[29,8,128]{2,1,0:T(8,128)S(1)}, f32[29,8,128]{2,1,0:T(8,128)S(1)}, u32[]{:S(2)}, u32[]{:S(2)}) %collective-permute-start.5) | collective-permute-done | bytes 118816 | tf_op jit(solution)/shard_map/ppermute | solution.py:605
  41.5 0.0 collective-permute-done.6.rest_1_
  41.5 1.3 %collective-permute-done.7.rest_2_ = f32[29,8,128]{2,1,0:T(8,128)S(1)} collective-permute-done((f32[29,8,128]{2,1,0:T(8,128)S(1)}, f32[29,8,128]{2,1,0:T(8,128)S(1)}, u32[]{:S(2)}, u32[]{:S(2)}) %collective-permute-start.7) | collective-permute-done | bytes 118816 | tf_op jit(solution)/shard_map/ppermute | solution.py:605
  42.8 2.0 %second_ghosts.1.acc_in = f32[1125,8,128]{2,1,0:T(8,128)S(1)} custom-call(s32[1]{0:T(128)} %bitcast.place_ref, f32[1125,8,128]{2,1,0:T(8,128)S(1)} %get-tuple-element.33.acc_in, f32[500,8,128]{2,1,0:T(8,128)S(1)} %get-tuple-element.23.med_ref, s32[1,1536]{1,0:T(1,128)S(1)} %copy-done, ...), custom_call_target="tpu_custom_call", output_to_operand_aliasing={{}: (1, {})} | custom-call | flops 1000000000 | tf_op jit(solution)/shard_map/second_ghosts/pallas_call | solution.py:674
  44.8 0.2 other_sources.1
  45.0 2.3 %store.1 = (f32[1125,2,2,128]{3,2,1,0:T(2,128)}, f32[1125,2,2,128]{3,2,1,0:T(2,128)}) custom-call(f32[1125,2,2,2,128]{4,3,2,1,0:T(2,128)S(1)} %bitcast.28), custom_call_target="tpu_custom_call" | custom-call | flops 4000000000 | tf_op jit(solution)/shard_map/store/pallas_call | solution.py:691
  47.3 0.0 collective-permute-done.9.d_ref
  47.4 0.0 collective-permute-done.8.c_ref
  47.4 0.8 %gradient_total.1 = f32[3,125,256]{2,1,0:T(8,128)} custom-call(f32[3,64,256]{2,1,0:T(8,128)S(1)} %get-tuple-element.39.a_ref, f32[3,61,256]{2,1,0:T(8,128)S(1)} %get-tuple-element.40.b_ref, f32[3,64,256]{2,1,0:T(8,128)S(1)} %collective-permute-done.8.c_ref, f32[3,61,256]{2,1,0:T(8,128)S(1)} %collective-permute-done.9.d_ref), custom_call_target="tpu_custom_call" | custom-call | tf_op jit(solution)/shard_map/gradient_total/pallas_call | solution.py:695
  (1 shorter events, 0.0 us)
Async XLA Ops:
  0.6 3.0 %copy-start.1 = (s32[1,4,32]{2,1,0:T(4,128)S(1)}, s32[1,4,32]{2,1,0:T(4,128)}, u32[]{:S(2)}) copy-start(s32[1,4,32]{2,1,0:T(4,128)} %list_ref.5) | copy-start | bytes 1540
  3.6 9.1 %copy-start = (s32[1,1536]{1,0:T(1,128)S(1)}, s32[1,1536]{1,0:T(1,128)}, u32[]{:S(2)}) copy-start(s32[1,1536]{1,0:T(1,128)} %codes_ref.9) | copy-start | bytes 18436
  4.1 16.2 %collective-permute-start = (f32[29,8,128]{2,1,0:T(8,128)S(1)}, f32[29,8,128]{2,1,0:T(8,128)S(1)}, u32[]{:S(2)}, u32[]{:S(2)}) collective-permute-start(f32[29,8,128]{2,1,0:T(8,128)S(1)} %pack.3), channel_id=1, source_target_pairs={{0,4},{1,5},{2,6},{3,7},{4,0},{5,1},{6,2},{7,3},{8,12},{9,13},{10,... | collective-permute-start | bytes 356360 | tf_op jit(solution)/shard_map/ppermute | solution.py:605
  8.0 12.3 %collective-permute-start.1 = (f32[29,8,128]{2,1,0:T(8,128)S(1)}, f32[29,8,128]{2,1,0:T(8,128)S(1)}, u32[]{:S(2)}, u32[]{:S(2)}) collective-permute-start(f32[29,8,128]{2,1,0:T(8,128)S(1)} %get-tuple-element.26), channel_id=1, source_target_pairs={{0,1},{2,3},{4,5},{6,7},{1,0},{3,2},{5,4},{7,6},{8,9},{10,11},{12,... | collective-permute-start | bytes 356360 | tf_op jit(solution)/shard_map/ppermute | solution.py:605
  9.0 11.3 %collective-permute-start.2 = (f32[29,8,128]{2,1,0:T(8,128)S(1)}, f32[29,8,128]{2,1,0:T(8,128)S(1)}, u32[]{:S(2)}, u32[]{:S(2)}) collective-permute-start(f32[29,8,128]{2,1,0:T(8,128)S(1)} %get-tuple-element.27), channel_id=1, source_target_pairs={{1,2},{3,4},{5,6},{2,1},{4,3},{6,5},{9,10},{11,12},{13,14},{10,9},... | collective-permute-start | bytes 356360 | tf_op jit(solution)/shard_map/ppermute | solution.py:605
  29.4 8.8 %collective-permute-start.3 = (f32[3,64,256]{2,1,0:T(8,128)S(1)}, f32[3,64,256]{2,1,0:T(8,128)S(1)}, u32[]{:S(2)}, u32[]{:S(2)}) collective-permute-start(f32[3,64,256]{2,1,0:T(8,128)S(1)} %get-tuple-element.31.a_ref.grad_ref), channel_id=1, source_target_pairs={{0,8},{8,0},{16,24},{24,16},{1,9},{9,1},{17,25},{25,17},{2,10},{10... | collective-permute-start | bytes 589832 | tf_op jit(solution)/shard_map/ppermute | solution.py:581
  30.7 7.5 %collective-permute-start.4 = (f32[3,61,256]{2,1,0:T(8,128)S(1)}, f32[3,61,256]{2,1,0:T(8,128)S(1)}, u32[]{:S(2)}, u32[]{:S(2)}) collective-permute-start(f32[3,61,256]{2,1,0:T(8,128)S(1)} %get-tuple-element.32.b_ref), channel_id=1, source_target_pairs={{0,16},{8,24},{16,0},{24,8},{1,17},{9,25},{17,1},{25,9},{2,18},{10... | collective-permute-start | bytes 562184 | tf_op jit(solution)/shard_map/ppermute | solution.py:581
  32.9 8.6 %collective-permute-start.5 = (f32[29,8,128]{2,1,0:T(8,128)S(1)}, f32[29,8,128]{2,1,0:T(8,128)S(1)}, u32[]{:S(2)}, u32[]{:S(2)}) collective-permute-start(f32[29,8,128]{2,1,0:T(8,128)S(1)} %get-tuple-element.34), channel_id=1, source_target_pairs={{0,4},{1,5},{2,6},{3,7},{4,0},{5,1},{6,2},{7,3},{8,12},{9,13},{10,... | collective-permute-start | bytes 356360 | tf_op jit(solution)/shard_map/ppermute | solution.py:605
  33.1 8.5 %collective-permute-start.6 = (f32[29,8,128]{2,1,0:T(8,128)S(1)}, f32[29,8,128]{2,1,0:T(8,128)S(1)}, u32[]{:S(2)}, u32[]{:S(2)}) collective-permute-start(f32[29,8,128]{2,1,0:T(8,128)S(1)} %get-tuple-element.35), channel_id=1, source_target_pairs={{0,1},{2,3},{4,5},{6,7},{1,0},{3,2},{5,4},{7,6},{8,9},{10,11},{12,... | collective-permute-start | bytes 356360 | tf_op jit(solution)/shard_map/ppermute | solution.py:605
  35.5 7.3 %collective-permute-start.7 = (f32[29,8,128]{2,1,0:T(8,128)S(1)}, f32[29,8,128]{2,1,0:T(8,128)S(1)}, u32[]{:S(2)}, u32[]{:S(2)}) collective-permute-start(f32[29,8,128]{2,1,0:T(8,128)S(1)} %get-tuple-element.36), channel_id=1, source_target_pairs={{1,2},{3,4},{5,6},{2,1},{4,3},{6,5},{9,10},{11,12},{13,14},{10,9},... | collective-permute-start | bytes 356360 | tf_op jit(solution)/shard_map/ppermute | solution.py:605
  38.3 9.1 %collective-permute-start.8 = (f32[3,64,256]{2,1,0:T(8,128)S(1)}, f32[3,64,256]{2,1,0:T(8,128)S(1)}, u32[]{:S(2)}, u32[]{:S(2)}) collective-permute-start(f32[3,64,256]{2,1,0:T(8,128)S(1)} %get-tuple-element.39.a_ref), channel_id=1, source_target_pairs={{0,16},{8,24},{16,0},{24,8},{1,17},{9,25},{17,1},{25,9},{2,18},{10... | collective-permute-start | bytes 589832 | tf_op jit(solution)/shard_map/ppermute | solution.py:581
  38.6 8.8 %collective-permute-start.9 = (f32[3,61,256]{2,1,0:T(8,128)S(1)}, f32[3,61,256]{2,1,0:T(8,128)S(1)}, u32[]{:S(2)}, u32[]{:S(2)}) collective-permute-start(f32[3,61,256]{2,1,0:T(8,128)S(1)} %get-tuple-element.40.b_ref), channel_id=1, source_target_pairs={{0,8},{8,0},{16,24},{24,16},{1,9},{9,1},{17,25},{25,17},{2,10},{10... | collective-permute-start | bytes 562184 | tf_op jit(solution)/shard_map/ppermute | solution.py:581

commit v4 on v2

--- a/solution.py
+++ b/solution.py
@@ -151,7 +151,7 @@
     return [med[m * NODES + node] for m in range(4)]
 
 
-def volume_pass(state, turned, acc, med, products, average, scaled):
+def volume_pass(state, acc, med, products, average, scaled):
     def x_lines(j, carry):
         for k in range(5):
             for field, row in ((0, 3), (1, 8), (2, 7), (3, 0), (8, 1), (7, 2)):
@@ -194,7 +194,6 @@
             volume += [mu * r for r in (r23, r13, r12)]
             own = [state[row * NODES + node] for row in range(FIELDS)]
             for row in range(FIELDS):
-                turned[row * NODES + node] = swap_halves(own[row])
                 acc[row * NODES + node] = average(own[row], row * NODES + node) + volume[row]
             dual = [pltpu.roll(x, SUBS - 2, axis=0) for x in own]
             pressure = div * (dual[3] + dual[4] + dual[5])
@@ -223,7 +222,7 @@
                 emit(m, 8 * g, rows, h, (first + second)[:rows])
 
 
-def local_pass(state, turned, acc, med, codes_ref, slots, weight):
+def local_pass(state, acc, med, codes_ref, slots, weight):
     half = half_of()
     low = half == 0
     free_code = 6 * slots + 4 * 32
@@ -248,7 +247,7 @@
                 for k in range(FIELDS):
                     there = state[k * NODES + source]
                     outer = jnp.where(same, lane_pick(there, idx), 0.0)
-                    outer = jnp.where(cross, lane_pick(turned[k * NODES + source], idx), outer)
+                    outer = jnp.where(cross, lane_pick(swap_halves(there), idx), outer)
                     jump = outer - state[k * NODES + node]
                     jumps.append(jump * (factor_v if k < 3 else factor_s))
                 add_rows(acc, node, jumps, coefs(med, node), face // 2, 2 * (face % 2) - 1)
@@ -266,13 +265,13 @@
     return jnp.where(low, tile, turned), jnp.where(low, turned, tile), jnp.where(chosen, tile9, turned9)
 
 
-def ghost_pass(acc, med, codes_ref, ghost, axis, up, slots, scale):
+def ghost_pass(acc, med, codes_ref, ghost, axis, up, paired, slots, scale):
     low = half_of() == 0
     face = 2 * axis + up
     sign = (2 * up - 1).astype(jnp.float32)
     codes = code_tile(codes_ref, face, slots) - (6 * slots + 32 * face)
     inside = (codes >= 0) & (codes < 32)
-    weight = jnp.where(inside, scale, 0.0)
+    weight = jnp.where(inside, jnp.where(paired, scale, 0.0), 0.0)
     idx = codes & 31
     shifted = [idx + 32 * q for q in range(4)]
     start = side_offset(axis, up)
@@ -293,7 +292,7 @@
     lax.fori_loop(0, ORDER, body, 0, unroll=True)
 
 
-def other_sources(state, acc, med, codes_ref, ghosts, ups, axes, outer, slots, scale):
+def other_sources(state, acc, med, codes_ref, ghosts, ups, paired, axes, outer, slots, scale):
     half = half_of()
     low = half == 0
     first_ghost = 6 * slots
@@ -353,9 +352,9 @@
                         for k in range(FIELDS):
                             outer[k] = jnp.zeros((SUBS, LANES), jnp.float32)
 
-                    for ghost, up, line in zip(ghosts, ups, axes):
-
-                        @pl.when(origin == 6 + 2 * line + up)
+                    for ghost, up, pair_here, line in zip(ghosts, ups, paired, axes):
+
+                        @pl.when((origin == 6 + 2 * line + up) & pair_here)
                         def _(ghost=ghost):
                             idx = (codes - first_ghost) & 31
                             first, second, nine = ghost_tiles(ghost, p, low)
@@ -395,7 +394,12 @@
 
 
 def link_ups(place_ref, links):
-    return [1 - ((lax.div(place_ref[0], stride) + parity) & 1) for _, stride, parity in links]
+    return [1 - ((lax.div(place_ref[0], stride) + parity) & 1) for _, stride, parity, _ in links]
+
+
+def link_paired(place_ref, links, ups):
+    others = [place_ref[0] + (2 * up - 1) * link[1] for up, link in zip(ups, links)]
+    return [(other >= 0) & (other < link[3]) for other, link in zip(others, links)]
 
 
 def load_kernel(slots, links, mat_hbm, fwd_hbm, adj_hbm, state_ref, med_ref, mat_ref, sems, mat_sem):
@@ -444,13 +448,13 @@
             med_ref[m * NODES + node] = step_size * value
 
 
-def first_kernel(slots, links, counts_ref, state_ref, med_ref, codes_ref, acc_ref, grad_ref, live_ref, products, turned):
+def first_kernel(slots, links, counts_ref, state_ref, med_ref, codes_ref, acc_ref, grad_ref, live_ref, products):
     lane = lax.broadcasted_iota(jnp.int32, (SUBS, LANES), 1)
     count = jnp.broadcast_to(counts_ref[...].reshape(1, 1), (SUBS, LANES))
     live_ref[...] = jnp.where(half_of() * LANES + lane < count, 1.0, 0.0)
-    volume_pass(state_ref, turned, acc_ref, med_ref, products, lambda own, row: own, lambda value: value)
+    volume_pass(state_ref, acc_ref, med_ref, products, lambda own, row: own, lambda value: value)
     shot_sums(products, store_gradient(live_ref, [grad_ref], None))
-    local_pass(state_ref, turned, acc_ref, med_ref, codes_ref, slots, 0.5 * lift_weight)
+    local_pass(state_ref, acc_ref, med_ref, codes_ref, slots, 0.5 * lift_weight)
 
 
 def store_gradient(live_ref, grad_refs, earlier_ref):
@@ -470,47 +474,46 @@
     return emit
 
 
-def ghost_stage(slots, links, ups, state_ref, acc_ref, med_ref, codes_ref, ghosts, outer, scale):
+def add_ghosts(links, place_ref, acc_ref, med_ref, codes_ref, ghosts, slots, scale):
+    ups = link_ups(place_ref, links)
+    paired = link_paired(place_ref, links, ups)
+    for link, up, pair_here, ghost in zip(links, ups, paired, ghosts):
+        ghost_pass(acc_ref, med_ref, codes_ref, ghost, link[0], up, pair_here, slots, scale)
+
+
+def add_others(links, place_ref, state_ref, acc_ref, med_ref, codes_ref, ghosts, outer, slots, scale):
+    ups = link_ups(place_ref, links)
+    paired = link_paired(place_ref, links, ups)
     axes = [link[0] for link in links]
-    for axis, up, ghost in zip(axes, ups, ghosts):
-        ghost_pass(acc_ref, med_ref, codes_ref, ghost, axis, up, slots, scale)
-    other_sources(state_ref, acc_ref, med_ref, codes_ref, ghosts, ups, axes, outer, slots, scale)
+    other_sources(state_ref, acc_ref, med_ref, codes_ref, ghosts, ups, paired, axes, outer, slots, scale)
 
 
 def middle_kernel(slots, links, place_ref, acc_in, state_ref, med_ref, codes_ref, *rest):
     ghosts, (mid_ref, outer) = rest[: len(links)], rest[len(links) :]
-    ups = link_ups(place_ref, links)
-    ghost_stage(slots, links, ups, state_ref, mid_ref, med_ref, codes_ref, ghosts, outer, 0.5 * lift_weight)
+    add_ghosts(links, place_ref, mid_ref, med_ref, codes_ref, ghosts, slots, 0.5 * lift_weight)
+    add_others(links, place_ref, state_ref, mid_ref, med_ref, codes_ref, ghosts, outer, slots, 0.5 * lift_weight)
 
 
 def second_volume_kernel(
-    slots, links, live_ref, mid_ref, state_ref, med_ref, first_ref, acc_ref, turned, near_ref, far_ref, products
+    slots, links, live_ref, mid_ref, state_ref, med_ref, first_ref, acc_ref, near_ref, far_ref, products
 ):
     share = 0.5 * live_ref[...]
     volume_pass(
-        mid_ref, turned, acc_ref, med_ref, products,
+        mid_ref, acc_ref, med_ref, products,
         lambda own, row: share * (own + state_ref[row]), lambda value: share * value,
     )
     shot_sums(products, store_gradient(live_ref, [near_ref, far_ref], first_ref))
 
 
-def second_faces_kernel(slots, links, live_ref, acc_in, mid_ref, turned, med_ref, codes_ref, acc_ref):
+def second_faces_kernel(slots, links, live_ref, acc_in, mid_ref, med_ref, codes_ref, acc_ref):
     weight = (0.25 * lift_weight) * live_ref[...]
-    local_pass(mid_ref, turned, acc_ref, med_ref, codes_ref, slots, weight)
-
-
-def second_ghosts_kernel(chosen, slots, links, place_ref, acc_in, med_ref, codes_ref, *rest):
-    ghosts, acc_ref = rest[: len(chosen)], rest[-1]
-    ups = link_ups(place_ref, links)
-    for n, ghost in zip(chosen, ghosts):
-        ghost_pass(acc_ref, med_ref, codes_ref, ghost, links[n][0], ups[n], slots, 0.25 * lift_weight)
-
-
-def other_sources_kernel(slots, links, place_ref, acc_in, mid_ref, med_ref, codes_ref, *rest):
+    local_pass(mid_ref, acc_ref, med_ref, codes_ref, slots, weight)
+
+
+def second_ghosts_kernel(slots, links, place_ref, acc_in, mid_ref, med_ref, codes_ref, *rest):
     ghosts, (acc_ref, outer) = rest[: len(links)], rest[len(links) :]
-    ups = link_ups(place_ref, links)
-    axes = [link[0] for link in links]
-    other_sources(mid_ref, acc_ref, med_ref, codes_ref, ghosts, ups, axes, outer, slots, 0.25 * lift_weight)
+    add_ghosts(links, place_ref, acc_ref, med_ref, codes_ref, ghosts, slots, 0.25 * lift_weight)
+    add_others(links, place_ref, mid_ref, acc_ref, med_ref, codes_ref, ghosts, outer, slots, 0.25 * lift_weight)
 
 
 def partial_kernel(slots, links, acc_in, a_ref, b_ref, near_ref, far_ref, acc_ref, first_ref, second_ref):
@@ -541,7 +544,9 @@
         for parity in range(2):
             pairs = [(d, d + stride) for d in range(devices - stride) if (d // stride) % 2 == parity]
             if pairs:
-                links.append((axis, stride, parity, pairs + [(b, a) for a, b in pairs]))
+                alone = set(range(devices)) - {d for pair in pairs for d in pair}
+                route = pairs + [(b, a) for a, b in pairs] + [(d, d) for d in sorted(alone)]
+                links.append((axis, stride, parity, devices, route))
     return links
 
 
@@ -566,11 +571,11 @@
         return cut.transpose(3, 0, 1, 2, 4).reshape(shots, fields, nodes, slots)
 
     links = tree_links(lax.axis_size("dom"))
-    axes = tuple(link[:3] for link in links)
+    axes = tuple(link[:4] for link in links)
     place = lax.axis_index("dom").astype(jnp.int32).reshape(1)
 
     def exchange(sends, line):
-        routes = [link[3] for link in links if link[0] == line]
+        routes = [link[4] for link in links if link[0] == line]
         return [lax.ppermute(send, "dom", route) for send, route in zip(sends, routes)]
 
     vmem = pl.BlockSpec(memory_space=pltpu.VMEM)
@@ -617,15 +622,15 @@
         )
         ghosts += exchange(sends, line)
     acc, grad_first, live = call(
-        first_kernel, [state_shape, grad_shape, pltpu.VMEM((SUBS, LANES), f32)], [vmem] + [vmem] * 3, "first_section", 8, [products, pltpu.VMEM((rows, SUBS, LANES), f32)]
+        first_kernel, [state_shape, grad_shape, pltpu.VMEM((SUBS, LANES), f32)], [vmem] + [vmem] * 3, "first_section", 8, [products]
     )(counts, state, med, neighbours)
     (mid,) = call(
         middle_kernel, [state_shape], [smem] + [vmem] * (4 + count), "first_ghosts", 4, [outer], aliases={1: 0}
     )(place, acc, state, med, neighbours, *ghosts)
     cut = (nodes // 2 + SUBS // 2) // SUBS * SUBS
     part_shapes = [pltpu.VMEM((3, size, slots), f32) for size in (cut, nodes - cut)]
-    acc, turned, *halved = call(
-        second_volume_kernel, [state_shape] * 2 + part_shapes, [vmem] + [vmem] * 4, "second_volume", 0, [products]
+    acc, *halved = call(
+        second_volume_kernel, [state_shape] + part_shapes, [vmem] + [vmem] * 4, "second_volume", 0, [products]
     )(live, mid, state, med, grad_first)
     sends = call(late_pack_kernel, [send_shape] * count, [smem] + [vmem] * 3, "pack", 0.5)(
         place, mid, send_list, halved[0]
@@ -635,15 +640,8 @@
     if doubling:
         pieces = [swapped(halved[0], "shot", 1), swapped(halved[1], "shot", 2)]
     (acc,) = call(
-        second_faces_kernel, [state_shape], [vmem] * 6, "second_faces", 0.5, aliases={1: 0}
-    )(live, acc, mid, turned, med, neighbours)
-
-    def add_ghosts(acc, chosen, micros):
-        (acc,) = call(
-            functools.partial(second_ghosts_kernel, chosen), [state_shape], [smem] + [vmem] * (3 + len(chosen)),
-            "second_ghosts", micros, aliases={1: 0},
-        )(place, acc, med, neighbours, *[ghosts[n] for n in chosen])
-        return acc
+        second_faces_kernel, [state_shape], [vmem] * 5, "second_faces", 0.5, aliases={1: 0}
+    )(live, acc, mid, med, neighbours)
 
     if doubling:
         acc, *parts = call(
@@ -652,9 +650,8 @@
         pieces = [swapped(parts[0], "shot", 2), swapped(parts[1], "shot", 1)]
     else:
         gradient = lax.psum(jnp.concatenate(halved, axis=1), "shot")
-    acc = add_ghosts(acc, range(count), 1)
     (acc,) = call(
-        other_sources_kernel, [state_shape], [smem] + [vmem] * (4 + count), "other_sources", 0, [outer], aliases={1: 0}
+        second_ghosts_kernel, [state_shape], [smem] + [vmem] * (4 + count), "second_ghosts", 1, [outer], aliases={1: 0}
     )(place, acc, mid, med, neighbours, *ghosts)
     fwd, adj = call(store_kernel, [part_shape, part_shape], [vmem], "store", 4, [field_sems], [hbm, hbm])(
         acc.reshape(apart)

time: 44 us -> 43.3 us (0.984)
  Pallas kernels: 25.8 us -> 24.7 us
    pallas_call x4 -> x3, Pallas kernels: 9.22 us -> 8.6 us  [the longest x1 3.59 us: shards(): call(second_volume_kernel, [state_shape] + part_shapes, [vmem] + [vmem] *...]
    ppermute x6, waiting for transfers between devices: 1.01 us -> 1.46 us  [exchange(): lax.ppermute(send, 'dom', route)]
  transfers between devices with their start and end apart: 10 -> 10, of which waited for: 2 -> 3; matrix products, arithmetic and copies ran while one was open for 0% -> 0% of each run, Pallas kernels for 37% -> 35%
where the time goes in v4:
time: 43.3 us; the launch traced here: 42.9 us
  Pallas kernels  24.7 us (57%)
  starting transfers between devices  15.1 us (35%)
  waiting for transfers between devices  1.67 us (4%)
  between operations  1.44 us (3%)
    ppermute x6, starting transfers between devices, exchange(): lax.ppermute(send, 'dom', route)  12 us
    pallas_call x1, Pallas kernels, shards(): call(first_kernel, [state_shape, grad_shape, pltpu.VMEM((SUBS, LANES), f3...  6.01 us
    pallas_call x1, Pallas kernels, shards(): call(second_volume_kernel, [state_shape] + part_shapes, [vmem] + [vmem] *...  3.59 us
    pallas_call x1, Pallas kernels, shards(): call(second_faces_kernel, [state_shape], [vmem] * 5, 'second_faces', 0.5,...  3.1 us
    ppermute x4, starting transfers between devices, swapped(): return lax.ppermute(block, axis, route)  3.06 us
    pallas_call x1, Pallas kernels, shards(): call(load_kernel, [pltpu.VMEM(apart, f32), med_shape], [hbm] * 3, 'load',...  2.98 us
    pallas_call x1, Pallas kernels, shards(): call(store_kernel, [part_shape, part_shape], [vmem], 'store', 4, [field_s...  2.29 us
    pallas_call x1, Pallas kernels, shards(): call(middle_kernel, [state_shape], [smem] + [vmem] * (4 + count), 'first_...  1.91 us
  transfers between devices with their start and end apart: 10, of which 3 were waited for; matrix products, arithmetic and copies ran while one was open for 0% of the time, Pallas kernels for 35%

profile of v4, /device:TPU:1, one launch (start us, length us, event | category | flops | bytes accessed | tf_op | source)
XLA Modules:
  0.0 42.9 jit_solution(6176747748559060479)
XLA Ops:
  0.6 0.0 copy-start.1
  0.6 3.0 %load.1 = (f32[1125,2,2,2,128]{4,3,2,1,0:T(2,128)S(1)}, f32[500,8,128]{2,1,0:T(8,128)S(1)}) custom-call(f32[3,125,256]{2,1,0:T(8,128)} %mat_hbm.1, f32[1125,2,2,128]{3,2,1,0:T(2,128)} %bitcast.29, f32[1125,2,2,128]{3,2,1,0:T(2,128)} %bitcast.30), custom_call_target="tpu_custom_call" | custom-call | flops 4000000000 | tf_op jit(solution)/shard_map/load/pallas_call | solution.py:609
  3.6 0.0 copy-done.1
  3.6 0.0 copy-start
  3.7 0.4 pack.3
  4.1 3.2 %collective-permute-start = (f32[29,8,128]{2,1,0:T(8,128)S(1)}, f32[29,8,128]{2,1,0:T(8,128)S(1)}, u32[]{:S(2)}, u32[]{:S(2)}) collective-permute-start(f32[29,8,128]{2,1,0:T(8,128)S(1)} %pack.3), channel_id=1, source_target_pairs={{0,4},{1,5},{2,6},{3,7},{4,0},{5,1},{6,2},{7,3},{8,12},{9,13},{10,... | collective-permute-start | bytes 356360 | tf_op jit(solution)/shard_map/ppermute | solution.py:579
  7.3 0.7 %pack.4 = (f32[29,8,128]{2,1,0:T(8,128)S(1)}, f32[29,8,128]{2,1,0:T(8,128)S(1)}) custom-call(s32[1]{0:T(128)} %bitcast.place_ref, f32[1125,8,128]{2,1,0:T(8,128)S(1)} %bitcast.24, s32[1,4,32]{2,1,0:T(4,128)S(1)} %copy-done.1), custom_call_target="tpu_custom_call" | custom-call | tf_op jit(solution)/shard_map/pack/pallas_call | solution.py:620
  8.0 1.0 %collective-permute-start.1 = (f32[29,8,128]{2,1,0:T(8,128)S(1)}, f32[29,8,128]{2,1,0:T(8,128)S(1)}, u32[]{:S(2)}, u32[]{:S(2)}) collective-permute-start(f32[29,8,128]{2,1,0:T(8,128)S(1)} %get-tuple-element.25), channel_id=1, source_target_pairs={{0,1},{2,3},{4,5},{6,7},{1,0},{3,2},{5,4},{7,6},{8,9},{10,11},{12,... | collective-permute-start | bytes 356360 | tf_op jit(solution)/shard_map/ppermute | solution.py:579
  9.0 3.1 %collective-permute-start.2 = (f32[29,8,128]{2,1,0:T(8,128)S(1)}, f32[29,8,128]{2,1,0:T(8,128)S(1)}, u32[]{:S(2)}, u32[]{:S(2)}) collective-permute-start(f32[29,8,128]{2,1,0:T(8,128)S(1)} %get-tuple-element.26), channel_id=1, source_target_pairs={{1,2},{3,4},{5,6},{2,1},{4,3},{6,5},{0,0},{7,7},{9,10},{11,12},{13... | collective-permute-start | bytes 356360 | tf_op jit(solution)/shard_map/ppermute | solution.py:579
  12.7 0.0 copy-done
  12.7 6.0 %first_section.1 = (f32[1125,8,128]{2,1,0:T(8,128)S(1)}, f32[3,125,256]{2,1,0:T(8,128)S(1)}, f32[8,128]{1,0:T(8,128)S(1)}) custom-call(s32[1]{0:T(128)S(6)} %copy.21.counts_ref, f32[1125,8,128]{2,1,0:T(8,128)S(1)} %bitcast.25, f32[500,8,128]{2,1,0:T(8,128)S(1)} %get-tuple-element.22.med_ref, s32[1,1536]{1,0:T(1,128)S(1)} %copy-done), custom_call_target="tpu_custom_call" | custom-call | flops 8000000000 | tf_op jit(solution)/shard_map/first_section/pallas_call | solution.py:624
  18.8 0.0 collective-permute-done.rest_0_
  18.8 0.0 collective-permute-done.1.rest_1_
  18.8 0.0 collective-permute-done.2.rest_2_
  18.8 1.9 %first_ghosts.1.mid_ref.state_ref = f32[1125,8,128]{2,1,0:T(8,128)S(1)} custom-call(s32[1]{0:T(128)} %bitcast.place_ref, f32[1125,8,128]{2,1,0:T(8,128)S(1)} %get-tuple-element.24.acc_in, f32[1125,8,128]{2,1,0:T(8,128)S(1)} %bitcast.26, f32[500,8,128]{2,1,0:T(8,128)S(1)} %get-tuple-element.22.med_ref, ...), custom_call_target="tpu_custom_call", output_to_operand_aliasing={{}: (1, {})} | custom-call | flops 4000000000 | tf_op jit(solution)/shard_map/first_ghosts/pallas_call | solution.py:627
  20.7 3.6 %second_volume.1 = (f32[1125,8,128]{2,1,0:T(8,128)S(1)}, f32[3,64,256]{2,1,0:T(8,128)S(1)}, f32[3,61,256]{2,1,0:T(8,128)S(1)}) custom-call(f32[8,128]{1,0:T(8,128)S(1)} %get-tuple-element.23.live_ref, f32[1125,8,128]{2,1,0:T(8,128)S(1)} %first_ghosts.1.mid_ref.state_ref, f32[1125,8,128]{2,1,0:T(8,128)S(1)} %bitcast.27, ...), custom_call_target="tpu_custom_call" | custom-call | tf_op jit(solution)/shard_map/second_volume/pallas_call | solution.py:632
  24.3 1.3 %collective-permute-start.3 = (f32[3,64,256]{2,1,0:T(8,128)S(1)}, f32[3,64,256]{2,1,0:T(8,128)S(1)}, u32[]{:S(2)}, u32[]{:S(2)}) collective-permute-start(f32[3,64,256]{2,1,0:T(8,128)S(1)} %get-tuple-element.29.a_ref.grad_ref), channel_id=1, source_target_pairs={{0,8},{8,0},{16,24},{24,16},{1,9},{9,1},{17,25},{25,17},{2,10},{10... | collective-permute-start | bytes 589832 | tf_op jit(solution)/shard_map/ppermute | solution.py:555
  25.6 1.2 %collective-permute-start.4 = (f32[3,61,256]{2,1,0:T(8,128)S(1)}, f32[3,61,256]{2,1,0:T(8,128)S(1)}, u32[]{:S(2)}, u32[]{:S(2)}) collective-permute-start(f32[3,61,256]{2,1,0:T(8,128)S(1)} %get-tuple-element.30.b_ref), channel_id=1, source_target_pairs={{0,16},{8,24},{16,0},{24,8},{1,17},{9,25},{17,1},{25,9},{2,18},{10... | collective-permute-start | bytes 562184 | tf_op jit(solution)/shard_map/ppermute | solution.py:555
  26.8 1.0 %pack.5 = (f32[29,8,128]{2,1,0:T(8,128)S(1)}, f32[29,8,128]{2,1,0:T(8,128)S(1)}, f32[29,8,128]{2,1,0:T(8,128)S(1)}) custom-call(s32[1]{0:T(128)} %bitcast.place_ref, f32[1125,8,128]{2,1,0:T(8,128)S(1)} %first_ghosts.1.mid_ref.state_ref, s32[1,4,32]{2,1,0:T(4,128)S(1)} %copy-done.1, f32[3,64,256]{2,1,0:T(8,128)S(1)} %get-tuple-element.29.a_ref.grad_ref), custom_call_target="tpu_custom_call" | custom-call | flops 500000000 | tf_op jit(solution)/shard_map/pack/pallas_call | solution.py:635
  27.8 0.1 collective-permute-start.5
  28.0 2.5 %collective-permute-start.6 = (f32[29,8,128]{2,1,0:T(8,128)S(1)}, f32[29,8,128]{2,1,0:T(8,128)S(1)}, u32[]{:S(2)}, u32[]{:S(2)}) collective-permute-start(f32[29,8,128]{2,1,0:T(8,128)S(1)} %get-tuple-element.33), channel_id=1, source_target_pairs={{0,1},{2,3},{4,5},{6,7},{1,0},{3,2},{5,4},{7,6},{8,9},{10,11},{12,... | collective-permute-start | bytes 356360 | tf_op jit(solution)/shard_map/ppermute | solution.py:579
  30.4 2.1 %collective-permute-start.7 = (f32[29,8,128]{2,1,0:T(8,128)S(1)}, f32[29,8,128]{2,1,0:T(8,128)S(1)}, u32[]{:S(2)}, u32[]{:S(2)}) collective-permute-start(f32[29,8,128]{2,1,0:T(8,128)S(1)} %get-tuple-element.34), channel_id=1, source_target_pairs={{1,2},{3,4},{5,6},{2,1},{4,3},{6,5},{0,0},{7,7},{9,10},{11,12},{13... | collective-permute-start | bytes 356360 | tf_op jit(solution)/shard_map/ppermute | solution.py:579
  32.5 3.1 %second_faces.1.acc_in = f32[1125,8,128]{2,1,0:T(8,128)S(1)} custom-call(f32[8,128]{1,0:T(8,128)S(1)} %get-tuple-element.23.live_ref, f32[1125,8,128]{2,1,0:T(8,128)S(1)} %get-tuple-element.28.acc_in, f32[1125,8,128]{2,1,0:T(8,128)S(1)} %first_ghosts.1.mid_ref.state_ref, ...), custom_call_target="tpu_custom_call", output_to_operand_aliasing={{}: (1, {})} | custom-call | flops 500000000 | tf_op jit(solution)/shard_map/second_faces/pallas_call | solution.py:642
  35.6 0.0 collective-permute-done.4.far_ref
  35.6 0.0 collective-permute-done.3.near_ref
  35.7 0.3 collective-permute-start.8
  36.0 0.3 collective-permute-start.9
  36.2 0.2 collective-permute-done.5.rest_0_
  36.4 0.0 collective-permute-done.6.rest_1_
  36.4 1.3 %collective-permute-done.7.rest_2_ = f32[29,8,128]{2,1,0:T(8,128)S(1)} collective-permute-done((f32[29,8,128]{2,1,0:T(8,128)S(1)}, f32[29,8,128]{2,1,0:T(8,128)S(1)}, u32[]{:S(2)}, u32[]{:S(2)}) %collective-permute-start.7) | collective-permute-done | bytes 118816 | tf_op jit(solution)/shard_map/ppermute | solution.py:579
  37.7 1.9 %second_ghosts.1 = f32[1125,8,128]{2,1,0:T(8,128)S(1)} custom-call(s32[1]{0:T(128)} %bitcast.place_ref, f32[1125,8,128]{2,1,0:T(8,128)S(1)} %get-tuple-element.31.acc_in, f32[1125,8,128]{2,1,0:T(8,128)S(1)} %first_ghosts.1.mid_ref.state_ref, f32[500,8,128]{2,1,0:T(8,128)S(1)} %get-tuple-element.22.med_ref, ...), custom_call_target="tpu_custom_call", output_to_operand_aliasing={{}: (1, {})} | custom-call | flops 1000000000 | tf_op jit(solution)/shard_map/second_ghosts/pallas_call | solution.py:653
  39.6 2.3 %store.1 = (f32[1125,2,2,128]{3,2,1,0:T(2,128)}, f32[1125,2,2,128]{3,2,1,0:T(2,128)}) custom-call(f32[1125,2,2,2,128]{4,3,2,1,0:T(2,128)S(1)} %bitcast.28), custom_call_target="tpu_custom_call" | custom-call | flops 4000000000 | tf_op jit(solution)/shard_map/store/pallas_call | solution.py:656
  41.9 0.2 collective-permute-done.9.d_ref
  42.1 0.0 collective-permute-done.8.c_ref
  42.1 0.8 %gradient_total.1 = f32[3,125,256]{2,1,0:T(8,128)} custom-call(f32[3,64,256]{2,1,0:T(8,128)S(1)} %get-tuple-element.37.a_ref, f32[3,61,256]{2,1,0:T(8,128)S(1)} %get-tuple-element.38.b_ref, f32[3,64,256]{2,1,0:T(8,128)S(1)} %collective-permute-done.8.c_ref, f32[3,61,256]{2,1,0:T(8,128)S(1)} %collective-permute-done.9.d_ref), custom_call_target="tpu_custom_call" | custom-call | tf_op jit(solution)/shard_map/gradient_total/pallas_call | solution.py:660
  (1 shorter events, 0.0 us)
Async XLA Ops:
  0.6 3.0 %copy-start.1 = (s32[1,4,32]{2,1,0:T(4,128)S(1)}, s32[1,4,32]{2,1,0:T(4,128)}, u32[]{:S(2)}) copy-start(s32[1,4,32]{2,1,0:T(4,128)} %list_ref.5) | copy-start | bytes 1540
  3.6 9.1 %copy-start = (s32[1,1536]{1,0:T(1,128)S(1)}, s32[1,1536]{1,0:T(1,128)}, u32[]{:S(2)}) copy-start(s32[1,1536]{1,0:T(1,128)} %codes_ref.7) | copy-start | bytes 18436
  4.1 14.7 %collective-permute-start = (f32[29,8,128]{2,1,0:T(8,128)S(1)}, f32[29,8,128]{2,1,0:T(8,128)S(1)}, u32[]{:S(2)}, u32[]{:S(2)}) collective-permute-start(f32[29,8,128]{2,1,0:T(8,128)S(1)} %pack.3), channel_id=1, source_target_pairs={{0,4},{1,5},{2,6},{3,7},{4,0},{5,1},{6,2},{7,3},{8,12},{9,13},{10,... | collective-permute-start | bytes 356360 | tf_op jit(solution)/shard_map/ppermute | solution.py:579
  8.0 10.8 %collective-permute-start.1 = (f32[29,8,128]{2,1,0:T(8,128)S(1)}, f32[29,8,128]{2,1,0:T(8,128)S(1)}, u32[]{:S(2)}, u32[]{:S(2)}) collective-permute-start(f32[29,8,128]{2,1,0:T(8,128)S(1)} %get-tuple-element.25), channel_id=1, source_target_pairs={{0,1},{2,3},{4,5},{6,7},{1,0},{3,2},{5,4},{7,6},{8,9},{10,11},{12,... | collective-permute-start | bytes 356360 | tf_op jit(solution)/shard_map/ppermute | solution.py:579
  9.0 9.8 %collective-permute-start.2 = (f32[29,8,128]{2,1,0:T(8,128)S(1)}, f32[29,8,128]{2,1,0:T(8,128)S(1)}, u32[]{:S(2)}, u32[]{:S(2)}) collective-permute-start(f32[29,8,128]{2,1,0:T(8,128)S(1)} %get-tuple-element.26), channel_id=1, source_target_pairs={{1,2},{3,4},{5,6},{2,1},{4,3},{6,5},{0,0},{7,7},{9,10},{11,12},{13... | collective-permute-start | bytes 356360 | tf_op jit(solution)/shard_map/ppermute | solution.py:579
  24.3 11.3 %collective-permute-start.3 = (f32[3,64,256]{2,1,0:T(8,128)S(1)}, f32[3,64,256]{2,1,0:T(8,128)S(1)}, u32[]{:S(2)}, u32[]{:S(2)}) collective-permute-start(f32[3,64,256]{2,1,0:T(8,128)S(1)} %get-tuple-element.29.a_ref.grad_ref), channel_id=1, source_target_pairs={{0,8},{8,0},{16,24},{24,16},{1,9},{9,1},{17,25},{25,17},{2,10},{10... | collective-permute-start | bytes 589832 | tf_op jit(solution)/shard_map/ppermute | solution.py:555
  25.6 10.0 %collective-permute-start.4 = (f32[3,61,256]{2,1,0:T(8,128)S(1)}, f32[3,61,256]{2,1,0:T(8,128)S(1)}, u32[]{:S(2)}, u32[]{:S(2)}) collective-permute-start(f32[3,61,256]{2,1,0:T(8,128)S(1)} %get-tuple-element.30.b_ref), channel_id=1, source_target_pairs={{0,16},{8,24},{16,0},{24,8},{1,17},{9,25},{17,1},{25,9},{2,18},{10... | collective-permute-start | bytes 562184 | tf_op jit(solution)/shard_map/ppermute | solution.py:555
  27.8 8.6 %collective-permute-start.5 = (f32[29,8,128]{2,1,0:T(8,128)S(1)}, f32[29,8,128]{2,1,0:T(8,128)S(1)}, u32[]{:S(2)}, u32[]{:S(2)}) collective-permute-start(f32[29,8,128]{2,1,0:T(8,128)S(1)} %get-tuple-element.32), channel_id=1, source_target_pairs={{0,4},{1,5},{2,6},{3,7},{4,0},{5,1},{6,2},{7,3},{8,12},{9,13},{10,... | collective-permute-start | bytes 356360 | tf_op jit(solution)/shard_map/ppermute | solution.py:579
  28.0 8.5 %collective-permute-start.6 = (f32[29,8,128]{2,1,0:T(8,128)S(1)}, f32[29,8,128]{2,1,0:T(8,128)S(1)}, u32[]{:S(2)}, u32[]{:S(2)}) collective-permute-start(f32[29,8,128]{2,1,0:T(8,128)S(1)} %get-tuple-element.33), channel_id=1, source_target_pairs={{0,1},{2,3},{4,5},{6,7},{1,0},{3,2},{5,4},{7,6},{8,9},{10,11},{12,... | collective-permute-start | bytes 356360 | tf_op jit(solution)/shard_map/ppermute | solution.py:579
  30.4 7.3 %collective-permute-start.7 = (f32[29,8,128]{2,1,0:T(8,128)S(1)}, f32[29,8,128]{2,1,0:T(8,128)S(1)}, u32[]{:S(2)}, u32[]{:S(2)}) collective-permute-start(f32[29,8,128]{2,1,0:T(8,128)S(1)} %get-tuple-element.34), channel_id=1, source_target_pairs={{1,2},{3,4},{5,6},{2,1},{4,3},{6,5},{0,0},{7,7},{9,10},{11,12},{13... | collective-permute-start | bytes 356360 | tf_op jit(solution)/shard_map/ppermute | solution.py:579
  35.7 6.4 %collective-permute-start.8 = (f32[3,64,256]{2,1,0:T(8,128)S(1)}, f32[3,64,256]{2,1,0:T(8,128)S(1)}, u32[]{:S(2)}, u32[]{:S(2)}) collective-permute-start(f32[3,64,256]{2,1,0:T(8,128)S(1)} %get-tuple-element.37.a_ref), channel_id=1, source_target_pairs={{0,16},{8,24},{16,0},{24,8},{1,17},{9,25},{17,1},{25,9},{2,18},{10... | collective-permute-start | bytes 589832 | tf_op jit(solution)/shard_map/ppermute | solution.py:555
  36.0 6.1 %collective-permute-start.9 = (f32[3,61,256]{2,1,0:T(8,128)S(1)}, f32[3,61,256]{2,1,0:T(8,128)S(1)}, u32[]{:S(2)}, u32[]{:S(2)}) collective-permute-start(f32[3,61,256]{2,1,0:T(8,128)S(1)} %get-tuple-element.38.b_ref), channel_id=1, source_target_pairs={{0,8},{8,0},{16,24},{24,16},{1,9},{9,1},{17,25},{25,17},{2,10},{10... | collective-permute-start | bytes 562184 | tf_op jit(solution)/shard_map/ppermute | solution.py:555

commit v5 on v4

--- a/solution.py
+++ b/solution.py
@@ -639,10 +639,6 @@
     doubling = lax.axis_size("shot") == 4
     if doubling:
         pieces = [swapped(halved[0], "shot", 1), swapped(halved[1], "shot", 2)]
-    (acc,) = call(
-        second_faces_kernel, [state_shape], [vmem] * 5, "second_faces", 0.5, aliases={1: 0}
-    )(live, acc, mid, med, neighbours)
-
     if doubling:
         acc, *parts = call(
             partial_kernel, [state_shape] + part_shapes, [vmem] * 5, "gradient_partial", 0, aliases={0: 0}
@@ -650,6 +646,10 @@
         pieces = [swapped(parts[0], "shot", 2), swapped(parts[1], "shot", 1)]
     else:
         gradient = lax.psum(jnp.concatenate(halved, axis=1), "shot")
+    (acc,) = call(
+        second_faces_kernel, [state_shape], [vmem] * 5, "second_faces", 0.5, aliases={1: 0}
+    )(live, acc, mid, med, neighbours)
+
     (acc,) = call(
         second_ghosts_kernel, [state_shape], [smem] + [vmem] * (4 + count), "second_ghosts", 1, [outer], aliases={1: 0}
     )(place, acc, mid, med, neighbours, *ghosts)

time: 43.3 us -> 42.9 us (level)
  transfers between devices with their start and end apart: 10 -> 10, of which waited for: 3 -> 2; matrix products, arithmetic and copies ran while one was open for 0% -> 0% of each run, Pallas kernels for 35% -> 35%
where the time goes in v5:
time: 42.9 us; the launch traced here: 42.7 us
  Pallas kernels  24.7 us (58%)
  starting transfers between devices  15.1 us (35%)
  waiting for transfers between devices  1.47 us (3%)
  between operations  1.45 us (3%)
    ppermute x6, starting transfers between devices, exchange(): lax.ppermute(send, 'dom', route)  12 us
    pallas_call x1, Pallas kernels, shards(): call(first_kernel, [state_shape, grad_shape, pltpu.VMEM((SUBS, LANES), f3...  6.01 us
    pallas_call x1, Pallas kernels, shards(): call(second_volume_kernel, [state_shape] + part_shapes, [vmem] + [vmem] *...  3.59 us
    pallas_call x1, Pallas kernels, shards(): call(second_faces_kernel, [state_shape], [vmem] * 5, 'second_faces', 0.5,...  3.1 us
    ppermute x4, starting transfers between devices, swapped(): return lax.ppermute(block, axis, route)  3.06 us
    pallas_call x1, Pallas kernels, shards(): call(load_kernel, [pltpu.VMEM(apart, f32), med_shape], [hbm] * 3, 'load',...  2.98 us
    pallas_call x1, Pallas kernels, shards(): call(store_kernel, [part_shape, part_shape], [vmem], 'store', 4, [field_s...  2.29 us
    pallas_call x1, Pallas kernels, shards(): call(second_ghosts_kernel, [state_shape], [smem] + [vmem] * (4 + count),...  1.91 us
  transfers between devices with their start and end apart: 10, of which 2 were waited for; matrix products, arithmetic and copies ran while one was open for 0% of the time, Pallas kernels for 35%

profile of v5, /device:TPU:1, one launch (start us, length us, event | category | flops | bytes accessed | tf_op | source)
XLA Modules:
  0.0 42.7 jit_solution(17753748936854399333)
XLA Ops:
  0.6 0.0 copy-start.1
  0.6 3.0 %load.1 = (f32[1125,2,2,2,128]{4,3,2,1,0:T(2,128)S(1)}, f32[500,8,128]{2,1,0:T(8,128)S(1)}) custom-call(f32[3,125,256]{2,1,0:T(8,128)} %mat_hbm.1, f32[1125,2,2,128]{3,2,1,0:T(2,128)} %bitcast.29, f32[1125,2,2,128]{3,2,1,0:T(2,128)} %bitcast.30), custom_call_target="tpu_custom_call" | custom-call | flops 4000000000 | tf_op jit(solution)/shard_map/load/pallas_call | solution.py:609
  3.6 0.0 copy-done.1
  3.6 0.0 copy-start
  3.7 0.4 pack.3
  4.1 3.2 %collective-permute-start = (f32[29,8,128]{2,1,0:T(8,128)S(1)}, f32[29,8,128]{2,1,0:T(8,128)S(1)}, u32[]{:S(2)}, u32[]{:S(2)}) collective-permute-start(f32[29,8,128]{2,1,0:T(8,128)S(1)} %pack.3), channel_id=1, source_target_pairs={{0,4},{1,5},{2,6},{3,7},{4,0},{5,1},{6,2},{7,3},{8,12},{9,13},{10,... | collective-permute-start | bytes 356360 | tf_op jit(solution)/shard_map/ppermute | solution.py:579
  7.3 0.7 %pack.4 = (f32[29,8,128]{2,1,0:T(8,128)S(1)}, f32[29,8,128]{2,1,0:T(8,128)S(1)}) custom-call(s32[1]{0:T(128)} %bitcast.place_ref, f32[1125,8,128]{2,1,0:T(8,128)S(1)} %bitcast.24, s32[1,4,32]{2,1,0:T(4,128)S(1)} %copy-done.1), custom_call_target="tpu_custom_call" | custom-call | tf_op jit(solution)/shard_map/pack/pallas_call | solution.py:620
  8.0 1.0 %collective-permute-start.1 = (f32[29,8,128]{2,1,0:T(8,128)S(1)}, f32[29,8,128]{2,1,0:T(8,128)S(1)}, u32[]{:S(2)}, u32[]{:S(2)}) collective-permute-start(f32[29,8,128]{2,1,0:T(8,128)S(1)} %get-tuple-element.25), channel_id=1, source_target_pairs={{0,1},{2,3},{4,5},{6,7},{1,0},{3,2},{5,4},{7,6},{8,9},{10,11},{12,... | collective-permute-start | bytes 356360 | tf_op jit(solution)/shard_map/ppermute | solution.py:579
  9.0 3.1 %collective-permute-start.2 = (f32[29,8,128]{2,1,0:T(8,128)S(1)}, f32[29,8,128]{2,1,0:T(8,128)S(1)}, u32[]{:S(2)}, u32[]{:S(2)}) collective-permute-start(f32[29,8,128]{2,1,0:T(8,128)S(1)} %get-tuple-element.26), channel_id=1, source_target_pairs={{1,2},{3,4},{5,6},{2,1},{4,3},{6,5},{0,0},{7,7},{9,10},{11,12},{13... | collective-permute-start | bytes 356360 | tf_op jit(solution)/shard_map/ppermute | solution.py:579
  12.7 0.0 copy-done
  12.7 6.0 %first_section.1 = (f32[1125,8,128]{2,1,0:T(8,128)S(1)}, f32[3,125,256]{2,1,0:T(8,128)S(1)}, f32[8,128]{1,0:T(8,128)S(1)}) custom-call(s32[1]{0:T(128)S(6)} %copy.21.counts_ref, f32[1125,8,128]{2,1,0:T(8,128)S(1)} %bitcast.25, f32[500,8,128]{2,1,0:T(8,128)S(1)} %get-tuple-element.22.med_ref, s32[1,1536]{1,0:T(1,128)S(1)} %copy-done), custom_call_target="tpu_custom_call" | custom-call | flops 8000000000 | tf_op jit(solution)/shard_map/first_section/pallas_call | solution.py:624
  18.8 0.0 collective-permute-done.rest_0_
  18.8 0.0 collective-permute-done.1.rest_1_
  18.8 0.0 collective-permute-done.2.rest_2_
  18.8 1.9 %first_ghosts.1.mid_ref.state_ref = f32[1125,8,128]{2,1,0:T(8,128)S(1)} custom-call(s32[1]{0:T(128)} %bitcast.place_ref, f32[1125,8,128]{2,1,0:T(8,128)S(1)} %get-tuple-element.24.acc_in, f32[1125,8,128]{2,1,0:T(8,128)S(1)} %bitcast.26, f32[500,8,128]{2,1,0:T(8,128)S(1)} %get-tuple-element.22.med_ref, ...), custom_call_target="tpu_custom_call", output_to_operand_aliasing={{}: (1, {})} | custom-call | flops 4000000000 | tf_op jit(solution)/shard_map/first_ghosts/pallas_call | solution.py:627
  20.7 3.6 %second_volume.1 = (f32[1125,8,128]{2,1,0:T(8,128)S(1)}, f32[3,64,256]{2,1,0:T(8,128)S(1)}, f32[3,61,256]{2,1,0:T(8,128)S(1)}) custom-call(f32[8,128]{1,0:T(8,128)S(1)} %get-tuple-element.23.live_ref, f32[1125,8,128]{2,1,0:T(8,128)S(1)} %first_ghosts.1.mid_ref.state_ref, f32[1125,8,128]{2,1,0:T(8,128)S(1)} %bitcast.27, ...), custom_call_target="tpu_custom_call" | custom-call | tf_op jit(solution)/shard_map/second_volume/pallas_call | solution.py:632
  24.3 1.3 %collective-permute-start.3 = (f32[3,64,256]{2,1,0:T(8,128)S(1)}, f32[3,64,256]{2,1,0:T(8,128)S(1)}, u32[]{:S(2)}, u32[]{:S(2)}) collective-permute-start(f32[3,64,256]{2,1,0:T(8,128)S(1)} %get-tuple-element.29.a_ref.grad_ref), channel_id=1, source_target_pairs={{0,8},{8,0},{16,24},{24,16},{1,9},{9,1},{17,25},{25,17},{2,10},{10... | collective-permute-start | bytes 589832 | tf_op jit(solution)/shard_map/ppermute | solution.py:555
  25.6 1.2 %collective-permute-start.4 = (f32[3,61,256]{2,1,0:T(8,128)S(1)}, f32[3,61,256]{2,1,0:T(8,128)S(1)}, u32[]{:S(2)}, u32[]{:S(2)}) collective-permute-start(f32[3,61,256]{2,1,0:T(8,128)S(1)} %get-tuple-element.30.b_ref), channel_id=1, source_target_pairs={{0,16},{8,24},{16,0},{24,8},{1,17},{9,25},{17,1},{25,9},{2,18},{10... | collective-permute-start | bytes 562184 | tf_op jit(solution)/shard_map/ppermute | solution.py:555
  26.8 1.0 %pack.5 = (f32[29,8,128]{2,1,0:T(8,128)S(1)}, f32[29,8,128]{2,1,0:T(8,128)S(1)}, f32[29,8,128]{2,1,0:T(8,128)S(1)}) custom-call(s32[1]{0:T(128)} %bitcast.place_ref, f32[1125,8,128]{2,1,0:T(8,128)S(1)} %first_ghosts.1.mid_ref.state_ref, s32[1,4,32]{2,1,0:T(4,128)S(1)} %copy-done.1, f32[3,64,256]{2,1,0:T(8,128)S(1)} %get-tuple-element.29.a_ref.grad_ref), custom_call_target="tpu_custom_call" | custom-call | flops 500000000 | tf_op jit(solution)/shard_map/pack/pallas_call | solution.py:635
  27.8 0.1 collective-permute-start.5
  28.0 2.5 %collective-permute-start.6 = (f32[29,8,128]{2,1,0:T(8,128)S(1)}, f32[29,8,128]{2,1,0:T(8,128)S(1)}, u32[]{:S(2)}, u32[]{:S(2)}) collective-permute-start(f32[29,8,128]{2,1,0:T(8,128)S(1)} %get-tuple-element.33), channel_id=1, source_target_pairs={{0,1},{2,3},{4,5},{6,7},{1,0},{3,2},{5,4},{7,6},{8,9},{10,11},{12,... | collective-permute-start | bytes 356360 | tf_op jit(solution)/shard_map/ppermute | solution.py:579
  30.4 2.1 %collective-permute-start.7 = (f32[29,8,128]{2,1,0:T(8,128)S(1)}, f32[29,8,128]{2,1,0:T(8,128)S(1)}, u32[]{:S(2)}, u32[]{:S(2)}) collective-permute-start(f32[29,8,128]{2,1,0:T(8,128)S(1)} %get-tuple-element.34), channel_id=1, source_target_pairs={{1,2},{3,4},{5,6},{2,1},{4,3},{6,5},{0,0},{7,7},{9,10},{11,12},{13... | collective-permute-start | bytes 356360 | tf_op jit(solution)/shard_map/ppermute | solution.py:579
  32.5 0.0 collective-permute-done.4.far_ref
  32.5 0.0 collective-permute-done.3.near_ref
  32.6 0.3 collective-permute-start.8
  32.9 0.3 collective-permute-start.9
  33.1 3.1 %second_faces.1.acc_in = f32[1125,8,128]{2,1,0:T(8,128)S(1)} custom-call(f32[8,128]{1,0:T(8,128)S(1)} %get-tuple-element.23.live_ref, f32[1125,8,128]{2,1,0:T(8,128)S(1)} %get-tuple-element.31.acc_in, f32[1125,8,128]{2,1,0:T(8,128)S(1)} %first_ghosts.1.mid_ref.state_ref, ...), custom_call_target="tpu_custom_call", output_to_operand_aliasing={{}: (1, {})} | custom-call | flops 500000000 | tf_op jit(solution)/shard_map/second_faces/pallas_call | solution.py:649
  36.2 0.2 collective-permute-done.5.rest_0_
  36.4 0.0 collective-permute-done.6.rest_1_
  36.4 1.3 %collective-permute-done.7.rest_2_ = f32[29,8,128]{2,1,0:T(8,128)S(1)} collective-permute-done((f32[29,8,128]{2,1,0:T(8,128)S(1)}, f32[29,8,128]{2,1,0:T(8,128)S(1)}, u32[]{:S(2)}, u32[]{:S(2)}) %collective-permute-start.7) | collective-permute-done | bytes 118816 | tf_op jit(solution)/shard_map/ppermute | solution.py:579
  37.7 1.9 %second_ghosts.1 = f32[1125,8,128]{2,1,0:T(8,128)S(1)} custom-call(s32[1]{0:T(128)} %bitcast.place_ref, f32[1125,8,128]{2,1,0:T(8,128)S(1)} %second_faces.1.acc_in, f32[1125,8,128]{2,1,0:T(8,128)S(1)} %first_ghosts.1.mid_ref.state_ref, f32[500,8,128]{2,1,0:T(8,128)S(1)} %get-tuple-element.22.med_ref, ...), custom_call_target="tpu_custom_call", output_to_operand_aliasing={{}: (1, {})} | custom-call | flops 1000000000 | tf_op jit(solution)/shard_map/second_ghosts/pallas_call | solution.py:653
  39.6 2.3 %store.1 = (f32[1125,2,2,128]{3,2,1,0:T(2,128)}, f32[1125,2,2,128]{3,2,1,0:T(2,128)}) custom-call(f32[1125,2,2,2,128]{4,3,2,1,0:T(2,128)S(1)} %bitcast.28), custom_call_target="tpu_custom_call" | custom-call | flops 4000000000 | tf_op jit(solution)/shard_map/store/pallas_call | solution.py:656
  41.9 0.0 collective-permute-done.9.d_ref
  41.9 0.0 collective-permute-done.8.c_ref
  41.9 0.8 %gradient_total.1 = f32[3,125,256]{2,1,0:T(8,128)} custom-call(f32[3,64,256]{2,1,0:T(8,128)S(1)} %get-tuple-element.37.a_ref, f32[3,61,256]{2,1,0:T(8,128)S(1)} %get-tuple-element.38.b_ref, f32[3,64,256]{2,1,0:T(8,128)S(1)} %collective-permute-done.8.c_ref, f32[3,61,256]{2,1,0:T(8,128)S(1)} %collective-permute-done.9.d_ref), custom_call_target="tpu_custom_call" | custom-call | tf_op jit(solution)/shard_map/gradient_total/pallas_call | solution.py:660
  (1 shorter events, 0.0 us)
Async XLA Ops:
  0.6 3.0 %copy-start.1 = (s32[1,4,32]{2,1,0:T(4,128)S(1)}, s32[1,4,32]{2,1,0:T(4,128)}, u32[]{:S(2)}) copy-start(s32[1,4,32]{2,1,0:T(4,128)} %list_ref.5) | copy-start | bytes 1540
  3.6 9.1 %copy-start = (s32[1,1536]{1,0:T(1,128)S(1)}, s32[1,1536]{1,0:T(1,128)}, u32[]{:S(2)}) copy-start(s32[1,1536]{1,0:T(1,128)} %codes_ref.7) | copy-start | bytes 18436
  4.1 14.7 %collective-permute-start = (f32[29,8,128]{2,1,0:T(8,128)S(1)}, f32[29,8,128]{2,1,0:T(8,128)S(1)}, u32[]{:S(2)}, u32[]{:S(2)}) collective-permute-start(f32[29,8,128]{2,1,0:T(8,128)S(1)} %pack.3), channel_id=1, source_target_pairs={{0,4},{1,5},{2,6},{3,7},{4,0},{5,1},{6,2},{7,3},{8,12},{9,13},{10,... | collective-permute-start | bytes 356360 | tf_op jit(solution)/shard_map/ppermute | solution.py:579
  8.0 10.8 %collective-permute-start.1 = (f32[29,8,128]{2,1,0:T(8,128)S(1)}, f32[29,8,128]{2,1,0:T(8,128)S(1)}, u32[]{:S(2)}, u32[]{:S(2)}) collective-permute-start(f32[29,8,128]{2,1,0:T(8,128)S(1)} %get-tuple-element.25), channel_id=1, source_target_pairs={{0,1},{2,3},{4,5},{6,7},{1,0},{3,2},{5,4},{7,6},{8,9},{10,11},{12,... | collective-permute-start | bytes 356360 | tf_op jit(solution)/shard_map/ppermute | solution.py:579
  9.0 9.8 %collective-permute-start.2 = (f32[29,8,128]{2,1,0:T(8,128)S(1)}, f32[29,8,128]{2,1,0:T(8,128)S(1)}, u32[]{:S(2)}, u32[]{:S(2)}) collective-permute-start(f32[29,8,128]{2,1,0:T(8,128)S(1)} %get-tuple-element.26), channel_id=1, source_target_pairs={{1,2},{3,4},{5,6},{2,1},{4,3},{6,5},{0,0},{7,7},{9,10},{11,12},{13... | collective-permute-start | bytes 356360 | tf_op jit(solution)/shard_map/ppermute | solution.py:579
  24.3 8.2 %collective-permute-start.3 = (f32[3,64,256]{2,1,0:T(8,128)S(1)}, f32[3,64,256]{2,1,0:T(8,128)S(1)}, u32[]{:S(2)}, u32[]{:S(2)}) collective-permute-start(f32[3,64,256]{2,1,0:T(8,128)S(1)} %get-tuple-element.29.a_ref.grad_ref), channel_id=1, source_target_pairs={{0,8},{8,0},{16,24},{24,16},{1,9},{9,1},{17,25},{25,17},{2,10},{10... | collective-permute-start | bytes 589832 | tf_op jit(solution)/shard_map/ppermute | solution.py:555
  25.6 6.9 %collective-permute-start.4 = (f32[3,61,256]{2,1,0:T(8,128)S(1)}, f32[3,61,256]{2,1,0:T(8,128)S(1)}, u32[]{:S(2)}, u32[]{:S(2)}) collective-permute-start(f32[3,61,256]{2,1,0:T(8,128)S(1)} %get-tuple-element.30.b_ref), channel_id=1, source_target_pairs={{0,16},{8,24},{16,0},{24,8},{1,17},{9,25},{17,1},{25,9},{2,18},{10... | collective-permute-start | bytes 562184 | tf_op jit(solution)/shard_map/ppermute | solution.py:555
  27.8 8.6 %collective-permute-start.5 = (f32[29,8,128]{2,1,0:T(8,128)S(1)}, f32[29,8,128]{2,1,0:T(8,128)S(1)}, u32[]{:S(2)}, u32[]{:S(2)}) collective-permute-start(f32[29,8,128]{2,1,0:T(8,128)S(1)} %get-tuple-element.32), channel_id=1, source_target_pairs={{0,4},{1,5},{2,6},{3,7},{4,0},{5,1},{6,2},{7,3},{8,12},{9,13},{10,... | collective-permute-start | bytes 356360 | tf_op jit(solution)/shard_map/ppermute | solution.py:579
  28.0 8.5 %collective-permute-start.6 = (f32[29,8,128]{2,1,0:T(8,128)S(1)}, f32[29,8,128]{2,1,0:T(8,128)S(1)}, u32[]{:S(2)}, u32[]{:S(2)}) collective-permute-start(f32[29,8,128]{2,1,0:T(8,128)S(1)} %get-tuple-element.33), channel_id=1, source_target_pairs={{0,1},{2,3},{4,5},{6,7},{1,0},{3,2},{5,4},{7,6},{8,9},{10,11},{12,... | collective-permute-start | bytes 356360 | tf_op jit(solution)/shard_map/ppermute | solution.py:579
  30.4 7.3 %collective-permute-start.7 = (f32[29,8,128]{2,1,0:T(8,128)S(1)}, f32[29,8,128]{2,1,0:T(8,128)S(1)}, u32[]{:S(2)}, u32[]{:S(2)}) collective-permute-start(f32[29,8,128]{2,1,0:T(8,128)S(1)} %get-tuple-element.34), channel_id=1, source_target_pairs={{1,2},{3,4},{5,6},{2,1},{4,3},{6,5},{0,0},{7,7},{9,10},{11,12},{13... | collective-permute-start | bytes 356360 | tf_op jit(solution)/shard_map/ppermute | solution.py:579
  32.6 9.3 %collective-permute-start.8 = (f32[3,64,256]{2,1,0:T(8,128)S(1)}, f32[3,64,256]{2,1,0:T(8,128)S(1)}, u32[]{:S(2)}, u32[]{:S(2)}) collective-permute-start(f32[3,64,256]{2,1,0:T(8,128)S(1)} %get-tuple-element.37.a_ref), channel_id=1, source_target_pairs={{0,16},{8,24},{16,0},{24,8},{1,17},{9,25},{17,1},{25,9},{2,18},{10... | collective-permute-start | bytes 589832 | tf_op jit(solution)/shard_map/ppermute | solution.py:555
  32.9 9.0 %collective-permute-start.9 = (f32[3,61,256]{2,1,0:T(8,128)S(1)}, f32[3,61,256]{2,1,0:T(8,128)S(1)}, u32[]{:S(2)}, u32[]{:S(2)}) collective-permute-start(f32[3,61,256]{2,1,0:T(8,128)S(1)} %get-tuple-element.38.b_ref), channel_id=1, source_target_pairs={{0,8},{8,0},{16,24},{24,16},{1,9},{9,1},{17,25},{25,17},{2,10},{10... | collective-permute-start | bytes 562184 | tf_op jit(solution)/shard_map/ppermute | solution.py:555

commit v6 on v5

--- a/solution.py
+++ b/solution.py
@@ -160,7 +160,7 @@
                     acc[row * NODES + 25 * i + 5 * j + k] = out[i]
         return carry
 
-    lax.fori_loop(0, ORDER, x_lines, 0)
+    lax.fori_loop(0, ORDER, x_lines, 0, unroll=True)
 
     def y_lines(i, carry):
         for k in range(5):
@@ -171,7 +171,7 @@
                     acc[at] = acc[at] + out[j] if more else out[j]
         return carry
 
-    lax.fori_loop(0, ORDER, y_lines, 0)
+    lax.fori_loop(0, ORDER, y_lines, 0, unroll=True)
 
     def z_line(first):
         parts = {}
@@ -208,7 +208,7 @@
             z_line(25 * i + 5 * j)
         return carry
 
-    lax.fori_loop(0, ORDER, z_lines, 0)
+    lax.fori_loop(0, ORDER, z_lines, 0, unroll=True)
 
 
 def shot_sums(products, emit):
@@ -521,19 +521,30 @@
     second_ref[...] = b_ref[...] + far_ref[...]
 
 
-def total_kernel(slots, links, a_ref, b_ref, c_ref, d_ref, grad_ref):
-    cut = a_ref.shape[1]
-    grad_ref[:, :cut] = a_ref[...] + c_ref[...]
-    grad_ref[:, cut:] = b_ref[...] + d_ref[...]
-
-
-def store_kernel(slots, links, acc_ref, fwd_hbm, adj_hbm, sems):
+def store_copies(acc_ref, fwd_hbm, adj_hbm, sems):
     copies = []
     for k in range(FIELDS):
         span = pl.ds(k * NODES, NODES)
         for n, far in enumerate((fwd_hbm, adj_hbm)):
             copies.append(pltpu.make_async_copy(acc_ref.at[span, :, n], far.at[span], sems.at[n, k]))
             copies[-1].start()
+    return copies
+
+
+def store_kernel(slots, links, acc_ref, fwd_hbm, adj_hbm, sems):
+    for copy in store_copies(acc_ref, fwd_hbm, adj_hbm, sems):
+        copy.wait()
+
+
+def store_and_sum_kernel(
+    slots, links, acc_ref, a_ref, b_ref, c_ref, d_ref, fwd_hbm, adj_hbm, grad_hbm, sems, grad_ref, grad_sem
+):
+    copies = store_copies(acc_ref, fwd_hbm, adj_hbm, sems)
+    cut = a_ref.shape[1]
+    grad_ref[:, :cut] = a_ref[...] + c_ref[...]
+    grad_ref[:, cut:] = b_ref[...] + d_ref[...]
+    copies.append(pltpu.make_async_copy(grad_ref, grad_hbm, grad_sem))
+    copies[-1].start()
     for copy in copies:
         copy.wait()
 
@@ -653,13 +664,15 @@
     (acc,) = call(
         second_ghosts_kernel, [state_shape], [smem] + [vmem] * (4 + count), "second_ghosts", 1, [outer], aliases={1: 0}
     )(place, acc, mid, med, neighbours, *ghosts)
-    fwd, adj = call(store_kernel, [part_shape, part_shape], [vmem], "store", 4, [field_sems], [hbm, hbm])(
-        acc.reshape(apart)
-    )
     if doubling:
-        (gradient,) = call(
-            total_kernel, [jax.ShapeDtypeStruct(material.shape, f32)], [vmem] * 4, "gradient_total", 0
-        )(*parts, *pieces)
+        fwd, adj, gradient = call(
+            store_and_sum_kernel, [part_shape, part_shape, jax.ShapeDtypeStruct(material.shape, f32)], [vmem] * 5,
+            "store", 4, [field_sems, pltpu.VMEM(material.shape, f32), pltpu.SemaphoreType.DMA], [hbm] * 3,
+        )(acc.reshape(apart), *parts, *pieces)
+    else:
+        fwd, adj = call(store_kernel, [part_shape] * 2, [vmem], "store", 4, [field_sems], [hbm] * 2)(
+            acc.reshape(apart)
+        )
     return restored(fwd), restored(adj), gradient
 
 

time: 42.9 us -> 41.6 us (0.970)
  Pallas kernels: 24.7 us -> 23.3 us
    pallas_call x1, Pallas kernels: 6.01 us -> 5.08 us  [shards(): call(first_kernel, [state_shape, grad_shape, pltpu.VMEM((SUBS, LANES), f3...]
    pallas_call x2 -> x1, Pallas kernels: 3.08 us -> 2.43 us  [shards(): call(store_and_sum_kernel, [part_shape, part_shape, jax.ShapeDtypeStruct(...]
  transfers between devices with their start and end apart: 10 -> 10, of which waited for: 2 -> 2; matrix products, arithmetic and copies ran while one was open for 0% -> 0% of each run, Pallas kernels for 35% -> 29%
where the time goes in v6:
time: 41.6 us; the launch traced here: 41.5 us
  Pallas kernels  23.3 us (56%)
  starting transfers between devices  14.9 us (36%)
  waiting for transfers between devices  1.65 us (4%)
  between operations  1.61 us (4%)
    ppermute x6, starting transfers between devices, exchange(): lax.ppermute(send, 'dom', route)  11.8 us
    pallas_call x1, Pallas kernels, shards(): call(first_kernel, [state_shape, grad_shape, pltpu.VMEM((SUBS, LANES), f3...  5.08 us
    pallas_call x1, Pallas kernels, shards(): call(second_volume_kernel, [state_shape] + part_shapes, [vmem] + [vmem] *...  3.6 us
    pallas_call x1, Pallas kernels, shards(): call(second_faces_kernel, [state_shape], [vmem] * 5, 'second_faces', 0.5,...  3.1 us
    ppermute x4, starting transfers between devices, swapped(): return lax.ppermute(block, axis, route)  3.06 us
    pallas_call x1, Pallas kernels, shards(): call(load_kernel, [pltpu.VMEM(apart, f32), med_shape], [hbm] * 3, 'load',...  2.98 us
    pallas_call x1, Pallas kernels, shards(): call(store_and_sum_kernel, [part_shape, part_shape, jax.ShapeDtypeStruct(...  2.43 us
    pallas_call x1, Pallas kernels, shards(): call(middle_kernel, [state_shape], [smem] + [vmem] * (4 + count), 'first_...  2.08 us
  transfers between devices with their start and end apart: 10, of which 2 were waited for; matrix products, arithmetic and copies ran while one was open for 0% of the time, Pallas kernels for 29%

profile of v6, /device:TPU:1, one launch (start us, length us, event | category | flops | bytes accessed | tf_op | source)
XLA Modules:
  0.0 41.5 jit_solution(16743071208245098363)
XLA Ops:
  0.6 0.0 copy-start.1
  0.6 3.0 %load.1 = (f32[1125,2,2,2,128]{4,3,2,1,0:T(2,128)S(1)}, f32[500,8,128]{2,1,0:T(8,128)S(1)}) custom-call(f32[3,125,256]{2,1,0:T(8,128)} %mat_hbm.1, f32[1125,2,2,128]{3,2,1,0:T(2,128)} %bitcast.29, f32[1125,2,2,128]{3,2,1,0:T(2,128)} %bitcast.30), custom_call_target="tpu_custom_call" | custom-call | flops 4000000000 | tf_op jit(solution)/shard_map/load/pallas_call | solution.py:620
  3.6 0.0 copy-done.1
  3.6 0.0 copy-start
  3.7 0.4 pack.3
  4.0 3.2 %collective-permute-start = (f32[29,8,128]{2,1,0:T(8,128)S(1)}, f32[29,8,128]{2,1,0:T(8,128)S(1)}, u32[]{:S(2)}, u32[]{:S(2)}) collective-permute-start(f32[29,8,128]{2,1,0:T(8,128)S(1)} %pack.3), channel_id=1, source_target_pairs={{0,4},{1,5},{2,6},{3,7},{4,0},{5,1},{6,2},{7,3},{8,12},{9,13},{10,... | collective-permute-start | bytes 356360 | tf_op jit(solution)/shard_map/ppermute | solution.py:590
  7.3 0.7 %pack.4 = (f32[29,8,128]{2,1,0:T(8,128)S(1)}, f32[29,8,128]{2,1,0:T(8,128)S(1)}) custom-call(s32[1]{0:T(128)} %bitcast.place_ref, f32[1125,8,128]{2,1,0:T(8,128)S(1)} %bitcast.24, s32[1,4,32]{2,1,0:T(4,128)S(1)} %copy-done.1), custom_call_target="tpu_custom_call" | custom-call | tf_op jit(solution)/shard_map/pack/pallas_call | solution.py:631
  8.0 1.0 %collective-permute-start.1 = (f32[29,8,128]{2,1,0:T(8,128)S(1)}, f32[29,8,128]{2,1,0:T(8,128)S(1)}, u32[]{:S(2)}, u32[]{:S(2)}) collective-permute-start(f32[29,8,128]{2,1,0:T(8,128)S(1)} %get-tuple-element.26), channel_id=1, source_target_pairs={{0,1},{2,3},{4,5},{6,7},{1,0},{3,2},{5,4},{7,6},{8,9},{10,11},{12,... | collective-permute-start | bytes 356360 | tf_op jit(solution)/shard_map/ppermute | solution.py:590
  9.0 3.1 %collective-permute-start.2 = (f32[29,8,128]{2,1,0:T(8,128)S(1)}, f32[29,8,128]{2,1,0:T(8,128)S(1)}, u32[]{:S(2)}, u32[]{:S(2)}) collective-permute-start(f32[29,8,128]{2,1,0:T(8,128)S(1)} %get-tuple-element.27), channel_id=1, source_target_pairs={{1,2},{3,4},{5,6},{2,1},{4,3},{6,5},{0,0},{7,7},{9,10},{11,12},{13... | collective-permute-start | bytes 356360 | tf_op jit(solution)/shard_map/ppermute | solution.py:590
  12.7 0.0 copy-done
  12.7 5.1 %first_section.1 = (f32[1125,8,128]{2,1,0:T(8,128)S(1)}, f32[3,125,256]{2,1,0:T(8,128)S(1)}, f32[8,128]{1,0:T(8,128)S(1)}) custom-call(s32[1]{0:T(128)S(6)} %copy.21.counts_ref, f32[1125,8,128]{2,1,0:T(8,128)S(1)} %bitcast.25, f32[500,8,128]{2,1,0:T(8,128)S(1)} %get-tuple-element.23.med_ref, s32[1,1536]{1,0:T(1,128)S(1)} %copy-done), custom_call_target="tpu_custom_call" | custom-call | flops 8000000000 | tf_op jit(solution)/shard_map/first_section/pallas_call | solution.py:635
  17.8 0.0 collective-permute-done.rest_0_
  17.8 0.0 collective-permute-done.1.rest_1_
  17.9 0.0 collective-permute-done.2.rest_2_
  17.9 2.1 %first_ghosts.1.mid_ref.state_ref = f32[1125,8,128]{2,1,0:T(8,128)S(1)} custom-call(s32[1]{0:T(128)} %bitcast.place_ref, f32[1125,8,128]{2,1,0:T(8,128)S(1)} %get-tuple-element.25.acc_in, f32[1125,8,128]{2,1,0:T(8,128)S(1)} %bitcast.26, f32[500,8,128]{2,1,0:T(8,128)S(1)} %get-tuple-element.23.med_ref, ...), custom_call_target="tpu_custom_call", output_to_operand_aliasing={{}: (1, {})} | custom-call | flops 4000000000 | tf_op jit(solution)/shard_map/first_ghosts/pallas_call | solution.py:638
  19.9 3.6 %second_volume.1 = (f32[1125,8,128]{2,1,0:T(8,128)S(1)}, f32[3,64,256]{2,1,0:T(8,128)S(1)}, f32[3,61,256]{2,1,0:T(8,128)S(1)}) custom-call(f32[8,128]{1,0:T(8,128)S(1)} %get-tuple-element.24.live_ref, f32[1125,8,128]{2,1,0:T(8,128)S(1)} %first_ghosts.1.mid_ref.state_ref, f32[1125,8,128]{2,1,0:T(8,128)S(1)} %bitcast.27, ...), custom_call_target="tpu_custom_call" | custom-call | tf_op jit(solution)/shard_map/second_volume/pallas_call | solution.py:643
  23.6 1.3 %collective-permute-start.3 = (f32[3,64,256]{2,1,0:T(8,128)S(1)}, f32[3,64,256]{2,1,0:T(8,128)S(1)}, u32[]{:S(2)}, u32[]{:S(2)}) collective-permute-start(f32[3,64,256]{2,1,0:T(8,128)S(1)} %get-tuple-element.30.a_ref.grad_ref), channel_id=1, source_target_pairs={{0,8},{8,0},{16,24},{24,16},{1,9},{9,1},{17,25},{25,17},{2,10},{10... | collective-permute-start | bytes 589832 | tf_op jit(solution)/shard_map/ppermute | solution.py:566
  24.8 1.2 %collective-permute-start.4 = (f32[3,61,256]{2,1,0:T(8,128)S(1)}, f32[3,61,256]{2,1,0:T(8,128)S(1)}, u32[]{:S(2)}, u32[]{:S(2)}) collective-permute-start(f32[3,61,256]{2,1,0:T(8,128)S(1)} %get-tuple-element.31.b_ref), channel_id=1, source_target_pairs={{0,16},{8,24},{16,0},{24,8},{1,17},{9,25},{17,1},{25,9},{2,18},{10... | collective-permute-start | bytes 562184 | tf_op jit(solution)/shard_map/ppermute | solution.py:566
  26.1 1.0 %pack.5 = (f32[29,8,128]{2,1,0:T(8,128)S(1)}, f32[29,8,128]{2,1,0:T(8,128)S(1)}, f32[29,8,128]{2,1,0:T(8,128)S(1)}) custom-call(s32[1]{0:T(128)} %bitcast.place_ref, f32[1125,8,128]{2,1,0:T(8,128)S(1)} %first_ghosts.1.mid_ref.state_ref, s32[1,4,32]{2,1,0:T(4,128)S(1)} %copy-done.1, f32[3,64,256]{2,1,0:T(8,128)S(1)} %get-tuple-element.30.a_ref.grad_ref), custom_call_target="tpu_custom_call" | custom-call | flops 500000000 | tf_op jit(solution)/shard_map/pack/pallas_call | solution.py:646
  27.1 0.1 collective-permute-start.5
  27.2 2.5 %collective-permute-start.6 = (f32[29,8,128]{2,1,0:T(8,128)S(1)}, f32[29,8,128]{2,1,0:T(8,128)S(1)}, u32[]{:S(2)}, u32[]{:S(2)}) collective-permute-start(f32[29,8,128]{2,1,0:T(8,128)S(1)} %get-tuple-element.34), channel_id=1, source_target_pairs={{0,1},{2,3},{4,5},{6,7},{1,0},{3,2},{5,4},{7,6},{8,9},{10,11},{12,... | collective-permute-start | bytes 356360 | tf_op jit(solution)/shard_map/ppermute | solution.py:590
  29.7 1.9 %collective-permute-start.7 = (f32[29,8,128]{2,1,0:T(8,128)S(1)}, f32[29,8,128]{2,1,0:T(8,128)S(1)}, u32[]{:S(2)}, u32[]{:S(2)}) collective-permute-start(f32[29,8,128]{2,1,0:T(8,128)S(1)} %get-tuple-element.35), channel_id=1, source_target_pairs={{1,2},{3,4},{5,6},{2,1},{4,3},{6,5},{0,0},{7,7},{9,10},{11,12},{13... | collective-permute-start | bytes 356360 | tf_op jit(solution)/shard_map/ppermute | solution.py:590
  31.6 0.0 collective-permute-done.4.far_ref
  31.6 0.0 collective-permute-done.3.near_ref
  31.7 0.3 collective-permute-start.8
  32.0 0.3 collective-permute-start.9
  32.2 3.1 %second_faces.1.acc_in = f32[1125,8,128]{2,1,0:T(8,128)S(1)} custom-call(f32[8,128]{1,0:T(8,128)S(1)} %get-tuple-element.24.live_ref, f32[1125,8,128]{2,1,0:T(8,128)S(1)} %get-tuple-element.32.acc_in, f32[1125,8,128]{2,1,0:T(8,128)S(1)} %first_ghosts.1.mid_ref.state_ref, ...), custom_call_target="tpu_custom_call", output_to_operand_aliasing={{}: (1, {})} | custom-call | flops 500000000 | tf_op jit(solution)/shard_map/second_faces/pallas_call | solution.py:660
  35.3 0.4 collective-permute-done.5.rest_0_
  35.7 0.0 collective-permute-done.6.rest_1_
  35.7 1.3 %collective-permute-done.7.rest_2_ = f32[29,8,128]{2,1,0:T(8,128)S(1)} collective-permute-done((f32[29,8,128]{2,1,0:T(8,128)S(1)}, f32[29,8,128]{2,1,0:T(8,128)S(1)}, u32[]{:S(2)}, u32[]{:S(2)}) %collective-permute-start.7) | collective-permute-done | bytes 118816 | tf_op jit(solution)/shard_map/ppermute | solution.py:590
  36.9 1.9 %second_ghosts.1 = f32[1125,8,128]{2,1,0:T(8,128)S(1)} custom-call(s32[1]{0:T(128)} %bitcast.place_ref, f32[1125,8,128]{2,1,0:T(8,128)S(1)} %second_faces.1.acc_in, f32[1125,8,128]{2,1,0:T(8,128)S(1)} %first_ghosts.1.mid_ref.state_ref, f32[500,8,128]{2,1,0:T(8,128)S(1)} %get-tuple-element.23.med_ref, ...), custom_call_target="tpu_custom_call", output_to_operand_aliasing={{}: (1, {})} | custom-call | flops 1000000000 | tf_op jit(solution)/shard_map/second_ghosts/pallas_call | solution.py:664
  38.8 0.0 collective-permute-done.9.d_ref
  38.9 0.0 collective-permute-done.8.c_ref
  38.9 2.4 %store.1 = (f32[1125,2,2,128]{3,2,1,0:T(2,128)}, f32[1125,2,2,128]{3,2,1,0:T(2,128)}, f32[3,125,256]{2,1,0:T(8,128)}) custom-call(f32[1125,2,2,2,128]{4,3,2,1,0:T(2,128)S(1)} %bitcast.28, f32[3,64,256]{2,1,0:T(8,128)S(1)} %get-tuple-element.36.a_ref, f32[3,61,256]{2,1,0:T(8,128)S(1)} %get-tuple-element.37.b_ref, ...), custom_call_target="tpu_custom_call" | custom-call | flops 4000000000 | tf_op jit(solution)/shard_map/store/pallas_call | solution.py:668
  (1 shorter events, 0.0 us)
Async XLA Ops:
  0.6 3.0 %copy-start.1 = (s32[1,4,32]{2,1,0:T(4,128)S(1)}, s32[1,4,32]{2,1,0:T(4,128)}, u32[]{:S(2)}) copy-start(s32[1,4,32]{2,1,0:T(4,128)} %list_ref.5) | copy-start | bytes 1540
  3.6 9.1 %copy-start = (s32[1,1536]{1,0:T(1,128)S(1)}, s32[1,1536]{1,0:T(1,128)}, u32[]{:S(2)}) copy-start(s32[1,1536]{1,0:T(1,128)} %codes_ref.7) | copy-start | bytes 18436
  4.0 13.8 %collective-permute-start = (f32[29,8,128]{2,1,0:T(8,128)S(1)}, f32[29,8,128]{2,1,0:T(8,128)S(1)}, u32[]{:S(2)}, u32[]{:S(2)}) collective-permute-start(f32[29,8,128]{2,1,0:T(8,128)S(1)} %pack.3), channel_id=1, source_target_pairs={{0,4},{1,5},{2,6},{3,7},{4,0},{5,1},{6,2},{7,3},{8,12},{9,13},{10,... | collective-permute-start | bytes 356360 | tf_op jit(solution)/shard_map/ppermute | solution.py:590
  8.0 9.9 %collective-permute-start.1 = (f32[29,8,128]{2,1,0:T(8,128)S(1)}, f32[29,8,128]{2,1,0:T(8,128)S(1)}, u32[]{:S(2)}, u32[]{:S(2)}) collective-permute-start(f32[29,8,128]{2,1,0:T(8,128)S(1)} %get-tuple-element.26), channel_id=1, source_target_pairs={{0,1},{2,3},{4,5},{6,7},{1,0},{3,2},{5,4},{7,6},{8,9},{10,11},{12,... | collective-permute-start | bytes 356360 | tf_op jit(solution)/shard_map/ppermute | solution.py:590
  9.0 8.9 %collective-permute-start.2 = (f32[29,8,128]{2,1,0:T(8,128)S(1)}, f32[29,8,128]{2,1,0:T(8,128)S(1)}, u32[]{:S(2)}, u32[]{:S(2)}) collective-permute-start(f32[29,8,128]{2,1,0:T(8,128)S(1)} %get-tuple-element.27), channel_id=1, source_target_pairs={{1,2},{3,4},{5,6},{2,1},{4,3},{6,5},{0,0},{7,7},{9,10},{11,12},{13... | collective-permute-start | bytes 356360 | tf_op jit(solution)/shard_map/ppermute | solution.py:590
  23.6 8.0 %collective-permute-start.3 = (f32[3,64,256]{2,1,0:T(8,128)S(1)}, f32[3,64,256]{2,1,0:T(8,128)S(1)}, u32[]{:S(2)}, u32[]{:S(2)}) collective-permute-start(f32[3,64,256]{2,1,0:T(8,128)S(1)} %get-tuple-element.30.a_ref.grad_ref), channel_id=1, source_target_pairs={{0,8},{8,0},{16,24},{24,16},{1,9},{9,1},{17,25},{25,17},{2,10},{10... | collective-permute-start | bytes 589832 | tf_op jit(solution)/shard_map/ppermute | solution.py:566
  24.8 6.8 %collective-permute-start.4 = (f32[3,61,256]{2,1,0:T(8,128)S(1)}, f32[3,61,256]{2,1,0:T(8,128)S(1)}, u32[]{:S(2)}, u32[]{:S(2)}) collective-permute-start(f32[3,61,256]{2,1,0:T(8,128)S(1)} %get-tuple-element.31.b_ref), channel_id=1, source_target_pairs={{0,16},{8,24},{16,0},{24,8},{1,17},{9,25},{17,1},{25,9},{2,18},{10... | collective-permute-start | bytes 562184 | tf_op jit(solution)/shard_map/ppermute | solution.py:566
  27.1 8.6 %collective-permute-start.5 = (f32[29,8,128]{2,1,0:T(8,128)S(1)}, f32[29,8,128]{2,1,0:T(8,128)S(1)}, u32[]{:S(2)}, u32[]{:S(2)}) collective-permute-start(f32[29,8,128]{2,1,0:T(8,128)S(1)} %get-tuple-element.33), channel_id=1, source_target_pairs={{0,4},{1,5},{2,6},{3,7},{4,0},{5,1},{6,2},{7,3},{8,12},{9,13},{10,... | collective-permute-start | bytes 356360 | tf_op jit(solution)/shard_map/ppermute | solution.py:590
  27.2 8.5 %collective-permute-start.6 = (f32[29,8,128]{2,1,0:T(8,128)S(1)}, f32[29,8,128]{2,1,0:T(8,128)S(1)}, u32[]{:S(2)}, u32[]{:S(2)}) collective-permute-start(f32[29,8,128]{2,1,0:T(8,128)S(1)} %get-tuple-element.34), channel_id=1, source_target_pairs={{0,1},{2,3},{4,5},{6,7},{1,0},{3,2},{5,4},{7,6},{8,9},{10,11},{12,... | collective-permute-start | bytes 356360 | tf_op jit(solution)/shard_map/ppermute | solution.py:590
  29.7 7.3 %collective-permute-start.7 = (f32[29,8,128]{2,1,0:T(8,128)S(1)}, f32[29,8,128]{2,1,0:T(8,128)S(1)}, u32[]{:S(2)}, u32[]{:S(2)}) collective-permute-start(f32[29,8,128]{2,1,0:T(8,128)S(1)} %get-tuple-element.35), channel_id=1, source_target_pairs={{1,2},{3,4},{5,6},{2,1},{4,3},{6,5},{0,0},{7,7},{9,10},{11,12},{13... | collective-permute-start | bytes 356360 | tf_op jit(solution)/shard_map/ppermute | solution.py:590
  31.7 7.2 %collective-permute-start.8 = (f32[3,64,256]{2,1,0:T(8,128)S(1)}, f32[3,64,256]{2,1,0:T(8,128)S(1)}, u32[]{:S(2)}, u32[]{:S(2)}) collective-permute-start(f32[3,64,256]{2,1,0:T(8,128)S(1)} %get-tuple-element.36.a_ref), channel_id=1, source_target_pairs={{0,16},{8,24},{16,0},{24,8},{1,17},{9,25},{17,1},{25,9},{2,18},{10... | collective-permute-start | bytes 589832 | tf_op jit(solution)/shard_map/ppermute | solution.py:566
  32.0 6.9 %collective-permute-start.9 = (f32[3,61,256]{2,1,0:T(8,128)S(1)}, f32[3,61,256]{2,1,0:T(8,128)S(1)}, u32[]{:S(2)}, u32[]{:S(2)}) collective-permute-start(f32[3,61,256]{2,1,0:T(8,128)S(1)} %get-tuple-element.37.b_ref), channel_id=1, source_target_pairs={{0,8},{8,0},{16,24},{24,16},{1,9},{9,1},{17,25},{25,17},{2,10},{10... | collective-permute-start | bytes 562184 | tf_op jit(solution)/shard_map/ppermute | solution.py:566

commit v7 on v6

--- a/solution.py
+++ b/solution.py
@@ -428,10 +428,8 @@
     pack_links(slots, links, place_ref, state_ref, list_ref, sends, line)
 
 
-def late_pack_kernel(slots, links, place_ref, state_ref, list_ref, grad_ref, *sends):
-    across = sum(link[0] == 0 for link in links)
-    pack_links(slots, links, place_ref, state_ref, list_ref, sends[:across], 0)
-    pack_links(slots, links, place_ref, state_ref, list_ref, sends[across:], 1)
+def late_pack_kernel(line, slots, links, place_ref, state_ref, list_ref, grad_ref, *sends):
+    pack_links(slots, links, place_ref, state_ref, list_ref, sends, line)
 
 
 def spread_material(mat_ref, med_ref):
@@ -643,10 +641,12 @@
     acc, *halved = call(
         second_volume_kernel, [state_shape] + part_shapes, [vmem] + [vmem] * 4, "second_volume", 0, [products]
     )(live, mid, state, med, grad_first)
-    sends = call(late_pack_kernel, [send_shape] * count, [smem] + [vmem] * 3, "pack", 0.5)(
-        place, mid, send_list, halved[0]
-    )
-    ghosts = exchange(sends[:across], 0) + exchange(sends[across:], 1)
+    ghosts = []
+    for line in range(2):
+        sends = call(
+            functools.partial(late_pack_kernel, line), by_line[line], [smem] + [vmem] * 3, "pack", 0.25
+        )(place, mid, send_list, halved[0])
+        ghosts += exchange(sends, line)
     doubling = lax.axis_size("shot") == 4
     if doubling:
         pieces = [swapped(halved[0], "shot", 1), swapped(halved[1], "shot", 2)]

time: 41.6 us -> 41.2 us (level)
  waiting for transfers between devices: 1.65 us -> 0.87 us
    ppermute x6, waiting for transfers between devices: 1.64 us -> 0.86 us  [exchange(): lax.ppermute(send, 'dom', route)]
    pallas_call x1 -> x2, Pallas kernels: 1.01 us -> 1.08 us  [shards(): call(functools.partial(late_pack_kernel, line), by_line[line], [smem] + [...]
  transfers between devices with their start and end apart: 10 -> 10, of which waited for: 2 -> 1; matrix products, arithmetic and copies ran while one was open for 0% -> 0% of each run, Pallas kernels for 29% -> 29%
where the time goes in v7:
time: 41.2 us; the launch traced here: 40.8 us
  Pallas kernels  23.4 us (57%)
  starting transfers between devices  14.9 us (36%)
  between operations  1.62 us (4%)
  waiting for transfers between devices  0.87 us (2%)
    ppermute x6, starting transfers between devices, exchange(): lax.ppermute(send, 'dom', route)  11.9 us
    pallas_call x1, Pallas kernels, shards(): call(first_kernel, [state_shape, grad_shape, pltpu.VMEM((SUBS, LANES), f3...  5.08 us
    pallas_call x1, Pallas kernels, shards(): call(second_volume_kernel, [state_shape] + part_shapes, [vmem] + [vmem] *...  3.6 us
    pallas_call x1, Pallas kernels, shards(): call(second_faces_kernel, [state_shape], [vmem] * 5, 'second_faces', 0.5,...  3.1 us
    ppermute x4, starting transfers between devices, swapped(): return lax.ppermute(block, axis, route)  3.06 us
    pallas_call x1, Pallas kernels, shards(): call(load_kernel, [pltpu.VMEM(apart, f32), med_shape], [hbm] * 3, 'load',...  2.98 us
    pallas_call x1, Pallas kernels, shards(): call(store_and_sum_kernel, [part_shape, part_shape, jax.ShapeDtypeStruct(...  2.43 us
    pallas_call x1, Pallas kernels, shards(): call(middle_kernel, [state_shape], [smem] + [vmem] * (4 + count), 'first_...  2.08 us
  transfers between devices with their start and end apart: 10, of which 1 were waited for; matrix products, arithmetic and copies ran while one was open for 0% of the time, Pallas kernels for 29%

profile of v7, /device:TPU:1, one launch (start us, length us, event | category | flops | bytes accessed | tf_op | source)
XLA Modules:
  0.0 40.8 jit_solution(15174890629964032507)
XLA Ops:
  0.6 0.0 copy-start.1
  0.6 3.0 %load.1 = (f32[1125,2,2,2,128]{4,3,2,1,0:T(2,128)S(1)}, f32[500,8,128]{2,1,0:T(8,128)S(1)}) custom-call(f32[3,125,256]{2,1,0:T(8,128)} %mat_hbm.1, f32[1125,2,2,128]{3,2,1,0:T(2,128)} %bitcast.29, f32[1125,2,2,128]{3,2,1,0:T(2,128)} %bitcast.30), custom_call_target="tpu_custom_call" | custom-call | flops 4000000000 | tf_op jit(solution)/shard_map/load/pallas_call | solution.py:618
  3.6 0.0 copy-done.1
  3.6 0.0 copy-start
  3.7 0.4 pack.4
  4.0 3.2 %collective-permute-start = (f32[29,8,128]{2,1,0:T(8,128)S(1)}, f32[29,8,128]{2,1,0:T(8,128)S(1)}, u32[]{:S(2)}, u32[]{:S(2)}) collective-permute-start(f32[29,8,128]{2,1,0:T(8,128)S(1)} %pack.4), channel_id=1, source_target_pairs={{0,4},{1,5},{2,6},{3,7},{4,0},{5,1},{6,2},{7,3},{8,12},{9,13},{10,... | collective-permute-start | bytes 356360 | tf_op jit(solution)/shard_map/ppermute | solution.py:588
  7.3 0.7 %pack.5 = (f32[29,8,128]{2,1,0:T(8,128)S(1)}, f32[29,8,128]{2,1,0:T(8,128)S(1)}) custom-call(s32[1]{0:T(128)} %bitcast.place_ref, f32[1125,8,128]{2,1,0:T(8,128)S(1)} %bitcast.24, s32[1,4,32]{2,1,0:T(4,128)S(1)} %copy-done.1), custom_call_target="tpu_custom_call" | custom-call | tf_op jit(solution)/shard_map/pack/pallas_call | solution.py:629
  8.0 1.0 %collective-permute-start.1 = (f32[29,8,128]{2,1,0:T(8,128)S(1)}, f32[29,8,128]{2,1,0:T(8,128)S(1)}, u32[]{:S(2)}, u32[]{:S(2)}) collective-permute-start(f32[29,8,128]{2,1,0:T(8,128)S(1)} %get-tuple-element.25), channel_id=1, source_target_pairs={{0,1},{2,3},{4,5},{6,7},{1,0},{3,2},{5,4},{7,6},{8,9},{10,11},{12,... | collective-permute-start | bytes 356360 | tf_op jit(solution)/shard_map/ppermute | solution.py:588
  9.0 3.1 %collective-permute-start.2 = (f32[29,8,128]{2,1,0:T(8,128)S(1)}, f32[29,8,128]{2,1,0:T(8,128)S(1)}, u32[]{:S(2)}, u32[]{:S(2)}) collective-permute-start(f32[29,8,128]{2,1,0:T(8,128)S(1)} %get-tuple-element.26), channel_id=1, source_target_pairs={{1,2},{3,4},{5,6},{2,1},{4,3},{6,5},{0,0},{7,7},{9,10},{11,12},{13... | collective-permute-start | bytes 356360 | tf_op jit(solution)/shard_map/ppermute | solution.py:588
  12.7 0.0 copy-done
  12.7 5.1 %first_section.1 = (f32[1125,8,128]{2,1,0:T(8,128)S(1)}, f32[3,125,256]{2,1,0:T(8,128)S(1)}, f32[8,128]{1,0:T(8,128)S(1)}) custom-call(s32[1]{0:T(128)S(6)} %copy.21.counts_ref, f32[1125,8,128]{2,1,0:T(8,128)S(1)} %bitcast.25, f32[500,8,128]{2,1,0:T(8,128)S(1)} %get-tuple-element.22.med_ref, s32[1,1536]{1,0:T(1,128)S(1)} %copy-done), custom_call_target="tpu_custom_call" | custom-call | flops 8000000000 | tf_op jit(solution)/shard_map/first_section/pallas_call | solution.py:633
  17.8 0.0 collective-permute-done.rest_0_
  17.8 0.0 collective-permute-done.1.rest_1_
  17.9 0.0 collective-permute-done.2.rest_2_
  17.9 2.1 %first_ghosts.1.mid_ref.state_ref = f32[1125,8,128]{2,1,0:T(8,128)S(1)} custom-call(s32[1]{0:T(128)} %bitcast.place_ref, f32[1125,8,128]{2,1,0:T(8,128)S(1)} %get-tuple-element.24.acc_in, f32[1125,8,128]{2,1,0:T(8,128)S(1)} %bitcast.26, f32[500,8,128]{2,1,0:T(8,128)S(1)} %get-tuple-element.22.med_ref, ...), custom_call_target="tpu_custom_call", output_to_operand_aliasing={{}: (1, {})} | custom-call | flops 4000000000 | tf_op jit(solution)/shard_map/first_ghosts/pallas_call | solution.py:636
  19.9 3.6 %second_volume.1 = (f32[1125,8,128]{2,1,0:T(8,128)S(1)}, f32[3,64,256]{2,1,0:T(8,128)S(1)}, f32[3,61,256]{2,1,0:T(8,128)S(1)}) custom-call(f32[8,128]{1,0:T(8,128)S(1)} %get-tuple-element.23.live_ref, f32[1125,8,128]{2,1,0:T(8,128)S(1)} %first_ghosts.1.mid_ref.state_ref, f32[1125,8,128]{2,1,0:T(8,128)S(1)} %bitcast.27, ...), custom_call_target="tpu_custom_call" | custom-call | tf_op jit(solution)/shard_map/second_volume/pallas_call | solution.py:641
  23.6 1.3 %collective-permute-start.3 = (f32[3,64,256]{2,1,0:T(8,128)S(1)}, f32[3,64,256]{2,1,0:T(8,128)S(1)}, u32[]{:S(2)}, u32[]{:S(2)}) collective-permute-start(f32[3,64,256]{2,1,0:T(8,128)S(1)} %get-tuple-element.29.a_ref.grad_ref), channel_id=1, source_target_pairs={{0,8},{8,0},{16,24},{24,16},{1,9},{9,1},{17,25},{25,17},{2,10},{10... | collective-permute-start | bytes 589832 | tf_op jit(solution)/shard_map/ppermute | solution.py:564
  24.8 1.2 %collective-permute-start.4 = (f32[3,61,256]{2,1,0:T(8,128)S(1)}, f32[3,61,256]{2,1,0:T(8,128)S(1)}, u32[]{:S(2)}, u32[]{:S(2)}) collective-permute-start(f32[3,61,256]{2,1,0:T(8,128)S(1)} %get-tuple-element.30.b_ref), channel_id=1, source_target_pairs={{0,16},{8,24},{16,0},{24,8},{1,17},{9,25},{17,1},{25,9},{2,18},{10... | collective-permute-start | bytes 562184 | tf_op jit(solution)/shard_map/ppermute | solution.py:564
  26.1 0.4 pack.6
  26.5 0.1 collective-permute-start.5
  26.6 0.7 %pack.7 = (f32[29,8,128]{2,1,0:T(8,128)S(1)}, f32[29,8,128]{2,1,0:T(8,128)S(1)}) custom-call(s32[1]{0:T(128)} %bitcast.place_ref, f32[1125,8,128]{2,1,0:T(8,128)S(1)} %first_ghosts.1.mid_ref.state_ref, s32[1,4,32]{2,1,0:T(4,128)S(1)} %copy-done.1, f32[3,64,256]{2,1,0:T(8,128)S(1)} %get-tuple-element.29.a_ref.grad_ref), custom_call_target="tpu_custom_call" | custom-call | flops 250000000 | tf_op jit(solution)/shard_map/pack/pallas_call | solution.py:646
  27.3 2.5 %collective-permute-start.6 = (f32[29,8,128]{2,1,0:T(8,128)S(1)}, f32[29,8,128]{2,1,0:T(8,128)S(1)}, u32[]{:S(2)}, u32[]{:S(2)}) collective-permute-start(f32[29,8,128]{2,1,0:T(8,128)S(1)} %get-tuple-element.32), channel_id=1, source_target_pairs={{0,1},{2,3},{4,5},{6,7},{1,0},{3,2},{5,4},{7,6},{8,9},{10,11},{12,... | collective-permute-start | bytes 356360 | tf_op jit(solution)/shard_map/ppermute | solution.py:588
  29.8 1.9 %collective-permute-start.7 = (f32[29,8,128]{2,1,0:T(8,128)S(1)}, f32[29,8,128]{2,1,0:T(8,128)S(1)}, u32[]{:S(2)}, u32[]{:S(2)}) collective-permute-start(f32[29,8,128]{2,1,0:T(8,128)S(1)} %get-tuple-element.33), channel_id=1, source_target_pairs={{1,2},{3,4},{5,6},{2,1},{4,3},{6,5},{0,0},{7,7},{9,10},{11,12},{13... | collective-permute-start | bytes 356360 | tf_op jit(solution)/shard_map/ppermute | solution.py:588
  31.7 0.0 collective-permute-done.4.far_ref
  31.7 0.0 collective-permute-done.3.near_ref
  31.8 0.3 collective-permute-start.8
  32.1 0.3 collective-permute-start.9
  32.3 3.1 %second_faces.1.acc_in = f32[1125,8,128]{2,1,0:T(8,128)S(1)} custom-call(f32[8,128]{1,0:T(8,128)S(1)} %get-tuple-element.23.live_ref, f32[1125,8,128]{2,1,0:T(8,128)S(1)} %get-tuple-element.31.acc_in, f32[1125,8,128]{2,1,0:T(8,128)S(1)} %first_ghosts.1.mid_ref.state_ref, ...), custom_call_target="tpu_custom_call", output_to_operand_aliasing={{}: (1, {})} | custom-call | flops 500000000 | tf_op jit(solution)/shard_map/second_faces/pallas_call | solution.py:660
  35.5 0.0 collective-permute-done.5.rest_0_
  35.5 0.0 collective-permute-done.6.rest_1_
  35.5 0.8 %collective-permute-done.7.rest_2_ = f32[29,8,128]{2,1,0:T(8,128)S(1)} collective-permute-done((f32[29,8,128]{2,1,0:T(8,128)S(1)}, f32[29,8,128]{2,1,0:T(8,128)S(1)}, u32[]{:S(2)}, u32[]{:S(2)}) %collective-permute-start.7) | collective-permute-done | bytes 118816 | tf_op jit(solution)/shard_map/ppermute | solution.py:588
  36.3 1.9 %second_ghosts.1 = f32[1125,8,128]{2,1,0:T(8,128)S(1)} custom-call(s32[1]{0:T(128)} %bitcast.place_ref, f32[1125,8,128]{2,1,0:T(8,128)S(1)} %second_faces.1.acc_in, f32[1125,8,128]{2,1,0:T(8,128)S(1)} %first_ghosts.1.mid_ref.state_ref, f32[500,8,128]{2,1,0:T(8,128)S(1)} %get-tuple-element.22.med_ref, ...), custom_call_target="tpu_custom_call", output_to_operand_aliasing={{}: (1, {})} | custom-call | flops 1000000000 | tf_op jit(solution)/shard_map/second_ghosts/pallas_call | solution.py:664
  38.2 0.0 collective-permute-done.9.d_ref
  38.2 0.0 collective-permute-done.8.c_ref
  38.2 2.4 %store.1 = (f32[1125,2,2,128]{3,2,1,0:T(2,128)}, f32[1125,2,2,128]{3,2,1,0:T(2,128)}, f32[3,125,256]{2,1,0:T(8,128)}) custom-call(f32[1125,2,2,2,128]{4,3,2,1,0:T(2,128)S(1)} %bitcast.28, f32[3,64,256]{2,1,0:T(8,128)S(1)} %get-tuple-element.34.a_ref, f32[3,61,256]{2,1,0:T(8,128)S(1)} %get-tuple-element.35.b_ref, ...), custom_call_target="tpu_custom_call" | custom-call | flops 4000000000 | tf_op jit(solution)/shard_map/store/pallas_call | solution.py:668
  (1 shorter events, 0.0 us)
Async XLA Ops:
  0.6 3.0 %copy-start.1 = (s32[1,4,32]{2,1,0:T(4,128)S(1)}, s32[1,4,32]{2,1,0:T(4,128)}, u32[]{:S(2)}) copy-start(s32[1,4,32]{2,1,0:T(4,128)} %list_ref.7) | copy-start | bytes 1540
  3.6 9.1 %copy-start = (s32[1,1536]{1,0:T(1,128)S(1)}, s32[1,1536]{1,0:T(1,128)}, u32[]{:S(2)}) copy-start(s32[1,1536]{1,0:T(1,128)} %codes_ref.7) | copy-start | bytes 18436
  4.0 13.8 %collective-permute-start = (f32[29,8,128]{2,1,0:T(8,128)S(1)}, f32[29,8,128]{2,1,0:T(8,128)S(1)}, u32[]{:S(2)}, u32[]{:S(2)}) collective-permute-start(f32[29,8,128]{2,1,0:T(8,128)S(1)} %pack.4), channel_id=1, source_target_pairs={{0,4},{1,5},{2,6},{3,7},{4,0},{5,1},{6,2},{7,3},{8,12},{9,13},{10,... | collective-permute-start | bytes 356360 | tf_op jit(solution)/shard_map/ppermute | solution.py:588
  8.0 9.9 %collective-permute-start.1 = (f32[29,8,128]{2,1,0:T(8,128)S(1)}, f32[29,8,128]{2,1,0:T(8,128)S(1)}, u32[]{:S(2)}, u32[]{:S(2)}) collective-permute-start(f32[29,8,128]{2,1,0:T(8,128)S(1)} %get-tuple-element.25), channel_id=1, source_target_pairs={{0,1},{2,3},{4,5},{6,7},{1,0},{3,2},{5,4},{7,6},{8,9},{10,11},{12,... | collective-permute-start | bytes 356360 | tf_op jit(solution)/shard_map/ppermute | solution.py:588
  9.0 8.9 %collective-permute-start.2 = (f32[29,8,128]{2,1,0:T(8,128)S(1)}, f32[29,8,128]{2,1,0:T(8,128)S(1)}, u32[]{:S(2)}, u32[]{:S(2)}) collective-permute-start(f32[29,8,128]{2,1,0:T(8,128)S(1)} %get-tuple-element.26), channel_id=1, source_target_pairs={{1,2},{3,4},{5,6},{2,1},{4,3},{6,5},{0,0},{7,7},{9,10},{11,12},{13... | collective-permute-start | bytes 356360 | tf_op jit(solution)/shard_map/ppermute | solution.py:588
  23.6 8.2 %collective-permute-start.3 = (f32[3,64,256]{2,1,0:T(8,128)S(1)}, f32[3,64,256]{2,1,0:T(8,128)S(1)}, u32[]{:S(2)}, u32[]{:S(2)}) collective-permute-start(f32[3,64,256]{2,1,0:T(8,128)S(1)} %get-tuple-element.29.a_ref.grad_ref), channel_id=1, source_target_pairs={{0,8},{8,0},{16,24},{24,16},{1,9},{9,1},{17,25},{25,17},{2,10},{10... | collective-permute-start | bytes 589832 | tf_op jit(solution)/shard_map/ppermute | solution.py:564
  24.8 6.9 %collective-permute-start.4 = (f32[3,61,256]{2,1,0:T(8,128)S(1)}, f32[3,61,256]{2,1,0:T(8,128)S(1)}, u32[]{:S(2)}, u32[]{:S(2)}) collective-permute-start(f32[3,61,256]{2,1,0:T(8,128)S(1)} %get-tuple-element.30.b_ref), channel_id=1, source_target_pairs={{0,16},{8,24},{16,0},{24,8},{1,17},{9,25},{17,1},{25,9},{2,18},{10... | collective-permute-start | bytes 562184 | tf_op jit(solution)/shard_map/ppermute | solution.py:564
  26.5 9.0 %collective-permute-start.5 = (f32[29,8,128]{2,1,0:T(8,128)S(1)}, f32[29,8,128]{2,1,0:T(8,128)S(1)}, u32[]{:S(2)}, u32[]{:S(2)}) collective-permute-start(f32[29,8,128]{2,1,0:T(8,128)S(1)} %pack.6), channel_id=1, source_target_pairs={{0,4},{1,5},{2,6},{3,7},{4,0},{5,1},{6,2},{7,3},{8,12},{9,13},{10,... | collective-permute-start | bytes 356360 | tf_op jit(solution)/shard_map/ppermute | solution.py:588
  27.3 8.2 %collective-permute-start.6 = (f32[29,8,128]{2,1,0:T(8,128)S(1)}, f32[29,8,128]{2,1,0:T(8,128)S(1)}, u32[]{:S(2)}, u32[]{:S(2)}) collective-permute-start(f32[29,8,128]{2,1,0:T(8,128)S(1)} %get-tuple-element.32), channel_id=1, source_target_pairs={{0,1},{2,3},{4,5},{6,7},{1,0},{3,2},{5,4},{7,6},{8,9},{10,11},{12,... | collective-permute-start | bytes 356360 | tf_op jit(solution)/shard_map/ppermute | solution.py:588
  29.8 6.5 %collective-permute-start.7 = (f32[29,8,128]{2,1,0:T(8,128)S(1)}, f32[29,8,128]{2,1,0:T(8,128)S(1)}, u32[]{:S(2)}, u32[]{:S(2)}) collective-permute-start(f32[29,8,128]{2,1,0:T(8,128)S(1)} %get-tuple-element.33), channel_id=1, source_target_pairs={{1,2},{3,4},{5,6},{2,1},{4,3},{6,5},{0,0},{7,7},{9,10},{11,12},{13... | collective-permute-start | bytes 356360 | tf_op jit(solution)/shard_map/ppermute | solution.py:588
  31.8 6.4 %collective-permute-start.8 = (f32[3,64,256]{2,1,0:T(8,128)S(1)}, f32[3,64,256]{2,1,0:T(8,128)S(1)}, u32[]{:S(2)}, u32[]{:S(2)}) collective-permute-start(f32[3,64,256]{2,1,0:T(8,128)S(1)} %get-tuple-element.34.a_ref), channel_id=1, source_target_pairs={{0,16},{8,24},{16,0},{24,8},{1,17},{9,25},{17,1},{25,9},{2,18},{10... | collective-permute-start | bytes 589832 | tf_op jit(solution)/shard_map/ppermute | solution.py:564
  32.1 6.1 %collective-permute-start.9 = (f32[3,61,256]{2,1,0:T(8,128)S(1)}, f32[3,61,256]{2,1,0:T(8,128)S(1)}, u32[]{:S(2)}, u32[]{:S(2)}) collective-permute-start(f32[3,61,256]{2,1,0:T(8,128)S(1)} %get-tuple-element.35.b_ref), channel_id=1, source_target_pairs={{0,8},{8,0},{16,24},{24,16},{1,9},{9,1},{17,25},{25,17},{2,10},{10... | collective-permute-start | bytes 562184 | tf_op jit(solution)/shard_map/ppermute | solution.py:564
